TPU v7x, 32 devices: a whole 2x2x4 slice. The times are simulated.
32 devices in a mesh: blk: 8 (over y, x, core), group: 4 (over z).
Axes of the slice: x: 2, y: 2, z: 4, core: 2. Of those that a mesh axis runs over, the one named last changes fastest.
Arguments:
- visual_encoder_outputs: float32 [16384, 1152], P(('blk', 'group'))
- caption_encoder_outputs: float32 [16384, 1152], P(('blk', 'group'))
- partner_lookup_grid: int32 [2, 8], replicated, may hold values from 0 to 7, as said below
- sharpness_coefficient: float32 [1], replicated, may hold values from 8 to 30
- sigmoid_shift_term: float32 [1], replicated, may hold values from -6 to -2
Outputs:
- image_gradient: float32 [16384, 1152], P(('blk', 'group'))
- text_gradient: float32 [16384, 1152], P(('blk', 'group'))
Inputs may be any that keep to these rules, and one draw needn't show every extreme that they name: In each of the 2 rounds, partner_lookup_grid pairs index b of blk with index b XOR 2**k, where k is a bit position drawn for that round; the rounds' positions differ, so every matching is mutual and no index meets the same partner twice.
All inputs are finite; a program needn't handle non-finite values.
Results may differ from a plain program's by a relative error of at most 0.0049.
Values may be sent and summed in bfloat16 or wider, within the bound.
No kernel may reach another device: no remote copies, remote signals or barrier semaphores. Data moves between devices by JAX's collectives and lax.ppermute only.
A program may use at most 64 MiB of HBM per device.

v0:
```python
import functools
import itertools

import jax
import jax.numpy as jnp
from jax import lax
from jax.experimental import pallas as pl
from jax.experimental.pallas import tpu as pltpu
from jax.sharding import PartitionSpec as P

epsilon = 1e-06
log2_e = 1.4426950408889634
MIB = 1024 * 1024
VMEM = pl.BlockSpec(memory_space=pltpu.VMEM)
SMEM = pl.BlockSpec(memory_space=pltpu.SMEM)
BLOCK, STRIP, COLUMNS = 256, 256, 384


def cost(rows, other_rows, width):
    return pl.CostEstimate(
        flops=4 * rows * max(other_rows, 1) * width,
        bytes_accessed=8 * rows * width,
        transcendentals=2 * rows * other_rows,
    )


def call(body, name, operands, outs, work, smem=2, grid=None, out_specs=None, scratch=()):
    return pl.pallas_call(
        body,
        grid=grid or (),
        in_specs=[SMEM] * smem + [VMEM] * (len(operands) - smem),
        out_specs=out_specs or [VMEM] * len(outs),
        out_shape=[jax.ShapeDtypeStruct(shape, dtype) for shape, dtype in outs],
        scratch_shapes=list(scratch),
        name=name,
        compiler_params=pltpu.CompilerParams(vmem_limit_bytes=24 * MIB),
        cost_estimate=cost(*work),
    )(*operands)


def strips(count, size):
    return [(first, min(first + size, count)) for first in range(0, count, size)]


def normalized(raw):
    total = jnp.sum(raw * raw, axis=-1, keepdims=True)
    return (raw * lax.rsqrt(total + epsilon)).astype(jnp.bfloat16)


def coupling(own, other, scale, factor, shift, places=None):
    products = lax.dot_general(
        own, other, (((1,), (1,)), ((), ())), preferred_element_type=jnp.float32
    )
    powers = products * (-log2_e * scale) - log2_e * shift
    if places is not None:
        row = places[0] + lax.broadcasted_iota(jnp.int32, powers.shape, 0)
        column = places[1] + lax.broadcasted_iota(jnp.int32, powers.shape, 1)
        same = row == column
        powers = jnp.where(same, -powers, powers)
    below = 1.0 + jnp.exp2(powers)
    inverse = pl.reciprocal(below, approx=True)
    weights = factor * (inverse * (2.0 - below * inverse))
    if places is not None:
        weights = jnp.where(same, -weights, weights)
    return weights.astype(jnp.bfloat16)


def is_drawn(grid_ref, bit):
    drawn = jnp.bool_(False)
    for number in range(grid_ref.shape[0]):
        drawn = drawn | (grid_ref[number, 0] == (1 << bit))
    return drawn


def add_pairs(scales, shift, own_ref, rows, others, before_ref, out_ref, weights_ref, matched=False):
    first, block = rows
    rows = slice(first, first + block)
    own = own_ref[rows, :]
    places, left = [], 0
    for (scale, factor), other_ref in zip(scales, others):
        count, width = other_ref.shape
        for top, bottom in strips(count, STRIP):
            weights_ref[rows, left + top : left + bottom] = coupling(
                own, other_ref[top:bottom, :], scale, factor, shift, (first, top) if matched else None
            )
        places.append(slice(left, left + count))
        left += count
    for top, bottom in strips(width, COLUMNS):
        total = None if before_ref is None else before_ref[rows, top:bottom]
        for place, other_ref in zip(places, others):
            added = jnp.dot(
                weights_ref[rows, place], other_ref[:, top:bottom], preferred_element_type=jnp.float32
            )
            total = added if total is None else total + added
        out_ref[rows, top:bottom] = total


def blocks_of(count):
    return [(first, min(BLOCK, count - first)) for first in range(0, count, BLOCK)]


def scales_of(bits, scale_ref, grid_ref):
    scale = scale_ref[0]
    return [
        (scale, scale if bit is None else jnp.where(is_drawn(grid_ref, bit), scale, 0.0))
        for bit in bits
    ]


def diagonal_kernel(scale_ref, shift_ref, image_ref, text_ref, image_sum_ref, text_sum_ref, weights_ref):
    scale, shift = scale_ref[0], shift_ref[0]
    row_count, width = image_ref.shape
    for rows in blocks_of(row_count):
        add_pairs(
            [(scale, scale)], shift, image_ref, rows, [text_ref], None, image_sum_ref, weights_ref, True
        )
    for first, last in strips(row_count, STRIP):
        for left, right in strips(width, COLUMNS):
            text_sum_ref[first:last, left:right] = lax.dot_general(
                weights_ref[:, first:last], image_ref[:, left:right], (((0,), (0,)), ((), ())),
                preferred_element_type=jnp.float32,
            )


def diagonal(scale, shift, image_half, text_half):
    rows, width = image_half.shape
    return call(
        diagonal_kernel,
        "diagonal",
        [scale, shift, image_half, text_half],
        [((rows, width), jnp.float32)] * 2,
        (rows, 2 * rows, width),
        scratch=[pltpu.VMEM((rows, rows), jnp.bfloat16)],
    )


def near_kernel(
    scale_ref, shift_ref, image_ref, text_ref, both_ref, image_sum_ref, text_sum_ref,
    image_out_ref, text_out_ref, weights_ref,
):
    scales, shift = [(scale_ref[0], scale_ref[0])], shift_ref[0]
    row_count = image_ref.shape[0]
    texts_ref, images_ref = both_ref.at[:row_count, :], both_ref.at[row_count:, :]
    for rows in blocks_of(row_count):
        add_pairs(
            scales, shift, image_ref, rows, [texts_ref], image_sum_ref, image_out_ref, weights_ref
        )
    for rows in blocks_of(row_count):
        add_pairs(
            scales, shift, text_ref, rows, [images_ref], text_sum_ref, text_out_ref, weights_ref
        )


def with_near(bit, scale, shift, image_half, text_half):
    rows, width = image_half.shape
    both = exchanged(jnp.concatenate([text_half, image_half]), bit)
    image_sum, text_sum = diagonal(scale, shift, image_half, text_half)
    return tuple(call(
        near_kernel,
        "add_near",
        [scale, shift, image_half, text_half, both, image_sum, text_sum],
        [((rows, width), jnp.float32)] * 2,
        (rows, 2 * rows, width),
        scratch=[pltpu.VMEM((rows, rows), jnp.bfloat16)],
    ))


def without_near(scale, shift, image_half, text_half):
    return tuple(diagonal(scale, shift, image_half, text_half))


def add_up_kernel(bits, scale_ref, shift_ref, grid_ref, own_ref, sum_ref, *refs):
    *other_refs, out_ref, weights_ref = refs
    scales = scales_of(bits, scale_ref, grid_ref)
    for rows in blocks_of(own_ref.shape[0]):
        add_pairs(scales, shift_ref[0], own_ref, rows, other_refs, sum_ref, out_ref, weights_ref)


def add_up(scale, shift, grid, own, total, others, bits):
    rows, width = own.shape
    count = sum(x.shape[0] for x in others)
    return call(
        functools.partial(add_up_kernel, tuple(bits)),
        "add_up",
        [scale, shift, grid, own, total, *others],
        [((rows, width), jnp.float32)],
        (rows, count, width),
        smem=3,
        scratch=[pltpu.VMEM((rows, count), jnp.bfloat16)],
    )[0]


def finish_kernel(bits, scale_ref, shift_ref, grid_ref, own_ref, raw_ref, sum_ref, *refs):
    *other_refs, out_ref, weights_ref, total_ref, sems = refs
    scales = scales_of(bits, scale_ref, grid_ref)
    copies = []
    for number, (first, block) in enumerate(blocks_of(own_ref.shape[0])):
        add_pairs(
            scales, shift_ref[0], own_ref, (first, block), other_refs, sum_ref, total_ref, weights_ref
        )
        rows = pl.ds(first, block)
        raw, total = raw_ref[rows, :], total_ref[rows, :]
        inverse = lax.rsqrt(jnp.sum(raw * raw, axis=-1, keepdims=True) + epsilon)
        unit = raw * inverse
        radial = jnp.sum(unit * total, axis=-1, keepdims=True)
        total_ref[rows, :] = (total - unit * radial) * inverse
        copy = pltpu.make_async_copy(total_ref.at[rows, :], out_ref.at[rows, :], sems.at[number])
        copy.start()
        copies.append(copy)
    for copy in copies:
        copy.wait()


def finish(scale, shift, grid, own, raw, total, others, bits):
    rows, width = own.shape
    count = sum(x.shape[0] for x in others)
    return call(
        functools.partial(finish_kernel, tuple(bits)),
        "finish",
        [scale, shift, grid, own, raw, total, *others],
        [((rows, width), jnp.float32)],
        (rows, count, width),
        smem=3,
        out_specs=[pl.BlockSpec(memory_space=pl.ANY)],
        scratch=[
            pltpu.VMEM((rows, count), jnp.bfloat16),
            pltpu.VMEM((rows, width), jnp.float32),
            pltpu.SemaphoreType.DMA((len(blocks_of(rows)),)),
        ],
    )[0]


def passed_along(x, axis, by):
    count = lax.axis_size(axis)
    return lax.ppermute(x, axis, [(i, (i + by) % count) for i in range(count)])


def exchanged(x, bit):
    count = lax.axis_size("blk")
    return lax.ppermute(x, "blk", [(i, i ^ (1 << bit)) for i in range(count)])


def with_partners(bits, visual, caption, grid, scale, shift):
    cut = visual.shape[0] * 3 // 4
    near, far = [bit for bit in bits if bit == 0], [bit for bit in bits if bit != 0]
    text_half = normalized(caption)
    text_z = passed_along(text_half, "group", 1)
    far_texts = [exchanged(text_half, bit) for bit in far]
    image_half = normalized(visual)
    operands = (scale, shift, image_half, text_half)
    if near:
        image_sum, text_sum = lax.cond(
            jnp.any(grid[:, 0] == (1 << near[0])),
            functools.partial(with_near, near[0]),
            without_near,
            *operands,
        )
    else:
        image_sum, text_sum = without_near(*operands)
    image_first, image_last = image_half[:cut], image_half[cut:]
    image_first, image_last, text_z, image_sum, text_sum = lax.optimization_barrier(
        (image_first, image_last, text_z, image_sum, text_sum)
    )
    image_z_first = passed_along(image_first, "group", -1)
    image_z_last = passed_along(image_last, "group", -1)
    image_first, image_last, far_texts = lax.optimization_barrier(
        (image_first, image_last, far_texts)
    )
    far_images_first = [exchanged(image_first, bit) for bit in far]
    image_gradient = finish(
        scale, shift, grid, image_half, visual, image_sum, [*far_texts, text_z], [*far, None]
    )
    text_sum, image_last, image_gradient = lax.optimization_barrier(
        (text_sum, image_last, image_gradient)
    )
    far_images_last = [exchanged(image_last, bit) for bit in far[:1]]
    image_last, image_z_first = lax.optimization_barrier((image_last, image_z_first))
    far_images_last += [exchanged(image_last, bit) for bit in far[1:]]
    text_sum = add_up(
        scale, shift, grid, text_half, text_sum, [*far_images_first, image_z_first], [*far, None]
    )
    text_gradient = finish(
        scale, shift, grid, text_half, caption, text_sum,
        [*far_images_last, image_z_last], [*far, None],
    )
    return image_gradient, text_gradient


def on_device(
    visual_encoder_outputs,
    caption_encoder_outputs,
    partner_lookup_grid,
    sharpness_coefficient,
    sigmoid_shift_term,
):
    rounds, peers = partner_lookup_grid.shape
    bits = range(peers.bit_length() - 1)
    operands = (
        visual_encoder_outputs,
        caption_encoder_outputs,
        partner_lookup_grid,
        sharpness_coefficient,
        sigmoid_shift_term,
    )
    if len(bits) <= rounds + 1:
        return with_partners(bits, *operands)
    choices = list(itertools.combinations(bits, rounds))
    union = jnp.sum(partner_lookup_grid[:, 0])
    branch = jnp.int32(0)
    for number, choice in enumerate(choices):
        branch = jnp.where(union == sum(1 << bit for bit in choice), jnp.int32(number), branch)
    return lax.switch(
        branch, [functools.partial(with_partners, choice) for choice in choices], *operands
    )


def solution(mesh):
    placed = (P(("blk", "group"), None), P(("blk", "group"), None), P(), P(), P())
    return jax.shard_map(
        on_device,
        mesh=mesh,
        in_specs=placed,
        out_specs=(P(("blk", "group"), None), P(("blk", "group"), None)),
        check_vma=False,
    )
```

profile of v0, /device:TPU:0, one launch (start us, length us, event | category | flops | bytes accessed | tf_op | source)
XLA Modules:
  0.0 71.5 jit_solution(3379471505484292352)
XLA Ops:
  0.6 2.0 %multiply_reduce_fusion = f32[512]{0:T(512)S(1)} fusion(f32[512,1152]{1,0:T(8,128)} %raw_ref.3), kind=kLoop, calls=%fused_computation.2 | loop fusion | flops 1179136 | bytes 2361344 | tf_op jit(solution)/shard_map/reduce_sum | solution.py:46
  3.0 1.2 %multiply_convert_fusion.own_ref = bf16[512,1152]{1,0:T(8,128)(2,1)} fusion(f32[512,1152]{1,0:T(8,128)S(1)} %copy-done, f32[512]{0:T(512)S(1)} %add_rsqrt_fusion), kind=kLoop, calls=%fused_computation.1 | loop fusion | flops 1179648 | bytes 3540992 | tf_op jit(solution)/shard_map/convert_element_type | solution.py:47
  4.2 3.0 %collective-permute-start.1 = (bf16[512,1152]{1,0:T(8,128)(2,1)}, bf16[512,1152]{1,0:T(8,128)(2,1)S(1)}, u32[]{:S(2)}, u32[]{:S(2)}) collective-permute-start(bf16[512,1152]{1,0:T(8,128)(2,1)} %multiply_convert_fusion.own_ref), channel_id=1, source_target_pairs={{0,1},{1,2},{2,3},{3,0},{4,5},{5,6},{6,7},{7,4},{8,9},{9,10},{10,1... | collective-permute-start | bytes 3538952 | tf_op jit(solution)/shard_map/ppermute | solution.py:235
  7.3 1.5 %collective-permute-start.2 = (bf16[512,1152]{1,0:T(8,128)(2,1)}, bf16[512,1152]{1,0:T(8,128)(2,1)}, u32[]{:S(2)}, u32[]{:S(2)}) collective-permute-start(bf16[512,1152]{1,0:T(8,128)(2,1)} %multiply_convert_fusion.own_ref), channel_id=1, source_target_pairs={{0,8},{4,12},{8,0},{12,4},{16,24},{20,28},{24,16},{28,20},{1,9},{5... | collective-permute-start | bytes 3538952 | tf_op jit(solution)/shard_map/ppermute | solution.py:240
  8.8 1.5 %collective-permute-start.3 = (bf16[512,1152]{1,0:T(8,128)(2,1)}, bf16[512,1152]{1,0:T(8,128)(2,1)}, u32[]{:S(2)}, u32[]{:S(2)}) collective-permute-start(bf16[512,1152]{1,0:T(8,128)(2,1)} %multiply_convert_fusion.own_ref), channel_id=1, source_target_pairs={{0,16},{4,20},{8,24},{12,28},{16,0},{20,4},{24,8},{28,12},{1,17},{... | collective-permute-start | bytes 3538952 | tf_op jit(solution)/shard_map/ppermute | solution.py:240
  10.7 1.1 %slice.12 = bf16[384,1152]{1,0:T(8,128)(2,1)} slice(bf16[512,1152]{1,0:T(8,128)(2,1)S(1)} %multiply_convert_fusion.1.own_ref), slice={[0:384], [0:1152]} | slice | bytes 1769472 | tf_op jit(solution)/shard_map/slice | solution.py:260
  12.1 0.8 %slice.13 = bf16[128,1152]{1,0:T(8,128)(2,1)} slice(bf16[512,1152]{1,0:T(8,128)(2,1)S(1)} %multiply_convert_fusion.1.own_ref), slice={[384:512], [0:1152]} | slice | bytes 589824 | tf_op jit(solution)/shard_map/slice | solution.py:260
  12.9 0.6 compare_reduce_fusion
  14.2 15.6 %conditional.1 = ((f32[512,1152]{1,0:T(8,128)}, f32[512,1152]{1,0:T(8,128)})) conditional(s32[]{:T(128)} %convert_element_type.11, (f32[1]{0:T(128)}, f32[1]{0:T(128)}, bf16[512,1152]{1,0:T(8,128)(2,1)}, bf16[512,1152]{1,0:T(8,128)(2,1)}) %tuple.29, (bf16[512,1152]{1,0:T(8,128)(2,1)}, bf16[512,1152]{1,0:T(8,128)(2,1)}, f32[1]{0:T(128)}, ...), branch_computations={%region_3.0_spmd, %region_4.0_spmd} | conditional | flops 4836556800 | bytes 28311628 | solution.py:252
  14.2 1.9 %pad_maximum_fusion = bf16[1024,1152]{1,0:T(8,128)(2,1)S(1)} fusion(bf16[512,1152]{1,0:T(8,128)(2,1)} %get-tuple-element.22.image_ref, bf16[512,1152]{1,0:T(8,128)(2,1)} %get-tuple-element.23.text_ref), kind=kLoop, calls=%fused_computation | loop fusion | flops 4718592 | bytes 4718592 | tf_op jit(solution)/shard_map/cond/branch_1_fun/concatenate | solution.py:156
  16.2 5.6 %diagonal.3 = (f32[512,1152]{1,0:T(8,128)S(1)}, f32[512,1152]{1,0:T(8,128)S(1)}) custom-call(f32[1]{0:T(128)} %get-tuple-element.20.scale_ref, f32[1]{0:T(128)} %get-tuple-element.21.shift_ref, bf16[512,1152]{1,0:T(8,128)(2,1)S(1)} %copy-done.5, bf16[512,1152]{1,0:T(8,128)(2,1)} %get-tuple-element.23.text_ref), custom_call_target="tpu_custom_call" | custom-call | flops 2415919104 | bytes 4718592 | tf_op jit(solution)/shard_map/cond/branch_1_fun/diagonal/pallas_call | solution.py:28
  21.8 8.0 %add_near.1 = (f32[512,1152]{1,0:T(8,128)}, f32[512,1152]{1,0:T(8,128)}) custom-call(f32[1]{0:T(128)} %get-tuple-element.20.scale_ref, f32[1]{0:T(128)} %get-tuple-element.21.shift_ref, bf16[512,1152]{1,0:T(8,128)(2,1)S(1)} %copy-done.5, bf16[512,1152]{1,0:T(8,128)(2,1)} %get-tuple-element.23.text_ref, bf16[1024,1152]{1,0:T(8,128)(2,1)S(1)} %collective-permute-done.both_ref, ...), custom_call_target="tpu_custom_call" | custom-call | flops 2415919104 | bytes 4718592 | tf_op jit(solution)/shard_map/cond/branch_1_fun/add_near/pallas_call | solution.py:28
  29.8 5.7 %collective-permute-done.1.refs_2_ = bf16[512,1152]{1,0:T(8,128)(2,1)S(1)} collective-permute-done((bf16[512,1152]{1,0:T(8,128)(2,1)}, bf16[512,1152]{1,0:T(8,128)(2,1)S(1)}, u32[]{:S(2)}, u32[]{:S(2)}) %collective-permute-start.1) | collective-permute-done | bytes 1179680 | tf_op jit(solution)/shard_map/ppermute | solution.py:235
  35.5 1.7 %collective-permute-start.6 = (bf16[384,1152]{1,0:T(8,128)(2,1)}, bf16[384,1152]{1,0:T(8,128)(2,1)S(1)}, u32[]{:S(2)}, u32[]{:S(2)}) collective-permute-start(bf16[384,1152]{1,0:T(8,128)(2,1)} %slice.12), channel_id=1, source_target_pairs={{0,3},{1,0},{2,1},{3,2},{4,7},{5,4},{6,5},{7,6},{8,11},{9,8},{10,9... | collective-permute-start | bytes 2654216 | tf_op jit(solution)/shard_map/ppermute | solution.py:235
  37.2 1.5 %collective-permute-start.4 = (bf16[384,1152]{1,0:T(8,128)(2,1)}, bf16[384,1152]{1,0:T(8,128)(2,1)S(1)}, u32[]{:S(2)}, u32[]{:S(2)}) collective-permute-start(bf16[384,1152]{1,0:T(8,128)(2,1)} %slice.12), channel_id=1, source_target_pairs={{0,8},{4,12},{8,0},{12,4},{16,24},{20,28},{24,16},{28,20},{1,9},{5... | collective-permute-start | bytes 2654216 | tf_op jit(solution)/shard_map/ppermute | solution.py:240
  38.7 1.5 %collective-permute-start.5 = (bf16[384,1152]{1,0:T(8,128)(2,1)}, bf16[384,1152]{1,0:T(8,128)(2,1)S(1)}, u32[]{:S(2)}, u32[]{:S(2)}) collective-permute-start(bf16[384,1152]{1,0:T(8,128)(2,1)} %slice.12), channel_id=1, source_target_pairs={{0,16},{4,20},{8,24},{12,28},{16,0},{20,4},{24,8},{28,12},{1,17},{... | collective-permute-start | bytes 2654216 | tf_op jit(solution)/shard_map/ppermute | solution.py:240
  41.5 0.7 collective-permute-start.9
  42.2 1.7 %copy-done.2 = f32[512,1152]{1,0:T(8,128)S(1)} copy-done((f32[512,1152]{1,0:T(8,128)S(1)}, f32[512,1152]{1,0:T(8,128)}, u32[]{:S(2)}) %copy-start.2) | copy-done | bytes 2359320
  43.9 9.4 %finish.2 = f32[512,1152]{1,0:T(8,128)} custom-call(f32[1]{0:T(128)S(6)} %copy.11.scale_ref, f32[1]{0:T(128)S(6)} %copy.12.shift_ref, s32[2,8]{1,0:T(2,128)S(1)} %copy-done.3, bf16[512,1152]{1,0:T(8,128)(2,1)} %copy-done.4, f32[512,1152]{1,0:T(8,128)S(1)} %copy-done.2, f32[512,1152]{1,0:T(8,128)} %get-tuple-element.50.sum_ref, ...), custom_call_target="tpu_custom_call" | custom-call | flops 3623878656 | bytes 4718592 | tf_op jit(solution)/shard_map/finish/pallas_call | solution.py:28
  53.2 1.5 %collective-permute-start.7 = (bf16[128,1152]{1,0:T(8,128)(2,1)S(1)}, bf16[128,1152]{1,0:T(8,128)(2,1)S(1)}, u32[]{:S(2)}, u32[]{:S(2)}) collective-permute-start(bf16[128,1152]{1,0:T(8,128)(2,1)S(1)} %copy-done.6), channel_id=1, source_target_pairs={{0,8},{4,12},{8,0},{12,4},{16,24},{20,28},{24,16},{28,20},{1,9},{5... | collective-permute-start | bytes 884744 | tf_op jit(solution)/shard_map/ppermute | solution.py:240
  54.7 3.5 %collective-permute-done.6.refs_2_ = bf16[384,1152]{1,0:T(8,128)(2,1)S(1)} collective-permute-done((bf16[384,1152]{1,0:T(8,128)(2,1)}, bf16[384,1152]{1,0:T(8,128)(2,1)S(1)}, u32[]{:S(2)}, u32[]{:S(2)}) %collective-permute-start.6) | collective-permute-done | bytes 884768 | tf_op jit(solution)/shard_map/ppermute | solution.py:235
  58.3 1.5 %collective-permute-start.8 = (bf16[128,1152]{1,0:T(8,128)(2,1)S(1)}, bf16[128,1152]{1,0:T(8,128)(2,1)S(1)}, u32[]{:S(2)}, u32[]{:S(2)}) collective-permute-start(bf16[128,1152]{1,0:T(8,128)(2,1)S(1)} %copy-done.6), channel_id=1, source_target_pairs={{0,16},{4,20},{8,24},{12,28},{16,0},{20,4},{24,8},{28,12},{1,17},{... | collective-permute-start | bytes 884744 | tf_op jit(solution)/shard_map/ppermute | solution.py:240
  60.4 5.8 %add_up.1.sum_ref = f32[512,1152]{1,0:T(8,128)S(1)} custom-call(f32[1]{0:T(128)S(6)} %copy.11.scale_ref, f32[1]{0:T(128)S(6)} %copy.12.shift_ref, s32[2,8]{1,0:T(2,128)S(1)} %copy-done.3, bf16[512,1152]{1,0:T(8,128)(2,1)} %multiply_convert_fusion.own_ref, f32[512,1152]{1,0:T(8,128)S(1)} %copy-done.7, bf16[384,1152]{1,0:T(8,128)(2,1)S(1)} %collective-permute-done.4.refs_0_, ...), custom_call_target="tpu_custom_call" | custom-call | flops 2717908992 | bytes 4718592 | tf_op jit(solution)/shard_map/add_up/pallas_call | solution.py:28
  66.3 5.1 %finish.3 = f32[512,1152]{1,0:T(8,128)} custom-call(f32[1]{0:T(128)S(6)} %copy.11.scale_ref, f32[1]{0:T(128)S(6)} %copy.12.shift_ref, s32[2,8]{1,0:T(2,128)S(1)} %copy-done.3, bf16[512,1152]{1,0:T(8,128)(2,1)} %multiply_convert_fusion.own_ref, f32[512,1152]{1,0:T(8,128)S(1)} %copy-done, f32[512,1152]{1,0:T(8,128)S(1)} %add_up.1.sum_ref, ...), custom_call_target="tpu_custom_call" | custom-call | flops 905969664 | bytes 4718592 | tf_op jit(solution)/shard_map/finish/pallas_call | solution.py:28
  (28 shorter events, 1.8 us)
Async XLA Ops:
  0.6 2.4 %copy-start = (f32[512,1152]{1,0:T(8,128)S(1)}, f32[512,1152]{1,0:T(8,128)}, u32[]{:S(2)}) copy-start(f32[512,1152]{1,0:T(8,128)} %raw_ref.3) | copy-start | bytes 7077892
  2.7 7.6 %copy-start.1 = (f32[512,1152]{1,0:T(8,128)S(1)}, f32[512,1152]{1,0:T(8,128)}, u32[]{:S(2)}) copy-start(f32[512,1152]{1,0:T(8,128)} %raw_ref.2) | copy-start | bytes 7077892
  4.2 31.2 %collective-permute-start.1 = (bf16[512,1152]{1,0:T(8,128)(2,1)}, bf16[512,1152]{1,0:T(8,128)(2,1)S(1)}, u32[]{:S(2)}, u32[]{:S(2)}) collective-permute-start(bf16[512,1152]{1,0:T(8,128)(2,1)} %multiply_convert_fusion.own_ref), channel_id=1, source_target_pairs={{0,1},{1,2},{2,3},{3,0},{4,5},{5,6},{6,7},{7,4},{8,9},{9,10},{10,1... | collective-permute-start | bytes 3538952 | tf_op jit(solution)/shard_map/ppermute | solution.py:235
  7.3 29.9 %collective-permute-start.2 = (bf16[512,1152]{1,0:T(8,128)(2,1)}, bf16[512,1152]{1,0:T(8,128)(2,1)}, u32[]{:S(2)}, u32[]{:S(2)}) collective-permute-start(bf16[512,1152]{1,0:T(8,128)(2,1)} %multiply_convert_fusion.own_ref), channel_id=1, source_target_pairs={{0,8},{4,12},{8,0},{12,4},{16,24},{20,28},{24,16},{28,20},{1,9},{5... | collective-permute-start | bytes 3538952 | tf_op jit(solution)/shard_map/ppermute | solution.py:240
  8.8 28.5 %collective-permute-start.3 = (bf16[512,1152]{1,0:T(8,128)(2,1)}, bf16[512,1152]{1,0:T(8,128)(2,1)}, u32[]{:S(2)}, u32[]{:S(2)}) collective-permute-start(bf16[512,1152]{1,0:T(8,128)(2,1)} %multiply_convert_fusion.own_ref), channel_id=1, source_target_pairs={{0,16},{4,20},{8,24},{12,28},{16,0},{20,4},{24,8},{28,12},{1,17},{... | collective-permute-start | bytes 3538952 | tf_op jit(solution)/shard_map/ppermute | solution.py:240
  10.5 2.4 %copy-start.3 = (s32[2,8]{1,0:T(2,128)S(1)}, s32[2,8]{1,0:T(2,128)}, u32[]{:S(2)}) copy-start(s32[2,8]{1,0:T(2,128)} %grid_ref.5) | copy-start | bytes 196
  10.7 1.4 %copy-start.4 = (bf16[512,1152]{1,0:T(8,128)(2,1)}, bf16[512,1152]{1,0:T(8,128)(2,1)S(1)}, u32[]{:S(2)}) copy-start(bf16[512,1152]{1,0:T(8,128)(2,1)S(1)} %multiply_convert_fusion.1.own_ref) | copy-start | bytes 3538948
  14.2 2.0 %copy-start.5 = (bf16[512,1152]{1,0:T(8,128)(2,1)S(1)}, bf16[512,1152]{1,0:T(8,128)(2,1)}, u32[]{:S(2)}) copy-start(bf16[512,1152]{1,0:T(8,128)(2,1)} %get-tuple-element.22.image_ref) | copy-start | bytes 3538948 | tf_op jit(solution)/shard_map/cond
  16.1 5.7 %collective-permute-start = (bf16[1024,1152]{1,0:T(8,128)(2,1)S(1)}, bf16[1024,1152]{1,0:T(8,128)(2,1)S(1)}, u32[]{:S(2)}, u32[]{:S(2)}) collective-permute-start(bf16[1024,1152]{1,0:T(8,128)(2,1)S(1)} %pad_maximum_fusion), channel_id=1, source_target_pairs={{0,4},{4,0},{8,12},{12,8},{16,20},{20,16},{24,28},{28,24},{1,5},{5... | collective-permute-start | bytes 7077896 | tf_op jit(solution)/shard_map/cond/branch_1_fun/ppermute | solution.py:240
  35.5 22.8 %collective-permute-start.6 = (bf16[384,1152]{1,0:T(8,128)(2,1)}, bf16[384,1152]{1,0:T(8,128)(2,1)S(1)}, u32[]{:S(2)}, u32[]{:S(2)}) collective-permute-start(bf16[384,1152]{1,0:T(8,128)(2,1)} %slice.12), channel_id=1, source_target_pairs={{0,3},{1,0},{2,1},{3,2},{4,7},{5,4},{6,5},{7,6},{8,11},{9,8},{10,9... | collective-permute-start | bytes 2654216 | tf_op jit(solution)/shard_map/ppermute | solution.py:235
  37.2 22.8 %collective-permute-start.4 = (bf16[384,1152]{1,0:T(8,128)(2,1)}, bf16[384,1152]{1,0:T(8,128)(2,1)S(1)}, u32[]{:S(2)}, u32[]{:S(2)}) collective-permute-start(bf16[384,1152]{1,0:T(8,128)(2,1)} %slice.12), channel_id=1, source_target_pairs={{0,8},{4,12},{8,0},{12,4},{16,24},{20,28},{24,16},{28,20},{1,9},{5... | collective-permute-start | bytes 2654216 | tf_op jit(solution)/shard_map/ppermute | solution.py:240
  38.7 21.7 %collective-permute-start.5 = (bf16[384,1152]{1,0:T(8,128)(2,1)}, bf16[384,1152]{1,0:T(8,128)(2,1)S(1)}, u32[]{:S(2)}, u32[]{:S(2)}) collective-permute-start(bf16[384,1152]{1,0:T(8,128)(2,1)} %slice.12), channel_id=1, source_target_pairs={{0,16},{4,20},{8,24},{12,28},{16,0},{20,4},{24,8},{28,12},{1,17},{... | collective-permute-start | bytes 2654216 | tf_op jit(solution)/shard_map/ppermute | solution.py:240
  41.5 24.7 %collective-permute-start.9 = (bf16[128,1152]{1,0:T(8,128)(2,1)}, bf16[128,1152]{1,0:T(8,128)(2,1)S(1)}, u32[]{:S(2)}, u32[]{:S(2)}) collective-permute-start(bf16[128,1152]{1,0:T(8,128)(2,1)} %slice.13), channel_id=1, source_target_pairs={{0,3},{1,0},{2,1},{3,2},{4,7},{5,4},{6,5},{7,6},{8,11},{9,8},{10,9... | collective-permute-start | bytes 884744 | tf_op jit(solution)/shard_map/ppermute | solution.py:235
  42.2 1.7 %copy-start.2 = (f32[512,1152]{1,0:T(8,128)S(1)}, f32[512,1152]{1,0:T(8,128)}, u32[]{:S(2)}) copy-start(f32[512,1152]{1,0:T(8,128)} %raw_ref.2) | copy-start | bytes 7077892
  43.9 9.4 %copy-start.6 = (bf16[128,1152]{1,0:T(8,128)(2,1)S(1)}, bf16[128,1152]{1,0:T(8,128)(2,1)}, u32[]{:S(2)}) copy-start(bf16[128,1152]{1,0:T(8,128)(2,1)} %slice.13) | copy-start | bytes 884740
  43.9 16.6 %copy-start.7 = (f32[512,1152]{1,0:T(8,128)S(1)}, f32[512,1152]{1,0:T(8,128)}, u32[]{:S(2)}) copy-start(f32[512,1152]{1,0:T(8,128)} %get-tuple-element.55.sum_ref) | copy-start | bytes 7077892
  53.2 13.0 %collective-permute-start.7 = (bf16[128,1152]{1,0:T(8,128)(2,1)S(1)}, bf16[128,1152]{1,0:T(8,128)(2,1)S(1)}, u32[]{:S(2)}, u32[]{:S(2)}) collective-permute-start(bf16[128,1152]{1,0:T(8,128)(2,1)S(1)} %copy-done.6), channel_id=1, source_target_pairs={{0,8},{4,12},{8,0},{12,4},{16,24},{20,28},{24,16},{28,20},{1,9},{5... | collective-permute-start | bytes 884744 | tf_op jit(solution)/shard_map/ppermute | solution.py:240
  58.3 8.0 %collective-permute-start.8 = (bf16[128,1152]{1,0:T(8,128)(2,1)S(1)}, bf16[128,1152]{1,0:T(8,128)(2,1)S(1)}, u32[]{:S(2)}, u32[]{:S(2)}) collective-permute-start(bf16[128,1152]{1,0:T(8,128)(2,1)S(1)} %copy-done.6), channel_id=1, source_target_pairs={{0,16},{4,20},{8,24},{12,28},{16,0},{20,4},{24,8},{28,12},{1,17},{... | collective-permute-start | bytes 884744 | tf_op jit(solution)/shard_map/ppermute | solution.py:240
where the time goes:
time: 71.9 us; the launch traced here: 71.5 us
  Pallas kernels  33.8 us (47%)
  starting transfers between devices  14.5 us (20%)
  waiting for transfers between devices  9.88 us (14%)
  other arithmetic  6.25 us (9%)
  local copies, waits for them, and re-layouts  4.13 us (6%)
  between operations  2.85 us (4%)
    pallas_call x5, Pallas kernels, call(): pl.pallas_call(body, grid=grid or (), in_specs=[SMEM] * smem + [VMEM] * (...  33.8 us
    ppermute x3, waiting for transfers between devices, passed_along(): return lax.ppermute(x, axis, [(i, (i + by) % count) for i in range(count)])  9.22 us
    ppermute x7, starting transfers between devices, exchanged(): return lax.ppermute(x, 'blk', [(i, i ^ 1 << bit) for i in range(count)])  9.07 us
    ppermute x3, starting transfers between devices, passed_along(): return lax.ppermute(x, axis, [(i, (i + by) % count) for i in range(count)])  5.45 us
    reduce_sum x2, other arithmetic, normalized(): total = jnp.sum(raw * raw, axis=-1, keepdims=True)  2.27 us
    unnamed x14, local copies, waits for them, and re-layouts  2.26 us
    concatenate x1, other arithmetic, with_near(): both = exchanged(jnp.concatenate([text_half, image_half]), bit)  1.9 us
    slice x2, local copies, waits for them, and re-layouts, with_partners(): image_first, image_last = (image_half[:cut], image_half[cut:])  1.86 us
  transfers between devices with their start and end apart: 10, of which 4 were waited for; matrix products, arithmetic and copies ran while one was open for 7% of the time, Pallas kernels for 40%

commit v1 on v0

--- a/solution.py
+++ b/solution.py
@@ -135,12 +135,11 @@
 
 
 def near_kernel(
-    scale_ref, shift_ref, image_ref, text_ref, both_ref, image_sum_ref, text_sum_ref,
-    image_out_ref, text_out_ref, weights_ref,
+    bit, scale_ref, shift_ref, grid_ref, image_ref, text_ref, image_sum_ref, text_sum_ref, texts_ref,
+    images_ref, image_out_ref, text_out_ref, weights_ref,
 ):
-    scales, shift = [(scale_ref[0], scale_ref[0])], shift_ref[0]
+    scales, shift = scales_of([bit], scale_ref, grid_ref), shift_ref[0]
     row_count = image_ref.shape[0]
-    texts_ref, images_ref = both_ref.at[:row_count, :], both_ref.at[row_count:, :]
     for rows in blocks_of(row_count):
         add_pairs(
             scales, shift, image_ref, rows, [texts_ref], image_sum_ref, image_out_ref, weights_ref
@@ -151,22 +150,17 @@
         )
 
 
-def with_near(bit, scale, shift, image_half, text_half):
+def add_near(scale, shift, grid, image_half, text_half, image_sum, text_sum, texts, images, bit):
     rows, width = image_half.shape
-    both = exchanged(jnp.concatenate([text_half, image_half]), bit)
-    image_sum, text_sum = diagonal(scale, shift, image_half, text_half)
-    return tuple(call(
-        near_kernel,
+    return call(
+        functools.partial(near_kernel, bit),
         "add_near",
-        [scale, shift, image_half, text_half, both, image_sum, text_sum],
+        [scale, shift, grid, image_half, text_half, image_sum, text_sum, texts, images],
         [((rows, width), jnp.float32)] * 2,
         (rows, 2 * rows, width),
+        smem=3,
         scratch=[pltpu.VMEM((rows, rows), jnp.bfloat16)],
-    ))
-
-
-def without_near(scale, shift, image_half, text_half):
-    return tuple(diagonal(scale, shift, image_half, text_half))
+    )
 
 
 def add_up_kernel(bits, scale_ref, shift_ref, grid_ref, own_ref, sum_ref, *refs):
@@ -247,17 +241,9 @@
     text_z = passed_along(text_half, "group", 1)
     far_texts = [exchanged(text_half, bit) for bit in far]
     image_half = normalized(visual)
-    operands = (scale, shift, image_half, text_half)
-    if near:
-        image_sum, text_sum = lax.cond(
-            jnp.any(grid[:, 0] == (1 << near[0])),
-            functools.partial(with_near, near[0]),
-            without_near,
-            *operands,
-        )
-    else:
-        image_sum, text_sum = without_near(*operands)
     image_first, image_last = image_half[:cut], image_half[cut:]
+    boths = [(exchanged(text_half, bit), exchanged(image_half, bit)) for bit in near]
+    image_sum, text_sum = diagonal(scale, shift, image_half, text_half)
     image_first, image_last, text_z, image_sum, text_sum = lax.optimization_barrier(
         (image_first, image_last, text_z, image_sum, text_sum)
     )
@@ -267,6 +253,10 @@
         (image_first, image_last, far_texts)
     )
     far_images_first = [exchanged(image_first, bit) for bit in far]
+    for (texts, images), bit in zip(boths, near):
+        image_sum, text_sum = add_near(
+            scale, shift, grid, image_half, text_half, image_sum, text_sum, texts, images, bit
+        )
     image_gradient = finish(
         scale, shift, grid, image_half, visual, image_sum, [*far_texts, text_z], [*far, None]
     )

time: 71.9 us -> 68.7 us (0.955)
  waiting for transfers between devices: 9.88 us -> 23.8 us
  Pallas kernels: 33.8 us -> 24.2 us
  local copies, waits for them, and re-layouts: 4.13 us -> 0.41 us
  other arithmetic: 6.25 us -> 2.68 us
    ppermute x3, waiting for transfers between devices: 9.22 us -> 23.4 us  [passed_along(): return lax.ppermute(x, axis, [(i, (i + by) % count) for i in range(count)])]
    pallas_call x5, Pallas kernels: 33.8 us -> 24.2 us  [call(): pl.pallas_call(body, grid=grid or (), in_specs=[SMEM] * smem + [VMEM] * (...]
    unnamed x14 -> x6, local copies, waits for them, and re-layouts: 2.26 us -> 0.31 us
    concatenate x1 -> x0, other arithmetic: 1.9 us -> none  [with_near(): both = exchanged(jnp.concatenate([text_half, image_half]), bit)]
    slice x2, local copies, waits for them, and re-layouts: 1.86 us -> 0.09 us  [with_partners(): image_first, image_last = (image_half[:cut], image_half[cut:])]
    convert_element_type x2, other arithmetic: 1.43 us -> 0.4 us  [normalized(): return (raw * lax.rsqrt(total + epsilon)).astype(jnp.bfloat16)]
    ppermute x7 -> x8, starting transfers between devices: 9.07 us -> 9.19 us  [exchanged(): return lax.ppermute(x, 'blk', [(i, i ^ 1 << bit) for i in range(count)])]
  transfers between devices with their start and end apart: 10 -> 11, of which waited for: 4 -> 4; matrix products, arithmetic and copies ran while one was open for 7% -> 1% of each run, Pallas kernels for 40% -> 29%
where the time goes in v1:
time: 68.7 us; the launch traced here: 68.5 us
  Pallas kernels  24.2 us (35%)
  waiting for transfers between devices  23.8 us (35%)
  starting transfers between devices  15.2 us (22%)
  other arithmetic  2.68 us (4%)
  between operations  2.22 us (3%)
    pallas_call x5, Pallas kernels, call(): pl.pallas_call(body, grid=grid or (), in_specs=[SMEM] * smem + [VMEM] * (...  24.2 us
    ppermute x3, waiting for transfers between devices, passed_along(): return lax.ppermute(x, axis, [(i, (i + by) % count) for i in range(count)])  23.4 us
    ppermute x8, starting transfers between devices, exchanged(): return lax.ppermute(x, 'blk', [(i, i ^ 1 << bit) for i in range(count)])  9.19 us
    ppermute x3, starting transfers between devices, passed_along(): return lax.ppermute(x, axis, [(i, (i + by) % count) for i in range(count)])  5.96 us
    reduce_sum x2, other arithmetic, normalized(): total = jnp.sum(raw * raw, axis=-1, keepdims=True)  2.27 us
  transfers between devices with their start and end apart: 11, of which 4 were waited for; matrix products, arithmetic and copies ran while one was open for 1% of the time, Pallas kernels for 29%

profile of v1, /device:TPU:0, one launch (start us, length us, event | category | flops | bytes accessed | tf_op | source)
XLA Modules:
  0.0 68.5 jit_solution(14487059039862595798)
XLA Ops:
  0.6 2.0 %multiply_reduce_fusion = f32[512]{0:T(512)S(1)} fusion(f32[512,1152]{1,0:T(8,128)} %raw_ref.3), kind=kLoop, calls=%fused_computation.1 | loop fusion | flops 1179136 | bytes 2361344 | tf_op jit(solution)/shard_map/reduce_sum | solution.py:46
  2.7 0.3 copy-done
  3.0 0.2 multiply_convert_fusion.text_ref.own_ref
  3.2 3.1 %collective-permute-start = (bf16[512,1152]{1,0:T(8,128)(2,1)S(1)}, bf16[512,1152]{1,0:T(8,128)(2,1)S(1)}, u32[]{:S(2)}, u32[]{:S(2)}) collective-permute-start(bf16[512,1152]{1,0:T(8,128)(2,1)S(1)} %multiply_convert_fusion.text_ref.own_ref), channel_id=1, source_target_pairs={{0,1},{1,2},{2,3},{3,0},{4,5},{5,6},{6,7},{7,4},{8,9},{9,10},{10,1... | collective-permute-start | bytes 3538952 | tf_op jit(solution)/shard_map/ppermute | solution.py:229
  6.3 1.5 %collective-permute-start.3 = (bf16[512,1152]{1,0:T(8,128)(2,1)S(1)}, bf16[512,1152]{1,0:T(8,128)(2,1)S(1)}, u32[]{:S(2)}, u32[]{:S(2)}) collective-permute-start(bf16[512,1152]{1,0:T(8,128)(2,1)S(1)} %multiply_convert_fusion.text_ref.own_ref), channel_id=1, source_target_pairs={{0,8},{4,12},{8,0},{12,4},{16,24},{20,28},{24,16},{28,20},{1,9},{5... | collective-permute-start | bytes 3538952 | tf_op jit(solution)/shard_map/ppermute | solution.py:234
  7.8 1.5 %collective-permute-start.4 = (bf16[512,1152]{1,0:T(8,128)(2,1)S(1)}, bf16[512,1152]{1,0:T(8,128)(2,1)S(1)}, u32[]{:S(2)}, u32[]{:S(2)}) collective-permute-start(bf16[512,1152]{1,0:T(8,128)(2,1)S(1)} %multiply_convert_fusion.text_ref.own_ref), channel_id=1, source_target_pairs={{0,16},{4,20},{8,24},{12,28},{16,0},{20,4},{24,8},{28,12},{1,17},{... | collective-permute-start | bytes 3538952 | tf_op jit(solution)/shard_map/ppermute | solution.py:234
  9.3 0.2 multiply_reduce_fusion.1
  9.5 0.2 multiply_convert_fusion.1.image_ref.own_ref
  9.8 0.1 collective-permute-start.2
  11.2 3.0 %diagonal.1 = (f32[512,1152]{1,0:T(8,128)S(1)}, f32[512,1152]{1,0:T(8,128)S(1)}) custom-call(f32[1]{0:T(128)S(6)} %copy.7.scale_ref, f32[1]{0:T(128)S(6)} %copy.8.shift_ref, bf16[512,1152]{1,0:T(8,128)(2,1)S(1)} %multiply_convert_fusion.1.image_ref.own_ref, bf16[512,1152]{1,0:T(8,128)(2,1)S(1)} %multiply_convert_fusion.text_ref.own_ref), custom_call_target="tpu_custom_call" | custom-call | flops 2415919104 | bytes 4718592 | tf_op jit(solution)/shard_map/diagonal/pallas_call | solution.py:28
  14.2 20.0 %collective-permute-done.refs_2_ = bf16[512,1152]{1,0:T(8,128)(2,1)S(1)} collective-permute-done((bf16[512,1152]{1,0:T(8,128)(2,1)S(1)}, bf16[512,1152]{1,0:T(8,128)(2,1)S(1)}, u32[]{:S(2)}, u32[]{:S(2)}) %collective-permute-start) | collective-permute-done | bytes 1179680 | tf_op jit(solution)/shard_map/ppermute | solution.py:229
  34.3 1.7 %collective-permute-start.7 = (bf16[384,1152]{1,0:T(8,128)(2,1)S(1)}, bf16[384,1152]{1,0:T(8,128)(2,1)S(1)}, u32[]{:S(2)}, u32[]{:S(2)}) collective-permute-start(bf16[384,1152]{1,0:T(8,128)(2,1)S(1)} %slice.8), channel_id=1, source_target_pairs={{0,3},{1,0},{2,1},{3,2},{4,7},{5,4},{6,5},{7,6},{8,11},{9,8},{10,9... | collective-permute-start | bytes 2654216 | tf_op jit(solution)/shard_map/ppermute | solution.py:229
  36.0 1.5 %collective-permute-start.5 = (bf16[384,1152]{1,0:T(8,128)(2,1)S(1)}, bf16[384,1152]{1,0:T(8,128)(2,1)S(1)}, u32[]{:S(2)}, u32[]{:S(2)}) collective-permute-start(bf16[384,1152]{1,0:T(8,128)(2,1)S(1)} %slice.8), channel_id=1, source_target_pairs={{0,8},{4,12},{8,0},{12,4},{16,24},{20,28},{24,16},{28,20},{1,9},{5... | collective-permute-start | bytes 2654216 | tf_op jit(solution)/shard_map/ppermute | solution.py:234
  37.5 1.5 %collective-permute-start.6 = (bf16[384,1152]{1,0:T(8,128)(2,1)S(1)}, bf16[384,1152]{1,0:T(8,128)(2,1)S(1)}, u32[]{:S(2)}, u32[]{:S(2)}) collective-permute-start(bf16[384,1152]{1,0:T(8,128)(2,1)S(1)} %slice.8), channel_id=1, source_target_pairs={{0,16},{4,20},{8,24},{12,28},{16,0},{20,4},{24,8},{28,12},{1,17},{... | collective-permute-start | bytes 2654216 | tf_op jit(solution)/shard_map/ppermute | solution.py:234
  39.0 1.1 %collective-permute-start.10 = (bf16[128,1152]{1,0:T(8,128)(2,1)S(1)}, bf16[128,1152]{1,0:T(8,128)(2,1)S(1)}, u32[]{:S(2)}, u32[]{:S(2)}) collective-permute-start(bf16[128,1152]{1,0:T(8,128)(2,1)S(1)} %slice.9), channel_id=1, source_target_pairs={{0,3},{1,0},{2,1},{3,2},{4,7},{5,4},{6,5},{7,6},{8,11},{9,8},{10,9... | collective-permute-start | bytes 884744 | tf_op jit(solution)/shard_map/ppermute | solution.py:229
  40.2 4.5 %add_near.1 = (f32[512,1152]{1,0:T(8,128)S(1)}, f32[512,1152]{1,0:T(8,128)S(1)}) custom-call(f32[1]{0:T(128)S(6)} %copy.7.scale_ref, f32[1]{0:T(128)S(6)} %copy.8.shift_ref, s32[2,8]{1,0:T(2,128)S(1)} %copy-done.2, bf16[512,1152]{1,0:T(8,128)(2,1)S(1)} %multiply_convert_fusion.1.image_ref.own_ref, ...), custom_call_target="tpu_custom_call" | custom-call | flops 2415919104 | bytes 4718592 | tf_op jit(solution)/shard_map/add_near/pallas_call | solution.py:28
  44.7 7.2 %finish.2 = f32[512,1152]{1,0:T(8,128)} custom-call(f32[1]{0:T(128)S(6)} %copy.7.scale_ref, f32[1]{0:T(128)S(6)} %copy.8.shift_ref, s32[2,8]{1,0:T(2,128)S(1)} %copy-done.2, bf16[512,1152]{1,0:T(8,128)(2,1)S(1)} %multiply_convert_fusion.1.image_ref.own_ref, f32[512,1152]{1,0:T(8,128)S(1)} %copy-done.1, f32[512,1152]{1,0:T(8,128)S(1)} %get-tuple-element.28.sum_ref, ...), custom_call_target="tpu_custom_call" | custom-call | flops 3623878656 | bytes 4718592 | tf_op jit(solution)/shard_map/finish/pallas_call | solution.py:28
  51.9 1.6 %collective-permute-start.8 = (bf16[128,1152]{1,0:T(8,128)(2,1)S(1)}, bf16[128,1152]{1,0:T(8,128)(2,1)S(1)}, u32[]{:S(2)}, u32[]{:S(2)}) collective-permute-start(bf16[128,1152]{1,0:T(8,128)(2,1)S(1)} %slice.9), channel_id=1, source_target_pairs={{0,8},{4,12},{8,0},{12,4},{16,24},{20,28},{24,16},{28,20},{1,9},{5... | collective-permute-start | bytes 884744 | tf_op jit(solution)/shard_map/ppermute | solution.py:234
  53.5 3.3 %collective-permute-done.7.refs_2_ = bf16[384,1152]{1,0:T(8,128)(2,1)S(1)} collective-permute-done((bf16[384,1152]{1,0:T(8,128)(2,1)S(1)}, bf16[384,1152]{1,0:T(8,128)(2,1)S(1)}, u32[]{:S(2)}, u32[]{:S(2)}) %collective-permute-start.7) | collective-permute-done | bytes 884768 | tf_op jit(solution)/shard_map/ppermute | solution.py:229
  56.9 1.5 %collective-permute-start.9 = (bf16[128,1152]{1,0:T(8,128)(2,1)S(1)}, bf16[128,1152]{1,0:T(8,128)(2,1)S(1)}, u32[]{:S(2)}, u32[]{:S(2)}) collective-permute-start(bf16[128,1152]{1,0:T(8,128)(2,1)S(1)} %slice.9), channel_id=1, source_target_pairs={{0,16},{4,20},{8,24},{12,28},{16,0},{20,4},{24,8},{28,12},{1,17},{... | collective-permute-start | bytes 884744 | tf_op jit(solution)/shard_map/ppermute | solution.py:234
  58.4 0.2 collective-permute-done.5.refs_0_
  58.6 0.2 collective-permute-done.6.refs_1_
  58.8 5.1 %add_up.1.sum_ref = f32[512,1152]{1,0:T(8,128)S(1)} custom-call(f32[1]{0:T(128)S(6)} %copy.7.scale_ref, f32[1]{0:T(128)S(6)} %copy.8.shift_ref, s32[2,8]{1,0:T(2,128)S(1)} %copy-done.2, bf16[512,1152]{1,0:T(8,128)(2,1)S(1)} %multiply_convert_fusion.text_ref.own_ref, f32[512,1152]{1,0:T(8,128)S(1)} %get-tuple-element.33.sum_ref, ...), custom_call_target="tpu_custom_call" | custom-call | flops 2717908992 | bytes 4718592 | tf_op jit(solution)/shard_map/add_up/pallas_call | solution.py:28
  64.0 4.4 %finish.3 = f32[512,1152]{1,0:T(8,128)} custom-call(f32[1]{0:T(128)S(6)} %copy.7.scale_ref, f32[1]{0:T(128)S(6)} %copy.8.shift_ref, s32[2,8]{1,0:T(2,128)S(1)} %copy-done.2, bf16[512,1152]{1,0:T(8,128)(2,1)S(1)} %multiply_convert_fusion.text_ref.own_ref, f32[512,1152]{1,0:T(8,128)S(1)} %copy-done, f32[512,1152]{1,0:T(8,128)S(1)} %add_up.1.sum_ref, ...), custom_call_target="tpu_custom_call" | custom-call | flops 905969664 | bytes 4718592 | tf_op jit(solution)/shard_map/finish/pallas_call | solution.py:28
  (17 shorter events, 0.1 us)
Async XLA Ops:
  0.6 2.4 %copy-start = (f32[512,1152]{1,0:T(8,128)S(1)}, f32[512,1152]{1,0:T(8,128)}, u32[]{:S(2)}) copy-start(f32[512,1152]{1,0:T(8,128)} %raw_ref.3) | copy-start | bytes 7077892
  2.7 6.6 %copy-start.1 = (f32[512,1152]{1,0:T(8,128)S(1)}, f32[512,1152]{1,0:T(8,128)}, u32[]{:S(2)}) copy-start(f32[512,1152]{1,0:T(8,128)} %raw_ref.2) | copy-start | bytes 7077892
  3.2 31.1 %collective-permute-start = (bf16[512,1152]{1,0:T(8,128)(2,1)S(1)}, bf16[512,1152]{1,0:T(8,128)(2,1)S(1)}, u32[]{:S(2)}, u32[]{:S(2)}) collective-permute-start(bf16[512,1152]{1,0:T(8,128)(2,1)S(1)} %multiply_convert_fusion.text_ref.own_ref), channel_id=1, source_target_pairs={{0,1},{1,2},{2,3},{3,0},{4,5},{5,6},{6,7},{7,4},{8,9},{9,10},{10,1... | collective-permute-start | bytes 3538952 | tf_op jit(solution)/shard_map/ppermute | solution.py:229
  6.3 32.8 %collective-permute-start.1 = (bf16[512,1152]{1,0:T(8,128)(2,1)S(1)}, bf16[512,1152]{1,0:T(8,128)(2,1)S(1)}, u32[]{:S(2)}, u32[]{:S(2)}) collective-permute-start(bf16[512,1152]{1,0:T(8,128)(2,1)S(1)} %multiply_convert_fusion.text_ref.own_ref), channel_id=1, source_target_pairs={{0,4},{4,0},{8,12},{12,8},{16,20},{20,16},{24,28},{28,24},{1,5},{5... | collective-permute-start | bytes 3538952 | tf_op jit(solution)/shard_map/ppermute | solution.py:234
  6.3 29.7 %collective-permute-start.3 = (bf16[512,1152]{1,0:T(8,128)(2,1)S(1)}, bf16[512,1152]{1,0:T(8,128)(2,1)S(1)}, u32[]{:S(2)}, u32[]{:S(2)}) collective-permute-start(bf16[512,1152]{1,0:T(8,128)(2,1)S(1)} %multiply_convert_fusion.text_ref.own_ref), channel_id=1, source_target_pairs={{0,8},{4,12},{8,0},{12,4},{16,24},{20,28},{24,16},{28,20},{1,9},{5... | collective-permute-start | bytes 3538952 | tf_op jit(solution)/shard_map/ppermute | solution.py:234
  7.8 28.2 %collective-permute-start.4 = (bf16[512,1152]{1,0:T(8,128)(2,1)S(1)}, bf16[512,1152]{1,0:T(8,128)(2,1)S(1)}, u32[]{:S(2)}, u32[]{:S(2)}) collective-permute-start(bf16[512,1152]{1,0:T(8,128)(2,1)S(1)} %multiply_convert_fusion.text_ref.own_ref), channel_id=1, source_target_pairs={{0,16},{4,20},{8,24},{12,28},{16,0},{20,4},{24,8},{28,12},{1,17},{... | collective-permute-start | bytes 3538952 | tf_op jit(solution)/shard_map/ppermute | solution.py:234
  9.8 30.4 %collective-permute-start.2 = (bf16[512,1152]{1,0:T(8,128)(2,1)S(1)}, bf16[512,1152]{1,0:T(8,128)(2,1)S(1)}, u32[]{:S(2)}, u32[]{:S(2)}) collective-permute-start(bf16[512,1152]{1,0:T(8,128)(2,1)S(1)} %multiply_convert_fusion.1.image_ref.own_ref), channel_id=1, source_target_pairs={{0,4},{4,0},{8,12},{12,8},{16,20},{20,16},{24,28},{28,24},{1,5},{5... | collective-permute-start | bytes 3538952 | tf_op jit(solution)/shard_map/ppermute | solution.py:234
  11.2 29.0 %copy-start.2 = (s32[2,8]{1,0:T(2,128)S(1)}, s32[2,8]{1,0:T(2,128)}, u32[]{:S(2)}) copy-start(s32[2,8]{1,0:T(2,128)} %grid_ref.7) | copy-start | bytes 196
  34.3 22.6 %collective-permute-start.7 = (bf16[384,1152]{1,0:T(8,128)(2,1)S(1)}, bf16[384,1152]{1,0:T(8,128)(2,1)S(1)}, u32[]{:S(2)}, u32[]{:S(2)}) collective-permute-start(bf16[384,1152]{1,0:T(8,128)(2,1)S(1)} %slice.8), channel_id=1, source_target_pairs={{0,3},{1,0},{2,1},{3,2},{4,7},{5,4},{6,5},{7,6},{8,11},{9,8},{10,9... | collective-permute-start | bytes 2654216 | tf_op jit(solution)/shard_map/ppermute | solution.py:229
  36.0 22.6 %collective-permute-start.5 = (bf16[384,1152]{1,0:T(8,128)(2,1)S(1)}, bf16[384,1152]{1,0:T(8,128)(2,1)S(1)}, u32[]{:S(2)}, u32[]{:S(2)}) collective-permute-start(bf16[384,1152]{1,0:T(8,128)(2,1)S(1)} %slice.8), channel_id=1, source_target_pairs={{0,8},{4,12},{8,0},{12,4},{16,24},{20,28},{24,16},{28,20},{1,9},{5... | collective-permute-start | bytes 2654216 | tf_op jit(solution)/shard_map/ppermute | solution.py:234
  37.5 21.3 %collective-permute-start.6 = (bf16[384,1152]{1,0:T(8,128)(2,1)S(1)}, bf16[384,1152]{1,0:T(8,128)(2,1)S(1)}, u32[]{:S(2)}, u32[]{:S(2)}) collective-permute-start(bf16[384,1152]{1,0:T(8,128)(2,1)S(1)} %slice.8), channel_id=1, source_target_pairs={{0,16},{4,20},{8,24},{12,28},{16,0},{20,4},{24,8},{28,12},{1,17},{... | collective-permute-start | bytes 2654216 | tf_op jit(solution)/shard_map/ppermute | solution.py:234
  39.0 24.9 %collective-permute-start.10 = (bf16[128,1152]{1,0:T(8,128)(2,1)S(1)}, bf16[128,1152]{1,0:T(8,128)(2,1)S(1)}, u32[]{:S(2)}, u32[]{:S(2)}) collective-permute-start(bf16[128,1152]{1,0:T(8,128)(2,1)S(1)} %slice.9), channel_id=1, source_target_pairs={{0,3},{1,0},{2,1},{3,2},{4,7},{5,4},{6,5},{7,6},{8,11},{9,8},{10,9... | collective-permute-start | bytes 884744 | tf_op jit(solution)/shard_map/ppermute | solution.py:229
  51.9 12.0 %collective-permute-start.8 = (bf16[128,1152]{1,0:T(8,128)(2,1)S(1)}, bf16[128,1152]{1,0:T(8,128)(2,1)S(1)}, u32[]{:S(2)}, u32[]{:S(2)}) collective-permute-start(bf16[128,1152]{1,0:T(8,128)(2,1)S(1)} %slice.9), channel_id=1, source_target_pairs={{0,8},{4,12},{8,0},{12,4},{16,24},{20,28},{24,16},{28,20},{1,9},{5... | collective-permute-start | bytes 884744 | tf_op jit(solution)/shard_map/ppermute | solution.py:234
  56.9 7.1 %collective-permute-start.9 = (bf16[128,1152]{1,0:T(8,128)(2,1)S(1)}, bf16[128,1152]{1,0:T(8,128)(2,1)S(1)}, u32[]{:S(2)}, u32[]{:S(2)}) collective-permute-start(bf16[128,1152]{1,0:T(8,128)(2,1)S(1)} %slice.9), channel_id=1, source_target_pairs={{0,16},{4,20},{8,24},{12,28},{16,0},{20,4},{24,8},{28,12},{1,17},{... | collective-permute-start | bytes 884744 | tf_op jit(solution)/shard_map/ppermute | solution.py:234

commit v2 on v1

--- a/solution.py
+++ b/solution.py
@@ -244,34 +244,32 @@
     image_first, image_last = image_half[:cut], image_half[cut:]
     boths = [(exchanged(text_half, bit), exchanged(image_half, bit)) for bit in near]
     image_sum, text_sum = diagonal(scale, shift, image_half, text_half)
+    far_first, boths = lax.optimization_barrier((image_first, boths))
     image_first, image_last, text_z, image_sum, text_sum = lax.optimization_barrier(
         (image_first, image_last, text_z, image_sum, text_sum)
     )
     image_z_first = passed_along(image_first, "group", -1)
-    image_z_last = passed_along(image_last, "group", -1)
-    image_first, image_last, far_texts = lax.optimization_barrier(
-        (image_first, image_last, far_texts)
-    )
-    far_images_first = [exchanged(image_first, bit) for bit in far]
+    far_images_first = [exchanged(far_first, bit) for bit in far]
     for (texts, images), bit in zip(boths, near):
         image_sum, text_sum = add_near(
             scale, shift, grid, image_half, text_half, image_sum, text_sum, texts, images, bit
         )
+    image_last, far_texts = lax.optimization_barrier((image_last, far_texts))
+    far_images_last = [exchanged(image_last, bit) for bit in far]
     image_gradient = finish(
         scale, shift, grid, image_half, visual, image_sum, [*far_texts, text_z], [*far, None]
     )
-    text_sum, image_last, image_gradient = lax.optimization_barrier(
-        (text_sum, image_last, image_gradient)
-    )
-    far_images_last = [exchanged(image_last, bit) for bit in far[:1]]
-    image_last, image_z_first = lax.optimization_barrier((image_last, image_z_first))
-    far_images_last += [exchanged(image_last, bit) for bit in far[1:]]
+    text_sum, image_last, far_images_first, image_gradient = lax.optimization_barrier(
+        (text_sum, image_last, far_images_first, image_gradient)
+    )
+    image_z_last = passed_along(image_last, "group", -1)
+    if far:
+        text_sum = add_up(scale, shift, grid, text_half, text_sum, far_images_first, far)
     text_sum = add_up(
-        scale, shift, grid, text_half, text_sum, [*far_images_first, image_z_first], [*far, None]
+        scale, shift, grid, text_half, text_sum, [*far_images_last, image_z_first], [*far, None]
     )
     text_gradient = finish(
-        scale, shift, grid, text_half, caption, text_sum,
-        [*far_images_last, image_z_last], [*far, None],
+        scale, shift, grid, text_half, caption, text_sum, [image_z_last], [None]
     )
     return image_gradient, text_gradient
 

time: 68.7 us -> 70.3 us (1.023)
  Pallas kernels: 24.2 us -> 25.1 us
    ppermute x8, waiting for transfers between devices: 0.45 us -> 4.2 us  [exchanged(): return lax.ppermute(x, 'blk', [(i, i ^ 1 << bit) for i in range(count)])]
    ppermute x3, waiting for transfers between devices: 23.4 us -> 20.1 us  [passed_along(): return lax.ppermute(x, axis, [(i, (i + by) % count) for i in range(count)])]
    ppermute x8, starting transfers between devices: 9.19 us -> 8.16 us  [exchanged(): return lax.ppermute(x, 'blk', [(i, i ^ 1 << bit) for i in range(count)])]
    pallas_call x5 -> x6, Pallas kernels: 24.2 us -> 25.1 us  [call(): pl.pallas_call(body, grid=grid or (), in_specs=[SMEM] * smem + [VMEM] * (...]
  transfers between devices with their start and end apart: 11 -> 11, of which waited for: 4 -> 3; matrix products, arithmetic and copies ran while one was open for 1% -> 1% of each run, Pallas kernels for 29% -> 31%
where the time goes in v2:
time: 70.3 us; the launch traced here: 70.2 us
  Pallas kernels  25.1 us (36%)
  waiting for transfers between devices  24.3 us (35%)
  starting transfers between devices  14.8 us (21%)
  other arithmetic  2.68 us (4%)
  between operations  2.26 us (3%)
  local copies, waits for them, and re-layouts  1.11 us (2%)
    pallas_call x6, Pallas kernels, call(): pl.pallas_call(body, grid=grid or (), in_specs=[SMEM] * smem + [VMEM] * (...  25.1 us
    ppermute x3, waiting for transfers between devices, passed_along(): return lax.ppermute(x, axis, [(i, (i + by) % count) for i in range(count)])  20.1 us
    ppermute x8, starting transfers between devices, exchanged(): return lax.ppermute(x, 'blk', [(i, i ^ 1 << bit) for i in range(count)])  8.16 us
    ppermute x3, starting transfers between devices, passed_along(): return lax.ppermute(x, axis, [(i, (i + by) % count) for i in range(count)])  6.62 us
    ppermute x8, waiting for transfers between devices, exchanged(): return lax.ppermute(x, 'blk', [(i, i ^ 1 << bit) for i in range(count)])  4.2 us
    reduce_sum x2, other arithmetic, normalized(): total = jnp.sum(raw * raw, axis=-1, keepdims=True)  2.27 us
  transfers between devices with their start and end apart: 11, of which 3 were waited for; matrix products, arithmetic and copies ran while one was open for 1% of the time, Pallas kernels for 31%

profile of v2, /device:TPU:0, one launch (start us, length us, event | category | flops | bytes accessed | tf_op | source)
XLA Modules:
  0.0 70.2 jit_solution(3219111496673401207)
XLA Ops:
  0.6 2.0 %multiply_reduce_fusion = f32[512]{0:T(512)S(1)} fusion(f32[512,1152]{1,0:T(8,128)} %raw_ref.3), kind=kLoop, calls=%fused_computation.1 | loop fusion | flops 1179136 | bytes 2361344 | tf_op jit(solution)/shard_map/reduce_sum | solution.py:46
  2.7 0.3 copy-done
  3.2 0.5 collective-permute-start.1
  3.7 0.7 %copy-done.1 = f32[512,1152]{1,0:T(8,128)S(1)} copy-done((f32[512,1152]{1,0:T(8,128)S(1)}, f32[512,1152]{1,0:T(8,128)}, u32[]{:S(2)}) %copy-start.1) | copy-done | bytes 2359320
  4.4 0.2 multiply_reduce_fusion.1
  4.9 0.5 collective-permute-start.2
  5.4 2.6 %collective-permute-start = (bf16[512,1152]{1,0:T(8,128)(2,1)S(1)}, bf16[512,1152]{1,0:T(8,128)(2,1)S(1)}, u32[]{:S(2)}, u32[]{:S(2)}) collective-permute-start(bf16[512,1152]{1,0:T(8,128)(2,1)S(1)} %multiply_convert_fusion.text_ref.own_ref), channel_id=1, source_target_pairs={{0,1},{1,2},{2,3},{3,0},{4,5},{5,6},{6,7},{7,4},{8,9},{9,10},{10,1... | collective-permute-start | bytes 3538952 | tf_op jit(solution)/shard_map/ppermute | solution.py:229
  8.0 1.5 %collective-permute-start.3 = (bf16[512,1152]{1,0:T(8,128)(2,1)S(1)}, bf16[512,1152]{1,0:T(8,128)(2,1)S(1)}, u32[]{:S(2)}, u32[]{:S(2)}) collective-permute-start(bf16[512,1152]{1,0:T(8,128)(2,1)S(1)} %multiply_convert_fusion.text_ref.own_ref), channel_id=1, source_target_pairs={{0,8},{4,12},{8,0},{12,4},{16,24},{20,28},{24,16},{28,20},{1,9},{5... | collective-permute-start | bytes 3538952 | tf_op jit(solution)/shard_map/ppermute | solution.py:234
  9.5 1.5 %collective-permute-start.4 = (bf16[512,1152]{1,0:T(8,128)(2,1)S(1)}, bf16[512,1152]{1,0:T(8,128)(2,1)S(1)}, u32[]{:S(2)}, u32[]{:S(2)}) collective-permute-start(bf16[512,1152]{1,0:T(8,128)(2,1)S(1)} %multiply_convert_fusion.text_ref.own_ref), channel_id=1, source_target_pairs={{0,16},{4,20},{8,24},{12,28},{16,0},{20,4},{24,8},{28,12},{1,17},{... | collective-permute-start | bytes 3538952 | tf_op jit(solution)/shard_map/ppermute | solution.py:234
  12.5 0.6 collective-permute-start.5
  13.1 0.5 collective-permute-start.6
  13.6 3.0 %diagonal.1 = (f32[512,1152]{1,0:T(8,128)S(1)}, f32[512,1152]{1,0:T(8,128)S(1)}) custom-call(f32[1]{0:T(128)S(6)} %copy.7.scale_ref, f32[1]{0:T(128)S(6)} %copy.8.shift_ref, bf16[512,1152]{1,0:T(8,128)(2,1)S(1)} %multiply_convert_fusion.1.image_ref.own_ref, bf16[512,1152]{1,0:T(8,128)(2,1)S(1)} %multiply_convert_fusion.text_ref.own_ref), custom_call_target="tpu_custom_call" | custom-call | flops 2415919104 | bytes 4718592 | tf_op jit(solution)/shard_map/diagonal/pallas_call | solution.py:28
  16.6 20.1 %collective-permute-done.refs_2_ = bf16[512,1152]{1,0:T(8,128)(2,1)S(1)} collective-permute-done((bf16[512,1152]{1,0:T(8,128)(2,1)S(1)}, bf16[512,1152]{1,0:T(8,128)(2,1)S(1)}, u32[]{:S(2)}, u32[]{:S(2)}) %collective-permute-start) | collective-permute-done | bytes 1179680 | tf_op jit(solution)/shard_map/ppermute | solution.py:229
  36.6 1.7 %collective-permute-start.9 = (bf16[384,1152]{1,0:T(8,128)(2,1)S(1)}, bf16[384,1152]{1,0:T(8,128)(2,1)S(1)}, u32[]{:S(2)}, u32[]{:S(2)}) collective-permute-start(bf16[384,1152]{1,0:T(8,128)(2,1)S(1)} %slice.8), channel_id=1, source_target_pairs={{0,3},{1,0},{2,1},{3,2},{4,7},{5,4},{6,5},{7,6},{8,11},{9,8},{10,9... | collective-permute-start | bytes 2654216 | tf_op jit(solution)/shard_map/ppermute | solution.py:229
  38.4 1.5 %collective-permute-start.7 = (bf16[128,1152]{1,0:T(8,128)(2,1)S(1)}, bf16[128,1152]{1,0:T(8,128)(2,1)S(1)}, u32[]{:S(2)}, u32[]{:S(2)}) collective-permute-start(bf16[128,1152]{1,0:T(8,128)(2,1)S(1)} %slice.9), channel_id=1, source_target_pairs={{0,8},{4,12},{8,0},{12,4},{16,24},{20,28},{24,16},{28,20},{1,9},{5... | collective-permute-start | bytes 884744 | tf_op jit(solution)/shard_map/ppermute | solution.py:234
  39.9 1.5 %collective-permute-start.8 = (bf16[128,1152]{1,0:T(8,128)(2,1)S(1)}, bf16[128,1152]{1,0:T(8,128)(2,1)S(1)}, u32[]{:S(2)}, u32[]{:S(2)}) collective-permute-start(bf16[128,1152]{1,0:T(8,128)(2,1)S(1)} %slice.9), channel_id=1, source_target_pairs={{0,16},{4,20},{8,24},{12,28},{16,0},{20,4},{24,8},{28,12},{1,17},{... | collective-permute-start | bytes 884744 | tf_op jit(solution)/shard_map/ppermute | solution.py:234
  41.4 4.5 %add_near.1 = (f32[512,1152]{1,0:T(8,128)S(1)}, f32[512,1152]{1,0:T(8,128)S(1)}) custom-call(f32[1]{0:T(128)S(6)} %copy.7.scale_ref, f32[1]{0:T(128)S(6)} %copy.8.shift_ref, s32[2,8]{1,0:T(2,128)S(1)} %copy-done.2, bf16[512,1152]{1,0:T(8,128)(2,1)S(1)} %multiply_convert_fusion.1.image_ref.own_ref, ...), custom_call_target="tpu_custom_call" | custom-call | flops 2415919104 | bytes 4718592 | tf_op jit(solution)/shard_map/add_near/pallas_call | solution.py:28
  46.0 7.2 %finish.2 = f32[512,1152]{1,0:T(8,128)} custom-call(f32[1]{0:T(128)S(6)} %copy.7.scale_ref, f32[1]{0:T(128)S(6)} %copy.8.shift_ref, s32[2,8]{1,0:T(2,128)S(1)} %copy-done.2, bf16[512,1152]{1,0:T(8,128)(2,1)S(1)} %multiply_convert_fusion.1.image_ref.own_ref, f32[512,1152]{1,0:T(8,128)S(1)} %copy-done.1, f32[512,1152]{1,0:T(8,128)S(1)} %get-tuple-element.32.sum_ref, ...), custom_call_target="tpu_custom_call" | custom-call | flops 3623878656 | bytes 4718592 | tf_op jit(solution)/shard_map/finish/pallas_call | solution.py:28
  53.2 2.7 %collective-permute-done.5.refs_0_ = bf16[384,1152]{1,0:T(8,128)(2,1)S(1)} collective-permute-done((bf16[384,1152]{1,0:T(8,128)(2,1)S(1)}, bf16[384,1152]{1,0:T(8,128)(2,1)S(1)}, u32[]{:S(2)}, u32[]{:S(2)}) %collective-permute-start.5) | collective-permute-done | bytes 884768 | tf_op jit(solution)/shard_map/ppermute | solution.py:234
  55.8 1.5 %collective-permute-done.6.refs_1_ = bf16[384,1152]{1,0:T(8,128)(2,1)S(1)} collective-permute-done((bf16[384,1152]{1,0:T(8,128)(2,1)S(1)}, bf16[384,1152]{1,0:T(8,128)(2,1)S(1)}, u32[]{:S(2)}, u32[]{:S(2)}) %collective-permute-start.6) | collective-permute-done | bytes 884768 | tf_op jit(solution)/shard_map/ppermute | solution.py:234
  57.3 2.2 %collective-permute-start.10 = (bf16[128,1152]{1,0:T(8,128)(2,1)S(1)}, bf16[128,1152]{1,0:T(8,128)(2,1)S(1)}, u32[]{:S(2)}, u32[]{:S(2)}) collective-permute-start(bf16[128,1152]{1,0:T(8,128)(2,1)S(1)} %slice.9), channel_id=1, source_target_pairs={{0,3},{1,0},{2,1},{3,2},{4,7},{5,4},{6,5},{7,6},{8,11},{9,8},{10,9... | collective-permute-start | bytes 884744 | tf_op jit(solution)/shard_map/ppermute | solution.py:229
  59.6 3.6 %add_up.2.sum_ref = f32[512,1152]{1,0:T(8,128)S(1)} custom-call(f32[1]{0:T(128)S(6)} %copy.7.scale_ref, f32[1]{0:T(128)S(6)} %copy.8.shift_ref, s32[2,8]{1,0:T(2,128)S(1)} %copy-done.2, bf16[512,1152]{1,0:T(8,128)(2,1)S(1)} %multiply_convert_fusion.text_ref.own_ref, f32[512,1152]{1,0:T(8,128)S(1)} %get-tuple-element.37.sum_ref, ...), custom_call_target="tpu_custom_call" | custom-call | flops 1811939328 | bytes 4718592 | tf_op jit(solution)/shard_map/add_up/pallas_call | solution.py:28
  63.2 3.5 %add_up.3.sum_ref = f32[512,1152]{1,0:T(8,128)S(1)} custom-call(f32[1]{0:T(128)S(6)} %copy.7.scale_ref, f32[1]{0:T(128)S(6)} %copy.8.shift_ref, s32[2,8]{1,0:T(2,128)S(1)} %copy-done.2, bf16[512,1152]{1,0:T(8,128)(2,1)S(1)} %multiply_convert_fusion.text_ref.own_ref, f32[512,1152]{1,0:T(8,128)S(1)} %add_up.2.sum_ref, ...), custom_call_target="tpu_custom_call" | custom-call | flops 1509949440 | bytes 4718592 | tf_op jit(solution)/shard_map/add_up/pallas_call | solution.py:28
  66.8 3.2 %finish.3 = f32[512,1152]{1,0:T(8,128)} custom-call(f32[1]{0:T(128)S(6)} %copy.7.scale_ref, f32[1]{0:T(128)S(6)} %copy.8.shift_ref, s32[2,8]{1,0:T(2,128)S(1)} %copy-done.2, bf16[512,1152]{1,0:T(8,128)(2,1)S(1)} %multiply_convert_fusion.text_ref.own_ref, f32[512,1152]{1,0:T(8,128)S(1)} %copy-done, f32[512,1152]{1,0:T(8,128)S(1)} %add_up.3.sum_ref, ...), custom_call_target="tpu_custom_call" | custom-call | flops 301989888 | bytes 4718592 | tf_op jit(solution)/shard_map/finish/pallas_call | solution.py:28
  (18 shorter events, 0.5 us)
Async XLA Ops:
  0.6 2.4 %copy-start = (f32[512,1152]{1,0:T(8,128)S(1)}, f32[512,1152]{1,0:T(8,128)}, u32[]{:S(2)}) copy-start(f32[512,1152]{1,0:T(8,128)} %raw_ref.3) | copy-start | bytes 7077892
  2.7 1.7 %copy-start.1 = (f32[512,1152]{1,0:T(8,128)S(1)}, f32[512,1152]{1,0:T(8,128)}, u32[]{:S(2)}) copy-start(f32[512,1152]{1,0:T(8,128)} %raw_ref.2) | copy-start | bytes 7077892
  3.2 9.3 %collective-permute-start.1 = (bf16[512,1152]{1,0:T(8,128)(2,1)S(1)}, bf16[512,1152]{1,0:T(8,128)(2,1)S(1)}, u32[]{:S(2)}, u32[]{:S(2)}) collective-permute-start(bf16[512,1152]{1,0:T(8,128)(2,1)S(1)} %multiply_convert_fusion.text_ref.own_ref), channel_id=1, source_target_pairs={{0,4},{4,0},{8,12},{12,8},{16,20},{20,16},{24,28},{28,24},{1,5},{5... | collective-permute-start | bytes 3538952 | tf_op jit(solution)/shard_map/ppermute | solution.py:234
  4.9 7.6 %collective-permute-start.2 = (bf16[512,1152]{1,0:T(8,128)(2,1)S(1)}, bf16[512,1152]{1,0:T(8,128)(2,1)S(1)}, u32[]{:S(2)}, u32[]{:S(2)}) collective-permute-start(bf16[512,1152]{1,0:T(8,128)(2,1)S(1)} %multiply_convert_fusion.1.image_ref.own_ref), channel_id=1, source_target_pairs={{0,4},{4,0},{8,12},{12,8},{16,20},{20,16},{24,28},{28,24},{1,5},{5... | collective-permute-start | bytes 3538952 | tf_op jit(solution)/shard_map/ppermute | solution.py:234
  5.4 31.2 %collective-permute-start = (bf16[512,1152]{1,0:T(8,128)(2,1)S(1)}, bf16[512,1152]{1,0:T(8,128)(2,1)S(1)}, u32[]{:S(2)}, u32[]{:S(2)}) collective-permute-start(bf16[512,1152]{1,0:T(8,128)(2,1)S(1)} %multiply_convert_fusion.text_ref.own_ref), channel_id=1, source_target_pairs={{0,1},{1,2},{2,3},{3,0},{4,5},{5,6},{6,7},{7,4},{8,9},{9,10},{10,1... | collective-permute-start | bytes 3538952 | tf_op jit(solution)/shard_map/ppermute | solution.py:229
  8.0 30.3 %collective-permute-start.3 = (bf16[512,1152]{1,0:T(8,128)(2,1)S(1)}, bf16[512,1152]{1,0:T(8,128)(2,1)S(1)}, u32[]{:S(2)}, u32[]{:S(2)}) collective-permute-start(bf16[512,1152]{1,0:T(8,128)(2,1)S(1)} %multiply_convert_fusion.text_ref.own_ref), channel_id=1, source_target_pairs={{0,8},{4,12},{8,0},{12,4},{16,24},{20,28},{24,16},{28,20},{1,9},{5... | collective-permute-start | bytes 3538952 | tf_op jit(solution)/shard_map/ppermute | solution.py:234
  9.5 28.9 %collective-permute-start.4 = (bf16[512,1152]{1,0:T(8,128)(2,1)S(1)}, bf16[512,1152]{1,0:T(8,128)(2,1)S(1)}, u32[]{:S(2)}, u32[]{:S(2)}) collective-permute-start(bf16[512,1152]{1,0:T(8,128)(2,1)S(1)} %multiply_convert_fusion.text_ref.own_ref), channel_id=1, source_target_pairs={{0,16},{4,20},{8,24},{12,28},{16,0},{20,4},{24,8},{28,12},{1,17},{... | collective-permute-start | bytes 3538952 | tf_op jit(solution)/shard_map/ppermute | solution.py:234
  12.4 29.0 %copy-start.2 = (s32[2,8]{1,0:T(2,128)S(1)}, s32[2,8]{1,0:T(2,128)}, u32[]{:S(2)}) copy-start(s32[2,8]{1,0:T(2,128)} %grid_ref.9) | copy-start | bytes 196
  12.5 43.3 %collective-permute-start.5 = (bf16[384,1152]{1,0:T(8,128)(2,1)S(1)}, bf16[384,1152]{1,0:T(8,128)(2,1)S(1)}, u32[]{:S(2)}, u32[]{:S(2)}) collective-permute-start(bf16[384,1152]{1,0:T(8,128)(2,1)S(1)} %slice.8), channel_id=1, source_target_pairs={{0,8},{4,12},{8,0},{12,4},{16,24},{20,28},{24,16},{28,20},{1,9},{5... | collective-permute-start | bytes 2654216 | tf_op jit(solution)/shard_map/ppermute | solution.py:234
  13.1 44.3 %collective-permute-start.6 = (bf16[384,1152]{1,0:T(8,128)(2,1)S(1)}, bf16[384,1152]{1,0:T(8,128)(2,1)S(1)}, u32[]{:S(2)}, u32[]{:S(2)}) collective-permute-start(bf16[384,1152]{1,0:T(8,128)(2,1)S(1)} %slice.8), channel_id=1, source_target_pairs={{0,16},{4,20},{8,24},{12,28},{16,0},{20,4},{24,8},{28,12},{1,17},{... | collective-permute-start | bytes 2654216 | tf_op jit(solution)/shard_map/ppermute | solution.py:234
  36.6 26.5 %collective-permute-start.9 = (bf16[384,1152]{1,0:T(8,128)(2,1)S(1)}, bf16[384,1152]{1,0:T(8,128)(2,1)S(1)}, u32[]{:S(2)}, u32[]{:S(2)}) collective-permute-start(bf16[384,1152]{1,0:T(8,128)(2,1)S(1)} %slice.8), channel_id=1, source_target_pairs={{0,3},{1,0},{2,1},{3,2},{4,7},{5,4},{6,5},{7,6},{8,11},{9,8},{10,9... | collective-permute-start | bytes 2654216 | tf_op jit(solution)/shard_map/ppermute | solution.py:229
  38.4 24.8 %collective-permute-start.7 = (bf16[128,1152]{1,0:T(8,128)(2,1)S(1)}, bf16[128,1152]{1,0:T(8,128)(2,1)S(1)}, u32[]{:S(2)}, u32[]{:S(2)}) collective-permute-start(bf16[128,1152]{1,0:T(8,128)(2,1)S(1)} %slice.9), channel_id=1, source_target_pairs={{0,8},{4,12},{8,0},{12,4},{16,24},{20,28},{24,16},{28,20},{1,9},{5... | collective-permute-start | bytes 884744 | tf_op jit(solution)/shard_map/ppermute | solution.py:234
  39.9 23.3 %collective-permute-start.8 = (bf16[128,1152]{1,0:T(8,128)(2,1)S(1)}, bf16[128,1152]{1,0:T(8,128)(2,1)S(1)}, u32[]{:S(2)}, u32[]{:S(2)}) collective-permute-start(bf16[128,1152]{1,0:T(8,128)(2,1)S(1)} %slice.9), channel_id=1, source_target_pairs={{0,16},{4,20},{8,24},{12,28},{16,0},{20,4},{24,8},{28,12},{1,17},{... | collective-permute-start | bytes 884744 | tf_op jit(solution)/shard_map/ppermute | solution.py:234
  57.3 9.4 %collective-permute-start.10 = (bf16[128,1152]{1,0:T(8,128)(2,1)S(1)}, bf16[128,1152]{1,0:T(8,128)(2,1)S(1)}, u32[]{:S(2)}, u32[]{:S(2)}) collective-permute-start(bf16[128,1152]{1,0:T(8,128)(2,1)S(1)} %slice.9), channel_id=1, source_target_pairs={{0,3},{1,0},{2,1},{3,2},{4,7},{5,4},{6,5},{7,6},{8,11},{9,8},{10,9... | collective-permute-start | bytes 884744 | tf_op jit(solution)/shard_map/ppermute | solution.py:229

commit v3 on v1

--- a/solution.py
+++ b/solution.py
@@ -13,7 +13,7 @@
 MIB = 1024 * 1024
 VMEM = pl.BlockSpec(memory_space=pltpu.VMEM)
 SMEM = pl.BlockSpec(memory_space=pltpu.SMEM)
-BLOCK, STRIP, COLUMNS = 256, 256, 384
+BLOCK, STRIP, COLUMNS, SLICE, LANES = 256, 256, 384, 64, 128
 
 
 def cost(rows, other_rows, width):
@@ -47,10 +47,7 @@
     return (raw * lax.rsqrt(total + epsilon)).astype(jnp.bfloat16)
 
 
-def coupling(own, other, scale, factor, shift, places=None):
-    products = lax.dot_general(
-        own, other, (((1,), (1,)), ((), ())), preferred_element_type=jnp.float32
-    )
+def coupled(products, scale, factor, shift, places=None):
     powers = products * (-log2_e * scale) - log2_e * shift
     if places is not None:
         row = places[0] + lax.broadcasted_iota(jnp.int32, powers.shape, 0)
@@ -72,27 +69,46 @@
     return drawn
 
 
-def add_pairs(scales, shift, own_ref, rows, others, before_ref, out_ref, weights_ref, matched=False):
+def add_pairs(scales, shift, own_ref, rows, others, before_ref, out_ref, weights_ref, raw_ref=None, matched=False):
     first, block = rows
-    rows = slice(first, first + block)
-    own = own_ref[rows, :]
+    own = own_ref[first : first + block, :]
+    pieces = strips(block, SLICE)
     places, left = [], 0
     for (scale, factor), other_ref in zip(scales, others):
         count, width = other_ref.shape
         for top, bottom in strips(count, STRIP):
-            weights_ref[rows, left + top : left + bottom] = coupling(
-                own, other_ref[top:bottom, :], scale, factor, shift, (first, top) if matched else None
+            products = lax.dot_general(
+                own, other_ref[top:bottom, :], (((1,), (1,)), ((), ())),
+                preferred_element_type=jnp.float32,
             )
+            for low, high in pieces:
+                weights_ref[first + low : first + high, left + top : left + bottom] = coupled(
+                    products[low:high], scale, factor, shift, (first + low, top) if matched else None
+                )
         places.append(slice(left, left + count))
         left += count
+    sums = [[0.0, 0.0] for _ in pieces]
     for top, bottom in strips(width, COLUMNS):
-        total = None if before_ref is None else before_ref[rows, top:bottom]
+        total = None
         for place, other_ref in zip(places, others):
             added = jnp.dot(
-                weights_ref[rows, place], other_ref[:, top:bottom], preferred_element_type=jnp.float32
+                weights_ref[first : first + block, place], other_ref[:, top:bottom],
+                preferred_element_type=jnp.float32,
             )
             total = added if total is None else total + added
-        out_ref[rows, top:bottom] = total
+        for number, (low, high) in enumerate(pieces):
+            part = total[low:high]
+            here = slice(first + low, first + high)
+            if before_ref is not None:
+                part = part + before_ref[here, top:bottom]
+            out_ref[here, top:bottom] = part
+            if raw_ref is not None:
+                raw = raw_ref[here, top:bottom]
+                for side in range(0, bottom - top, LANES):
+                    lanes = slice(side, side + LANES)
+                    sums[number][0] += raw[:, lanes] * raw[:, lanes]
+                    sums[number][1] += raw[:, lanes] * part[:, lanes]
+    return sums
 
 
 def blocks_of(count):
@@ -112,7 +128,8 @@
     row_count, width = image_ref.shape
     for rows in blocks_of(row_count):
         add_pairs(
-            [(scale, scale)], shift, image_ref, rows, [text_ref], None, image_sum_ref, weights_ref, True
+            [(scale, scale)], shift, image_ref, rows, [text_ref], None, image_sum_ref, weights_ref,
+            matched=True,
         )
     for first, last in strips(row_count, STRIP):
         for left, right in strips(width, COLUMNS):
@@ -188,17 +205,23 @@
     *other_refs, out_ref, weights_ref, total_ref, sems = refs
     scales = scales_of(bits, scale_ref, grid_ref)
     copies = []
-    for number, (first, block) in enumerate(blocks_of(own_ref.shape[0])):
-        add_pairs(
-            scales, shift_ref[0], own_ref, (first, block), other_refs, sum_ref, total_ref, weights_ref
-        )
+    for first, block in blocks_of(own_ref.shape[0]):
+        sums = add_pairs(
+            scales, shift_ref[0], own_ref, (first, block), other_refs, sum_ref, total_ref, weights_ref,
+            raw_ref,
+        )
+        for (squares, products), (low, high) in zip(sums, strips(block, SLICE)):
+            inverse = lax.rsqrt(jnp.sum(squares, axis=-1, keepdims=True) + epsilon)
+            radial = jnp.sum(products, axis=-1, keepdims=True) * (inverse * inverse * inverse)
+            here = slice(first + low, first + high)
+            for top, bottom in strips(own_ref.shape[1], COLUMNS):
+                total_ref[here, top:bottom] = (
+                    total_ref[here, top:bottom] * inverse - raw_ref[here, top:bottom] * radial
+                )
         rows = pl.ds(first, block)
-        raw, total = raw_ref[rows, :], total_ref[rows, :]
-        inverse = lax.rsqrt(jnp.sum(raw * raw, axis=-1, keepdims=True) + epsilon)
-        unit = raw * inverse
-        radial = jnp.sum(unit * total, axis=-1, keepdims=True)
-        total_ref[rows, :] = (total - unit * radial) * inverse
-        copy = pltpu.make_async_copy(total_ref.at[rows, :], out_ref.at[rows, :], sems.at[number])
+        copy = pltpu.make_async_copy(
+            total_ref.at[rows, :], out_ref.at[rows, :], sems.at[len(copies)]
+        )
         copy.start()
         copies.append(copy)
     for copy in copies:
@@ -249,9 +272,6 @@
     )
     image_z_first = passed_along(image_first, "group", -1)
     image_z_last = passed_along(image_last, "group", -1)
-    image_first, image_last, far_texts = lax.optimization_barrier(
-        (image_first, image_last, far_texts)
-    )
     far_images_first = [exchanged(image_first, bit) for bit in far]
     for (texts, images), bit in zip(boths, near):
         image_sum, text_sum = add_near(

time: 68.7 us -> 68.8 us (level)
  starting transfers between devices: 15.2 us -> 14.2 us
  waiting for transfers between devices: 23.8 us -> 24.7 us
    ppermute x3, waiting for transfers between devices: 23.4 us -> 24.2 us  [passed_along(): return lax.ppermute(x, axis, [(i, (i + by) % count) for i in range(count)])]
where the time goes in v3:
time: 68.8 us; the launch traced here: 68.6 us
  waiting for transfers between devices  24.7 us (36%)
  Pallas kernels  24.4 us (35%)
  starting transfers between devices  14.2 us (21%)
  other arithmetic  2.68 us (4%)
  between operations  2.22 us (3%)
    pallas_call x5, Pallas kernels, call(): pl.pallas_call(body, grid=grid or (), in_specs=[SMEM] * smem + [VMEM] * (...  24.4 us
    ppermute x3, waiting for transfers between devices, passed_along(): return lax.ppermute(x, axis, [(i, (i + by) % count) for i in range(count)])  24.2 us
    ppermute x8, starting transfers between devices, exchanged(): return lax.ppermute(x, 'blk', [(i, i ^ 1 << bit) for i in range(count)])  8.72 us
    ppermute x3, starting transfers between devices, passed_along(): return lax.ppermute(x, axis, [(i, (i + by) % count) for i in range(count)])  5.5 us
    reduce_sum x2, other arithmetic, normalized(): total = jnp.sum(raw * raw, axis=-1, keepdims=True)  2.27 us
  transfers between devices with their start and end apart: 11, of which 4 were waited for; matrix products, arithmetic and copies ran while one was open for 1% of the time, Pallas kernels for 29%

profile of v3, /device:TPU:0, one launch (start us, length us, event | category | flops | bytes accessed | tf_op | source)
XLA Modules:
  0.0 68.6 jit_solution(17173604311967357146)
XLA Ops:
  0.6 2.0 %multiply_reduce_fusion = f32[512]{0:T(512)S(1)} fusion(f32[512,1152]{1,0:T(8,128)} %raw_ref.3), kind=kLoop, calls=%fused_computation.1 | loop fusion | flops 1179136 | bytes 2361344 | tf_op jit(solution)/shard_map/reduce_sum | solution.py:46
  2.7 0.3 copy-done
  3.0 0.2 multiply_convert_fusion.text_ref.own_ref
  3.2 3.1 %collective-permute-start = (bf16[512,1152]{1,0:T(8,128)(2,1)S(1)}, bf16[512,1152]{1,0:T(8,128)(2,1)S(1)}, u32[]{:S(2)}, u32[]{:S(2)}) collective-permute-start(bf16[512,1152]{1,0:T(8,128)(2,1)S(1)} %multiply_convert_fusion.text_ref.own_ref), channel_id=1, source_target_pairs={{0,1},{1,2},{2,3},{3,0},{4,5},{5,6},{6,7},{7,4},{8,9},{9,10},{10,1... | collective-permute-start | bytes 3538952 | tf_op jit(solution)/shard_map/ppermute | solution.py:252
  6.3 0.2 multiply_reduce_fusion.1
  6.5 0.2 multiply_convert_fusion.1.image_ref.own_ref
  6.7 0.6 collective-permute-start.2
  7.3 1.5 %collective-permute-start.3 = (bf16[512,1152]{1,0:T(8,128)(2,1)S(1)}, bf16[512,1152]{1,0:T(8,128)(2,1)S(1)}, u32[]{:S(2)}, u32[]{:S(2)}) collective-permute-start(bf16[512,1152]{1,0:T(8,128)(2,1)S(1)} %multiply_convert_fusion.text_ref.own_ref), channel_id=1, source_target_pairs={{0,8},{4,12},{8,0},{12,4},{16,24},{20,28},{24,16},{28,20},{1,9},{5... | collective-permute-start | bytes 3538952 | tf_op jit(solution)/shard_map/ppermute | solution.py:257
  8.8 1.5 %collective-permute-start.4 = (bf16[512,1152]{1,0:T(8,128)(2,1)S(1)}, bf16[512,1152]{1,0:T(8,128)(2,1)S(1)}, u32[]{:S(2)}, u32[]{:S(2)}) collective-permute-start(bf16[512,1152]{1,0:T(8,128)(2,1)S(1)} %multiply_convert_fusion.text_ref.own_ref), channel_id=1, source_target_pairs={{0,16},{4,20},{8,24},{12,28},{16,0},{20,4},{24,8},{28,12},{1,17},{... | collective-permute-start | bytes 3538952 | tf_op jit(solution)/shard_map/ppermute | solution.py:257
  11.7 3.0 %diagonal.1 = (f32[512,1152]{1,0:T(8,128)S(1)}, f32[512,1152]{1,0:T(8,128)S(1)}) custom-call(f32[1]{0:T(128)S(6)} %copy.7.scale_ref, f32[1]{0:T(128)S(6)} %copy.8.shift_ref, bf16[512,1152]{1,0:T(8,128)(2,1)S(1)} %multiply_convert_fusion.1.image_ref.own_ref, bf16[512,1152]{1,0:T(8,128)(2,1)S(1)} %multiply_convert_fusion.text_ref.own_ref), custom_call_target="tpu_custom_call" | custom-call | flops 2415919104 | bytes 4718592 | tf_op jit(solution)/shard_map/diagonal/pallas_call | solution.py:28
  14.7 19.5 %collective-permute-done.refs_2_ = bf16[512,1152]{1,0:T(8,128)(2,1)S(1)} collective-permute-done((bf16[512,1152]{1,0:T(8,128)(2,1)S(1)}, bf16[512,1152]{1,0:T(8,128)(2,1)S(1)}, u32[]{:S(2)}, u32[]{:S(2)}) %collective-permute-start) | collective-permute-done | bytes 1179680 | tf_op jit(solution)/shard_map/ppermute | solution.py:252
  34.3 1.7 %collective-permute-start.7 = (bf16[384,1152]{1,0:T(8,128)(2,1)S(1)}, bf16[384,1152]{1,0:T(8,128)(2,1)S(1)}, u32[]{:S(2)}, u32[]{:S(2)}) collective-permute-start(bf16[384,1152]{1,0:T(8,128)(2,1)S(1)} %slice.8), channel_id=1, source_target_pairs={{0,3},{1,0},{2,1},{3,2},{4,7},{5,4},{6,5},{7,6},{8,11},{9,8},{10,9... | collective-permute-start | bytes 2654216 | tf_op jit(solution)/shard_map/ppermute | solution.py:252
  36.0 1.5 %collective-permute-start.5 = (bf16[384,1152]{1,0:T(8,128)(2,1)S(1)}, bf16[384,1152]{1,0:T(8,128)(2,1)S(1)}, u32[]{:S(2)}, u32[]{:S(2)}) collective-permute-start(bf16[384,1152]{1,0:T(8,128)(2,1)S(1)} %slice.8), channel_id=1, source_target_pairs={{0,8},{4,12},{8,0},{12,4},{16,24},{20,28},{24,16},{28,20},{1,9},{5... | collective-permute-start | bytes 2654216 | tf_op jit(solution)/shard_map/ppermute | solution.py:257
  37.5 1.5 %collective-permute-start.6 = (bf16[384,1152]{1,0:T(8,128)(2,1)S(1)}, bf16[384,1152]{1,0:T(8,128)(2,1)S(1)}, u32[]{:S(2)}, u32[]{:S(2)}) collective-permute-start(bf16[384,1152]{1,0:T(8,128)(2,1)S(1)} %slice.8), channel_id=1, source_target_pairs={{0,16},{4,20},{8,24},{12,28},{16,0},{20,4},{24,8},{28,12},{1,17},{... | collective-permute-start | bytes 2654216 | tf_op jit(solution)/shard_map/ppermute | solution.py:257
  39.0 4.5 %add_near.1 = (f32[512,1152]{1,0:T(8,128)S(1)}, f32[512,1152]{1,0:T(8,128)S(1)}) custom-call(f32[1]{0:T(128)S(6)} %copy.7.scale_ref, f32[1]{0:T(128)S(6)} %copy.8.shift_ref, s32[2,8]{1,0:T(2,128)S(1)} %copy-done.2, bf16[512,1152]{1,0:T(8,128)(2,1)S(1)} %multiply_convert_fusion.1.image_ref.own_ref, ...), custom_call_target="tpu_custom_call" | custom-call | flops 2415919104 | bytes 4718592 | tf_op jit(solution)/shard_map/add_near/pallas_call | solution.py:28
  43.6 0.7 collective-permute-start.10
  44.3 7.3 %finish.2 = f32[512,1152]{1,0:T(8,128)} custom-call(f32[1]{0:T(128)S(6)} %copy.7.scale_ref, f32[1]{0:T(128)S(6)} %copy.8.shift_ref, s32[2,8]{1,0:T(2,128)S(1)} %copy-done.2, bf16[512,1152]{1,0:T(8,128)(2,1)S(1)} %multiply_convert_fusion.1.image_ref.own_ref, f32[512,1152]{1,0:T(8,128)S(1)} %copy-done.1, f32[512,1152]{1,0:T(8,128)S(1)} %get-tuple-element.22.sum_ref, ...), custom_call_target="tpu_custom_call" | custom-call | flops 3623878656 | bytes 4718592 | tf_op jit(solution)/shard_map/finish/pallas_call | solution.py:28
  51.6 0.6 collective-permute-start.8
  52.2 4.7 %collective-permute-done.7.refs_2_ = bf16[384,1152]{1,0:T(8,128)(2,1)S(1)} collective-permute-done((bf16[384,1152]{1,0:T(8,128)(2,1)S(1)}, bf16[384,1152]{1,0:T(8,128)(2,1)S(1)}, u32[]{:S(2)}, u32[]{:S(2)}) %collective-permute-start.7) | collective-permute-done | bytes 884768 | tf_op jit(solution)/shard_map/ppermute | solution.py:252
  56.9 1.5 %collective-permute-start.9 = (bf16[128,1152]{1,0:T(8,128)(2,1)S(1)}, bf16[128,1152]{1,0:T(8,128)(2,1)S(1)}, u32[]{:S(2)}, u32[]{:S(2)}) collective-permute-start(bf16[128,1152]{1,0:T(8,128)(2,1)S(1)} %slice.9), channel_id=1, source_target_pairs={{0,16},{4,20},{8,24},{12,28},{16,0},{20,4},{24,8},{28,12},{1,17},{... | collective-permute-start | bytes 884744 | tf_op jit(solution)/shard_map/ppermute | solution.py:257
  58.4 0.2 collective-permute-done.5.refs_0_
  58.6 0.2 collective-permute-done.6.refs_1_
  58.8 5.1 %add_up.1.sum_ref = f32[512,1152]{1,0:T(8,128)S(1)} custom-call(f32[1]{0:T(128)S(6)} %copy.7.scale_ref, f32[1]{0:T(128)S(6)} %copy.8.shift_ref, s32[2,8]{1,0:T(2,128)S(1)} %copy-done.2, bf16[512,1152]{1,0:T(8,128)(2,1)S(1)} %multiply_convert_fusion.text_ref.own_ref, f32[512,1152]{1,0:T(8,128)S(1)} %get-tuple-element.25.sum_ref, ...), custom_call_target="tpu_custom_call" | custom-call | flops 2717908992 | bytes 4718592 | tf_op jit(solution)/shard_map/add_up/pallas_call | solution.py:28
  64.0 4.4 %finish.3 = f32[512,1152]{1,0:T(8,128)} custom-call(f32[1]{0:T(128)S(6)} %copy.7.scale_ref, f32[1]{0:T(128)S(6)} %copy.8.shift_ref, s32[2,8]{1,0:T(2,128)S(1)} %copy-done.2, bf16[512,1152]{1,0:T(8,128)(2,1)S(1)} %multiply_convert_fusion.text_ref.own_ref, f32[512,1152]{1,0:T(8,128)S(1)} %copy-done, f32[512,1152]{1,0:T(8,128)S(1)} %add_up.1.sum_ref, ...), custom_call_target="tpu_custom_call" | custom-call | flops 905969664 | bytes 4718592 | tf_op jit(solution)/shard_map/finish/pallas_call | solution.py:28
  (17 shorter events, 0.1 us)
Async XLA Ops:
  0.6 2.4 %copy-start = (f32[512,1152]{1,0:T(8,128)S(1)}, f32[512,1152]{1,0:T(8,128)}, u32[]{:S(2)}) copy-start(f32[512,1152]{1,0:T(8,128)} %raw_ref.3) | copy-start | bytes 7077892
  2.7 3.6 %copy-start.1 = (f32[512,1152]{1,0:T(8,128)S(1)}, f32[512,1152]{1,0:T(8,128)}, u32[]{:S(2)}) copy-start(f32[512,1152]{1,0:T(8,128)} %raw_ref.2) | copy-start | bytes 7077892
  3.2 31.1 %collective-permute-start = (bf16[512,1152]{1,0:T(8,128)(2,1)S(1)}, bf16[512,1152]{1,0:T(8,128)(2,1)S(1)}, u32[]{:S(2)}, u32[]{:S(2)}) collective-permute-start(bf16[512,1152]{1,0:T(8,128)(2,1)S(1)} %multiply_convert_fusion.text_ref.own_ref), channel_id=1, source_target_pairs={{0,1},{1,2},{2,3},{3,0},{4,5},{5,6},{6,7},{7,4},{8,9},{9,10},{10,1... | collective-permute-start | bytes 3538952 | tf_op jit(solution)/shard_map/ppermute | solution.py:252
  6.3 29.7 %collective-permute-start.1 = (bf16[512,1152]{1,0:T(8,128)(2,1)S(1)}, bf16[512,1152]{1,0:T(8,128)(2,1)S(1)}, u32[]{:S(2)}, u32[]{:S(2)}) collective-permute-start(bf16[512,1152]{1,0:T(8,128)(2,1)S(1)} %multiply_convert_fusion.text_ref.own_ref), channel_id=1, source_target_pairs={{0,4},{4,0},{8,12},{12,8},{16,20},{20,16},{24,28},{28,24},{1,5},{5... | collective-permute-start | bytes 3538952 | tf_op jit(solution)/shard_map/ppermute | solution.py:257
  6.7 30.8 %collective-permute-start.2 = (bf16[512,1152]{1,0:T(8,128)(2,1)S(1)}, bf16[512,1152]{1,0:T(8,128)(2,1)S(1)}, u32[]{:S(2)}, u32[]{:S(2)}) collective-permute-start(bf16[512,1152]{1,0:T(8,128)(2,1)S(1)} %multiply_convert_fusion.1.image_ref.own_ref), channel_id=1, source_target_pairs={{0,4},{4,0},{8,12},{12,8},{16,20},{20,16},{24,28},{28,24},{1,5},{5... | collective-permute-start | bytes 3538952 | tf_op jit(solution)/shard_map/ppermute | solution.py:257
  7.3 36.3 %collective-permute-start.3 = (bf16[512,1152]{1,0:T(8,128)(2,1)S(1)}, bf16[512,1152]{1,0:T(8,128)(2,1)S(1)}, u32[]{:S(2)}, u32[]{:S(2)}) collective-permute-start(bf16[512,1152]{1,0:T(8,128)(2,1)S(1)} %multiply_convert_fusion.text_ref.own_ref), channel_id=1, source_target_pairs={{0,8},{4,12},{8,0},{12,4},{16,24},{20,28},{24,16},{28,20},{1,9},{5... | collective-permute-start | bytes 3538952 | tf_op jit(solution)/shard_map/ppermute | solution.py:257
  8.8 35.5 %collective-permute-start.4 = (bf16[512,1152]{1,0:T(8,128)(2,1)S(1)}, bf16[512,1152]{1,0:T(8,128)(2,1)S(1)}, u32[]{:S(2)}, u32[]{:S(2)}) collective-permute-start(bf16[512,1152]{1,0:T(8,128)(2,1)S(1)} %multiply_convert_fusion.text_ref.own_ref), channel_id=1, source_target_pairs={{0,16},{4,20},{8,24},{12,28},{16,0},{20,4},{24,8},{28,12},{1,17},{... | collective-permute-start | bytes 3538952 | tf_op jit(solution)/shard_map/ppermute | solution.py:257
  11.7 27.3 %copy-start.2 = (s32[2,8]{1,0:T(2,128)S(1)}, s32[2,8]{1,0:T(2,128)}, u32[]{:S(2)}) copy-start(s32[2,8]{1,0:T(2,128)} %grid_ref.7) | copy-start | bytes 196
  34.3 22.6 %collective-permute-start.7 = (bf16[384,1152]{1,0:T(8,128)(2,1)S(1)}, bf16[384,1152]{1,0:T(8,128)(2,1)S(1)}, u32[]{:S(2)}, u32[]{:S(2)}) collective-permute-start(bf16[384,1152]{1,0:T(8,128)(2,1)S(1)} %slice.8), channel_id=1, source_target_pairs={{0,3},{1,0},{2,1},{3,2},{4,7},{5,4},{6,5},{7,6},{8,11},{9,8},{10,9... | collective-permute-start | bytes 2654216 | tf_op jit(solution)/shard_map/ppermute | solution.py:252
  36.0 22.6 %collective-permute-start.5 = (bf16[384,1152]{1,0:T(8,128)(2,1)S(1)}, bf16[384,1152]{1,0:T(8,128)(2,1)S(1)}, u32[]{:S(2)}, u32[]{:S(2)}) collective-permute-start(bf16[384,1152]{1,0:T(8,128)(2,1)S(1)} %slice.8), channel_id=1, source_target_pairs={{0,8},{4,12},{8,0},{12,4},{16,24},{20,28},{24,16},{28,20},{1,9},{5... | collective-permute-start | bytes 2654216 | tf_op jit(solution)/shard_map/ppermute | solution.py:257
  37.5 21.3 %collective-permute-start.6 = (bf16[384,1152]{1,0:T(8,128)(2,1)S(1)}, bf16[384,1152]{1,0:T(8,128)(2,1)S(1)}, u32[]{:S(2)}, u32[]{:S(2)}) collective-permute-start(bf16[384,1152]{1,0:T(8,128)(2,1)S(1)} %slice.8), channel_id=1, source_target_pairs={{0,16},{4,20},{8,24},{12,28},{16,0},{20,4},{24,8},{28,12},{1,17},{... | collective-permute-start | bytes 2654216 | tf_op jit(solution)/shard_map/ppermute | solution.py:257
  43.6 20.4 %collective-permute-start.10 = (bf16[128,1152]{1,0:T(8,128)(2,1)S(1)}, bf16[128,1152]{1,0:T(8,128)(2,1)S(1)}, u32[]{:S(2)}, u32[]{:S(2)}) collective-permute-start(bf16[128,1152]{1,0:T(8,128)(2,1)S(1)} %slice.9), channel_id=1, source_target_pairs={{0,3},{1,0},{2,1},{3,2},{4,7},{5,4},{6,5},{7,6},{8,11},{9,8},{10,9... | collective-permute-start | bytes 884744 | tf_op jit(solution)/shard_map/ppermute | solution.py:252
  51.6 12.4 %collective-permute-start.8 = (bf16[128,1152]{1,0:T(8,128)(2,1)S(1)}, bf16[128,1152]{1,0:T(8,128)(2,1)S(1)}, u32[]{:S(2)}, u32[]{:S(2)}) collective-permute-start(bf16[128,1152]{1,0:T(8,128)(2,1)S(1)} %slice.9), channel_id=1, source_target_pairs={{0,8},{4,12},{8,0},{12,4},{16,24},{20,28},{24,16},{28,20},{1,9},{5... | collective-permute-start | bytes 884744 | tf_op jit(solution)/shard_map/ppermute | solution.py:257
  56.9 7.1 %collective-permute-start.9 = (bf16[128,1152]{1,0:T(8,128)(2,1)S(1)}, bf16[128,1152]{1,0:T(8,128)(2,1)S(1)}, u32[]{:S(2)}, u32[]{:S(2)}) collective-permute-start(bf16[128,1152]{1,0:T(8,128)(2,1)S(1)} %slice.9), channel_id=1, source_target_pairs={{0,16},{4,20},{8,24},{12,28},{16,0},{20,4},{24,8},{28,12},{1,17},{... | collective-permute-start | bytes 884744 | tf_op jit(solution)/shard_map/ppermute | solution.py:257

commit v4 on v3

--- a/solution.py
+++ b/solution.py
@@ -13,7 +13,7 @@
 MIB = 1024 * 1024
 VMEM = pl.BlockSpec(memory_space=pltpu.VMEM)
 SMEM = pl.BlockSpec(memory_space=pltpu.SMEM)
-BLOCK, STRIP, COLUMNS, SLICE, LANES = 256, 256, 384, 64, 128
+BLOCK, STRIP, COLUMNS, SLICE, LANES = 512, 256, 384, 64, 128
 
 
 def cost(rows, other_rows, width):
@@ -213,17 +213,16 @@
         for (squares, products), (low, high) in zip(sums, strips(block, SLICE)):
             inverse = lax.rsqrt(jnp.sum(squares, axis=-1, keepdims=True) + epsilon)
             radial = jnp.sum(products, axis=-1, keepdims=True) * (inverse * inverse * inverse)
-            here = slice(first + low, first + high)
+            here = pl.ds(first + low, high - low)
             for top, bottom in strips(own_ref.shape[1], COLUMNS):
                 total_ref[here, top:bottom] = (
                     total_ref[here, top:bottom] * inverse - raw_ref[here, top:bottom] * radial
                 )
-        rows = pl.ds(first, block)
-        copy = pltpu.make_async_copy(
-            total_ref.at[rows, :], out_ref.at[rows, :], sems.at[len(copies)]
-        )
-        copy.start()
-        copies.append(copy)
+            copy = pltpu.make_async_copy(
+                total_ref.at[here, :], out_ref.at[here, :], sems.at[len(copies)]
+            )
+            copy.start()
+            copies.append(copy)
     for copy in copies:
         copy.wait()
 
@@ -242,7 +241,7 @@
         scratch=[
             pltpu.VMEM((rows, count), jnp.bfloat16),
             pltpu.VMEM((rows, width), jnp.float32),
-            pltpu.SemaphoreType.DMA((len(blocks_of(rows)),)),
+            pltpu.SemaphoreType.DMA((len(strips(rows, SLICE)),)),
         ],
     )[0]
 

time: 68.8 us -> 68.7 us (level)
  no operation moved by 1% of the time
where the time goes in v4:
time: 68.7 us; the launch traced here: 68.5 us
  waiting for transfers between devices  24.7 us (36%)
  Pallas kernels  24.3 us (35%)
  starting transfers between devices  14.2 us (21%)
  other arithmetic  2.68 us (4%)
  between operations  2.21 us (3%)
    pallas_call x5, Pallas kernels, call(): pl.pallas_call(body, grid=grid or (), in_specs=[SMEM] * smem + [VMEM] * (...  24.3 us
    ppermute x3, waiting for transfers between devices, passed_along(): return lax.ppermute(x, axis, [(i, (i + by) % count) for i in range(count)])  24.2 us
    ppermute x8, starting transfers between devices, exchanged(): return lax.ppermute(x, 'blk', [(i, i ^ 1 << bit) for i in range(count)])  8.72 us
    ppermute x3, starting transfers between devices, passed_along(): return lax.ppermute(x, axis, [(i, (i + by) % count) for i in range(count)])  5.5 us
    reduce_sum x2, other arithmetic, normalized(): total = jnp.sum(raw * raw, axis=-1, keepdims=True)  2.27 us
  transfers between devices with their start and end apart: 11, of which 4 were waited for; matrix products, arithmetic and copies ran while one was open for 1% of the time, Pallas kernels for 29%

profile of v4, /device:TPU:0, one launch (start us, length us, event | category | flops | bytes accessed | tf_op | source)
XLA Modules:
  0.0 68.5 jit_solution(11728982824270414061)
XLA Ops:
  0.6 2.0 %multiply_reduce_fusion = f32[512]{0:T(512)S(1)} fusion(f32[512,1152]{1,0:T(8,128)} %raw_ref.3), kind=kLoop, calls=%fused_computation.1 | loop fusion | flops 1179136 | bytes 2361344 | tf_op jit(solution)/shard_map/reduce_sum | solution.py:46
  2.7 0.3 copy-done
  3.0 0.2 multiply_convert_fusion.text_ref.own_ref
  3.2 3.1 %collective-permute-start = (bf16[512,1152]{1,0:T(8,128)(2,1)S(1)}, bf16[512,1152]{1,0:T(8,128)(2,1)S(1)}, u32[]{:S(2)}, u32[]{:S(2)}) collective-permute-start(bf16[512,1152]{1,0:T(8,128)(2,1)S(1)} %multiply_convert_fusion.text_ref.own_ref), channel_id=1, source_target_pairs={{0,1},{1,2},{2,3},{3,0},{4,5},{5,6},{6,7},{7,4},{8,9},{9,10},{10,1... | collective-permute-start | bytes 3538952 | tf_op jit(solution)/shard_map/ppermute | solution.py:251
  6.3 0.2 multiply_reduce_fusion.1
  6.5 0.2 multiply_convert_fusion.1.image_ref.own_ref
  6.7 0.6 collective-permute-start.2
  7.3 1.5 %collective-permute-start.3 = (bf16[512,1152]{1,0:T(8,128)(2,1)S(1)}, bf16[512,1152]{1,0:T(8,128)(2,1)S(1)}, u32[]{:S(2)}, u32[]{:S(2)}) collective-permute-start(bf16[512,1152]{1,0:T(8,128)(2,1)S(1)} %multiply_convert_fusion.text_ref.own_ref), channel_id=1, source_target_pairs={{0,8},{4,12},{8,0},{12,4},{16,24},{20,28},{24,16},{28,20},{1,9},{5... | collective-permute-start | bytes 3538952 | tf_op jit(solution)/shard_map/ppermute | solution.py:256
  8.8 1.5 %collective-permute-start.4 = (bf16[512,1152]{1,0:T(8,128)(2,1)S(1)}, bf16[512,1152]{1,0:T(8,128)(2,1)S(1)}, u32[]{:S(2)}, u32[]{:S(2)}) collective-permute-start(bf16[512,1152]{1,0:T(8,128)(2,1)S(1)} %multiply_convert_fusion.text_ref.own_ref), channel_id=1, source_target_pairs={{0,16},{4,20},{8,24},{12,28},{16,0},{20,4},{24,8},{28,12},{1,17},{... | collective-permute-start | bytes 3538952 | tf_op jit(solution)/shard_map/ppermute | solution.py:256
  11.7 2.8 %diagonal.1 = (f32[512,1152]{1,0:T(8,128)S(1)}, f32[512,1152]{1,0:T(8,128)S(1)}) custom-call(f32[1]{0:T(128)S(6)} %copy.7.scale_ref, f32[1]{0:T(128)S(6)} %copy.8.shift_ref, bf16[512,1152]{1,0:T(8,128)(2,1)S(1)} %multiply_convert_fusion.1.image_ref.own_ref, bf16[512,1152]{1,0:T(8,128)(2,1)S(1)} %multiply_convert_fusion.text_ref.own_ref), custom_call_target="tpu_custom_call" | custom-call | flops 2415919104 | bytes 4718592 | tf_op jit(solution)/shard_map/diagonal/pallas_call | solution.py:28
  14.6 19.7 %collective-permute-done.refs_2_ = bf16[512,1152]{1,0:T(8,128)(2,1)S(1)} collective-permute-done((bf16[512,1152]{1,0:T(8,128)(2,1)S(1)}, bf16[512,1152]{1,0:T(8,128)(2,1)S(1)}, u32[]{:S(2)}, u32[]{:S(2)}) %collective-permute-start) | collective-permute-done | bytes 1179680 | tf_op jit(solution)/shard_map/ppermute | solution.py:251
  34.3 1.7 %collective-permute-start.7 = (bf16[384,1152]{1,0:T(8,128)(2,1)S(1)}, bf16[384,1152]{1,0:T(8,128)(2,1)S(1)}, u32[]{:S(2)}, u32[]{:S(2)}) collective-permute-start(bf16[384,1152]{1,0:T(8,128)(2,1)S(1)} %slice.8), channel_id=1, source_target_pairs={{0,3},{1,0},{2,1},{3,2},{4,7},{5,4},{6,5},{7,6},{8,11},{9,8},{10,9... | collective-permute-start | bytes 2654216 | tf_op jit(solution)/shard_map/ppermute | solution.py:251
  36.0 1.5 %collective-permute-start.5 = (bf16[384,1152]{1,0:T(8,128)(2,1)S(1)}, bf16[384,1152]{1,0:T(8,128)(2,1)S(1)}, u32[]{:S(2)}, u32[]{:S(2)}) collective-permute-start(bf16[384,1152]{1,0:T(8,128)(2,1)S(1)} %slice.8), channel_id=1, source_target_pairs={{0,8},{4,12},{8,0},{12,4},{16,24},{20,28},{24,16},{28,20},{1,9},{5... | collective-permute-start | bytes 2654216 | tf_op jit(solution)/shard_map/ppermute | solution.py:256
  37.5 1.5 %collective-permute-start.6 = (bf16[384,1152]{1,0:T(8,128)(2,1)S(1)}, bf16[384,1152]{1,0:T(8,128)(2,1)S(1)}, u32[]{:S(2)}, u32[]{:S(2)}) collective-permute-start(bf16[384,1152]{1,0:T(8,128)(2,1)S(1)} %slice.8), channel_id=1, source_target_pairs={{0,16},{4,20},{8,24},{12,28},{16,0},{20,4},{24,8},{28,12},{1,17},{... | collective-permute-start | bytes 2654216 | tf_op jit(solution)/shard_map/ppermute | solution.py:256
  39.0 4.4 %add_near.1 = (f32[512,1152]{1,0:T(8,128)S(1)}, f32[512,1152]{1,0:T(8,128)S(1)}) custom-call(f32[1]{0:T(128)S(6)} %copy.7.scale_ref, f32[1]{0:T(128)S(6)} %copy.8.shift_ref, s32[2,8]{1,0:T(2,128)S(1)} %copy-done.2, bf16[512,1152]{1,0:T(8,128)(2,1)S(1)} %multiply_convert_fusion.1.image_ref.own_ref, ...), custom_call_target="tpu_custom_call" | custom-call | flops 2415919104 | bytes 4718592 | tf_op jit(solution)/shard_map/add_near/pallas_call | solution.py:28
  43.4 0.7 collective-permute-start.10
  44.1 7.6 %finish.2 = f32[512,1152]{1,0:T(8,128)} custom-call(f32[1]{0:T(128)S(6)} %copy.7.scale_ref, f32[1]{0:T(128)S(6)} %copy.8.shift_ref, s32[2,8]{1,0:T(2,128)S(1)} %copy-done.2, bf16[512,1152]{1,0:T(8,128)(2,1)S(1)} %multiply_convert_fusion.1.image_ref.own_ref, f32[512,1152]{1,0:T(8,128)S(1)} %copy-done.1, f32[512,1152]{1,0:T(8,128)S(1)} %get-tuple-element.22.sum_ref, ...), custom_call_target="tpu_custom_call" | custom-call | flops 3623878656 | bytes 4718592 | tf_op jit(solution)/shard_map/finish/pallas_call | solution.py:28
  51.7 0.6 collective-permute-start.8
  52.3 4.5 %collective-permute-done.7.refs_2_ = bf16[384,1152]{1,0:T(8,128)(2,1)S(1)} collective-permute-done((bf16[384,1152]{1,0:T(8,128)(2,1)S(1)}, bf16[384,1152]{1,0:T(8,128)(2,1)S(1)}, u32[]{:S(2)}, u32[]{:S(2)}) %collective-permute-start.7) | collective-permute-done | bytes 884768 | tf_op jit(solution)/shard_map/ppermute | solution.py:251
  56.9 1.5 %collective-permute-start.9 = (bf16[128,1152]{1,0:T(8,128)(2,1)S(1)}, bf16[128,1152]{1,0:T(8,128)(2,1)S(1)}, u32[]{:S(2)}, u32[]{:S(2)}) collective-permute-start(bf16[128,1152]{1,0:T(8,128)(2,1)S(1)} %slice.9), channel_id=1, source_target_pairs={{0,16},{4,20},{8,24},{12,28},{16,0},{20,4},{24,8},{28,12},{1,17},{... | collective-permute-start | bytes 884744 | tf_op jit(solution)/shard_map/ppermute | solution.py:256
  58.4 0.2 collective-permute-done.5.refs_0_
  58.6 0.2 collective-permute-done.6.refs_1_
  58.8 4.9 %add_up.1.sum_ref = f32[512,1152]{1,0:T(8,128)S(1)} custom-call(f32[1]{0:T(128)S(6)} %copy.7.scale_ref, f32[1]{0:T(128)S(6)} %copy.8.shift_ref, s32[2,8]{1,0:T(2,128)S(1)} %copy-done.2, bf16[512,1152]{1,0:T(8,128)(2,1)S(1)} %multiply_convert_fusion.text_ref.own_ref, f32[512,1152]{1,0:T(8,128)S(1)} %get-tuple-element.25.sum_ref, ...), custom_call_target="tpu_custom_call" | custom-call | flops 2717908992 | bytes 4718592 | tf_op jit(solution)/shard_map/add_up/pallas_call | solution.py:28
  63.8 4.6 %finish.3 = f32[512,1152]{1,0:T(8,128)} custom-call(f32[1]{0:T(128)S(6)} %copy.7.scale_ref, f32[1]{0:T(128)S(6)} %copy.8.shift_ref, s32[2,8]{1,0:T(2,128)S(1)} %copy-done.2, bf16[512,1152]{1,0:T(8,128)(2,1)S(1)} %multiply_convert_fusion.text_ref.own_ref, f32[512,1152]{1,0:T(8,128)S(1)} %copy-done, f32[512,1152]{1,0:T(8,128)S(1)} %add_up.1.sum_ref, ...), custom_call_target="tpu_custom_call" | custom-call | flops 905969664 | bytes 4718592 | tf_op jit(solution)/shard_map/finish/pallas_call | solution.py:28
  (17 shorter events, 0.2 us)
Async XLA Ops:
  0.6 2.4 %copy-start = (f32[512,1152]{1,0:T(8,128)S(1)}, f32[512,1152]{1,0:T(8,128)}, u32[]{:S(2)}) copy-start(f32[512,1152]{1,0:T(8,128)} %raw_ref.3) | copy-start | bytes 7077892
  2.7 3.6 %copy-start.1 = (f32[512,1152]{1,0:T(8,128)S(1)}, f32[512,1152]{1,0:T(8,128)}, u32[]{:S(2)}) copy-start(f32[512,1152]{1,0:T(8,128)} %raw_ref.2) | copy-start | bytes 7077892
  3.2 31.1 %collective-permute-start = (bf16[512,1152]{1,0:T(8,128)(2,1)S(1)}, bf16[512,1152]{1,0:T(8,128)(2,1)S(1)}, u32[]{:S(2)}, u32[]{:S(2)}) collective-permute-start(bf16[512,1152]{1,0:T(8,128)(2,1)S(1)} %multiply_convert_fusion.text_ref.own_ref), channel_id=1, source_target_pairs={{0,1},{1,2},{2,3},{3,0},{4,5},{5,6},{6,7},{7,4},{8,9},{9,10},{10,1... | collective-permute-start | bytes 3538952 | tf_op jit(solution)/shard_map/ppermute | solution.py:251
  6.3 29.7 %collective-permute-start.1 = (bf16[512,1152]{1,0:T(8,128)(2,1)S(1)}, bf16[512,1152]{1,0:T(8,128)(2,1)S(1)}, u32[]{:S(2)}, u32[]{:S(2)}) collective-permute-start(bf16[512,1152]{1,0:T(8,128)(2,1)S(1)} %multiply_convert_fusion.text_ref.own_ref), channel_id=1, source_target_pairs={{0,4},{4,0},{8,12},{12,8},{16,20},{20,16},{24,28},{28,24},{1,5},{5... | collective-permute-start | bytes 3538952 | tf_op jit(solution)/shard_map/ppermute | solution.py:256
  6.7 30.8 %collective-permute-start.2 = (bf16[512,1152]{1,0:T(8,128)(2,1)S(1)}, bf16[512,1152]{1,0:T(8,128)(2,1)S(1)}, u32[]{:S(2)}, u32[]{:S(2)}) collective-permute-start(bf16[512,1152]{1,0:T(8,128)(2,1)S(1)} %multiply_convert_fusion.1.image_ref.own_ref), channel_id=1, source_target_pairs={{0,4},{4,0},{8,12},{12,8},{16,20},{20,16},{24,28},{28,24},{1,5},{5... | collective-permute-start | bytes 3538952 | tf_op jit(solution)/shard_map/ppermute | solution.py:256
  7.3 36.1 %collective-permute-start.3 = (bf16[512,1152]{1,0:T(8,128)(2,1)S(1)}, bf16[512,1152]{1,0:T(8,128)(2,1)S(1)}, u32[]{:S(2)}, u32[]{:S(2)}) collective-permute-start(bf16[512,1152]{1,0:T(8,128)(2,1)S(1)} %multiply_convert_fusion.text_ref.own_ref), channel_id=1, source_target_pairs={{0,8},{4,12},{8,0},{12,4},{16,24},{20,28},{24,16},{28,20},{1,9},{5... | collective-permute-start | bytes 3538952 | tf_op jit(solution)/shard_map/ppermute | solution.py:256
  8.8 35.3 %collective-permute-start.4 = (bf16[512,1152]{1,0:T(8,128)(2,1)S(1)}, bf16[512,1152]{1,0:T(8,128)(2,1)S(1)}, u32[]{:S(2)}, u32[]{:S(2)}) collective-permute-start(bf16[512,1152]{1,0:T(8,128)(2,1)S(1)} %multiply_convert_fusion.text_ref.own_ref), channel_id=1, source_target_pairs={{0,16},{4,20},{8,24},{12,28},{16,0},{20,4},{24,8},{28,12},{1,17},{... | collective-permute-start | bytes 3538952 | tf_op jit(solution)/shard_map/ppermute | solution.py:256
  11.7 27.3 %copy-start.2 = (s32[2,8]{1,0:T(2,128)S(1)}, s32[2,8]{1,0:T(2,128)}, u32[]{:S(2)}) copy-start(s32[2,8]{1,0:T(2,128)} %grid_ref.7) | copy-start | bytes 196
  34.3 22.6 %collective-permute-start.7 = (bf16[384,1152]{1,0:T(8,128)(2,1)S(1)}, bf16[384,1152]{1,0:T(8,128)(2,1)S(1)}, u32[]{:S(2)}, u32[]{:S(2)}) collective-permute-start(bf16[384,1152]{1,0:T(8,128)(2,1)S(1)} %slice.8), channel_id=1, source_target_pairs={{0,3},{1,0},{2,1},{3,2},{4,7},{5,4},{6,5},{7,6},{8,11},{9,8},{10,9... | collective-permute-start | bytes 2654216 | tf_op jit(solution)/shard_map/ppermute | solution.py:251
  36.0 22.6 %collective-permute-start.5 = (bf16[384,1152]{1,0:T(8,128)(2,1)S(1)}, bf16[384,1152]{1,0:T(8,128)(2,1)S(1)}, u32[]{:S(2)}, u32[]{:S(2)}) collective-permute-start(bf16[384,1152]{1,0:T(8,128)(2,1)S(1)} %slice.8), channel_id=1, source_target_pairs={{0,8},{4,12},{8,0},{12,4},{16,24},{20,28},{24,16},{28,20},{1,9},{5... | collective-permute-start | bytes 2654216 | tf_op jit(solution)/shard_map/ppermute | solution.py:256
  37.5 21.3 %collective-permute-start.6 = (bf16[384,1152]{1,0:T(8,128)(2,1)S(1)}, bf16[384,1152]{1,0:T(8,128)(2,1)S(1)}, u32[]{:S(2)}, u32[]{:S(2)}) collective-permute-start(bf16[384,1152]{1,0:T(8,128)(2,1)S(1)} %slice.8), channel_id=1, source_target_pairs={{0,16},{4,20},{8,24},{12,28},{16,0},{20,4},{24,8},{28,12},{1,17},{... | collective-permute-start | bytes 2654216 | tf_op jit(solution)/shard_map/ppermute | solution.py:256
  43.4 20.3 %collective-permute-start.10 = (bf16[128,1152]{1,0:T(8,128)(2,1)S(1)}, bf16[128,1152]{1,0:T(8,128)(2,1)S(1)}, u32[]{:S(2)}, u32[]{:S(2)}) collective-permute-start(bf16[128,1152]{1,0:T(8,128)(2,1)S(1)} %slice.9), channel_id=1, source_target_pairs={{0,3},{1,0},{2,1},{3,2},{4,7},{5,4},{6,5},{7,6},{8,11},{9,8},{10,9... | collective-permute-start | bytes 884744 | tf_op jit(solution)/shard_map/ppermute | solution.py:251
  51.7 12.0 %collective-permute-start.8 = (bf16[128,1152]{1,0:T(8,128)(2,1)S(1)}, bf16[128,1152]{1,0:T(8,128)(2,1)S(1)}, u32[]{:S(2)}, u32[]{:S(2)}) collective-permute-start(bf16[128,1152]{1,0:T(8,128)(2,1)S(1)} %slice.9), channel_id=1, source_target_pairs={{0,8},{4,12},{8,0},{12,4},{16,24},{20,28},{24,16},{28,20},{1,9},{5... | collective-permute-start | bytes 884744 | tf_op jit(solution)/shard_map/ppermute | solution.py:256
  56.9 6.9 %collective-permute-start.9 = (bf16[128,1152]{1,0:T(8,128)(2,1)S(1)}, bf16[128,1152]{1,0:T(8,128)(2,1)S(1)}, u32[]{:S(2)}, u32[]{:S(2)}) collective-permute-start(bf16[128,1152]{1,0:T(8,128)(2,1)S(1)} %slice.9), channel_id=1, source_target_pairs={{0,16},{4,20},{8,24},{12,28},{16,0},{20,4},{24,8},{28,12},{1,17},{... | collective-permute-start | bytes 884744 | tf_op jit(solution)/shard_map/ppermute | solution.py:256

commit v5 on v3

--- a/solution.py
+++ b/solution.py
@@ -13,7 +13,7 @@
 MIB = 1024 * 1024
 VMEM = pl.BlockSpec(memory_space=pltpu.VMEM)
 SMEM = pl.BlockSpec(memory_space=pltpu.SMEM)
-BLOCK, STRIP, COLUMNS, SLICE, LANES = 256, 256, 384, 64, 128
+BLOCK, STRIP, COLUMNS, SLICE, LANES = 256, 256, 256, 64, 128
 
 
 def cost(rows, other_rows, width):
@@ -111,8 +111,8 @@
     return sums
 
 
-def blocks_of(count):
-    return [(first, min(BLOCK, count - first)) for first in range(0, count, BLOCK)]
+def blocks_of(count, size=BLOCK):
+    return [(first, min(size, count - first)) for first in range(0, count, size)]
 
 
 def scales_of(bits, scale_ref, grid_ref):
@@ -205,7 +205,7 @@
     *other_refs, out_ref, weights_ref, total_ref, sems = refs
     scales = scales_of(bits, scale_ref, grid_ref)
     copies = []
-    for first, block in blocks_of(own_ref.shape[0]):
+    for first, block in blocks_of(own_ref.shape[0], BLOCK // 2):
         sums = add_pairs(
             scales, shift_ref[0], own_ref, (first, block), other_refs, sum_ref, total_ref, weights_ref,
             raw_ref,
@@ -242,7 +242,7 @@
         scratch=[
             pltpu.VMEM((rows, count), jnp.bfloat16),
             pltpu.VMEM((rows, width), jnp.float32),
-            pltpu.SemaphoreType.DMA((len(blocks_of(rows)),)),
+            pltpu.SemaphoreType.DMA((len(blocks_of(rows, BLOCK // 2)),)),
         ],
     )[0]
 
@@ -258,7 +258,7 @@
 
 
 def with_partners(bits, visual, caption, grid, scale, shift):
-    cut = visual.shape[0] * 3 // 4
+    cut = visual.shape[0] // 2
     near, far = [bit for bit in bits if bit == 0], [bit for bit in bits if bit != 0]
     text_half = normalized(caption)
     text_z = passed_along(text_half, "group", 1)
@@ -267,31 +267,25 @@
     image_first, image_last = image_half[:cut], image_half[cut:]
     boths = [(exchanged(text_half, bit), exchanged(image_half, bit)) for bit in near]
     image_sum, text_sum = diagonal(scale, shift, image_half, text_half)
-    image_first, image_last, text_z, image_sum, text_sum = lax.optimization_barrier(
-        (image_first, image_last, text_z, image_sum, text_sum)
-    )
-    image_z_first = passed_along(image_first, "group", -1)
-    image_z_last = passed_along(image_last, "group", -1)
+    image_half, image_first, image_last, text_z, image_sum, text_sum = lax.optimization_barrier(
+        (image_half, image_first, image_last, text_z, image_sum, text_sum)
+    )
+    image_z = passed_along(image_half, "group", -1)
     far_images_first = [exchanged(image_first, bit) for bit in far]
     for (texts, images), bit in zip(boths, near):
         image_sum, text_sum = add_near(
             scale, shift, grid, image_half, text_half, image_sum, text_sum, texts, images, bit
         )
+    image_last, far_texts = lax.optimization_barrier((image_last, far_texts))
+    far_images_last = [exchanged(image_last, bit) for bit in far]
     image_gradient = finish(
         scale, shift, grid, image_half, visual, image_sum, [*far_texts, text_z], [*far, None]
     )
-    text_sum, image_last, image_gradient = lax.optimization_barrier(
-        (text_sum, image_last, image_gradient)
-    )
-    far_images_last = [exchanged(image_last, bit) for bit in far[:1]]
-    image_last, image_z_first = lax.optimization_barrier((image_last, image_z_first))
-    far_images_last += [exchanged(image_last, bit) for bit in far[1:]]
-    text_sum = add_up(
-        scale, shift, grid, text_half, text_sum, [*far_images_first, image_z_first], [*far, None]
-    )
+    text_sum, image_gradient = lax.optimization_barrier((text_sum, image_gradient))
+    if far:
+        text_sum = add_up(scale, shift, grid, text_half, text_sum, far_images_first, far)
     text_gradient = finish(
-        scale, shift, grid, text_half, caption, text_sum,
-        [*far_images_last, image_z_last], [*far, None],
+        scale, shift, grid, text_half, caption, text_sum, [*far_images_last, image_z], [*far, None]
     )
     return image_gradient, text_gradient
 

time: 68.8 us -> 70.9 us (1.031)
  waiting for transfers between devices: 24.7 us -> 28.5 us
  starting transfers between devices: 14.2 us -> 12 us
    ppermute x8, waiting for transfers between devices: 0.44 us -> 8.21 us  [exchanged(): return lax.ppermute(x, 'blk', [(i, i ^ 1 << bit) for i in range(count)])]
    ppermute x3 -> x2, waiting for transfers between devices: 24.2 us -> 20.3 us  [passed_along(): return lax.ppermute(x, axis, [(i, (i + by) % count) for i in range(count)])]
    ppermute x8, starting transfers between devices: 8.72 us -> 7.14 us  [exchanged(): return lax.ppermute(x, 'blk', [(i, i ^ 1 << bit) for i in range(count)])]
    ppermute x3 -> x2, starting transfers between devices: 5.5 us -> 4.82 us  [passed_along(): return lax.ppermute(x, axis, [(i, (i + by) % count) for i in range(count)])]
  transfers between devices with their start and end apart: 11 -> 10, of which waited for: 4 -> 4; matrix products, arithmetic and copies ran while one was open for 1% -> 1% of each run, Pallas kernels for 29% -> 26%
where the time goes in v5:
time: 70.9 us; the launch traced here: 70.7 us
  waiting for transfers between devices  28.5 us (40%)
  Pallas kernels  25 us (35%)
  starting transfers between devices  12 us (17%)
  other arithmetic  2.68 us (4%)
  between operations  2.19 us (3%)
    pallas_call x5, Pallas kernels, call(): pl.pallas_call(body, grid=grid or (), in_specs=[SMEM] * smem + [VMEM] * (...  25 us
    ppermute x2, waiting for transfers between devices, passed_along(): return lax.ppermute(x, axis, [(i, (i + by) % count) for i in range(count)])  20.3 us
    ppermute x8, waiting for transfers between devices, exchanged(): return lax.ppermute(x, 'blk', [(i, i ^ 1 << bit) for i in range(count)])  8.21 us
    ppermute x8, starting transfers between devices, exchanged(): return lax.ppermute(x, 'blk', [(i, i ^ 1 << bit) for i in range(count)])  7.14 us
    ppermute x2, starting transfers between devices, passed_along(): return lax.ppermute(x, axis, [(i, (i + by) % count) for i in range(count)])  4.82 us
    reduce_sum x2, other arithmetic, normalized(): total = jnp.sum(raw * raw, axis=-1, keepdims=True)  2.27 us
  transfers between devices with their start and end apart: 10, of which 4 were waited for; matrix products, arithmetic and copies ran while one was open for 1% of the time, Pallas kernels for 26%

profile of v5, /device:TPU:0, one launch (start us, length us, event | category | flops | bytes accessed | tf_op | source)
XLA Modules:
  0.0 70.7 jit_solution(5026891702422006951)
XLA Ops:
  0.6 2.0 %multiply_reduce_fusion = f32[512]{0:T(512)S(1)} fusion(f32[512,1152]{1,0:T(8,128)} %raw_ref.3), kind=kLoop, calls=%fused_computation.1 | loop fusion | flops 1179136 | bytes 2361344 | tf_op jit(solution)/shard_map/reduce_sum | solution.py:46
  2.7 0.3 copy-done
  3.0 0.2 multiply_convert_fusion.text_ref.own_ref
  3.2 3.1 %collective-permute-start = (bf16[512,1152]{1,0:T(8,128)(2,1)S(1)}, bf16[512,1152]{1,0:T(8,128)(2,1)S(1)}, u32[]{:S(2)}, u32[]{:S(2)}) collective-permute-start(bf16[512,1152]{1,0:T(8,128)(2,1)S(1)} %multiply_convert_fusion.text_ref.own_ref), channel_id=1, source_target_pairs={{0,1},{1,2},{2,3},{3,0},{4,5},{5,6},{6,7},{7,4},{8,9},{9,10},{10,1... | collective-permute-start | bytes 3538952 | tf_op jit(solution)/shard_map/ppermute | solution.py:252
  6.3 1.5 %collective-permute-start.3 = (bf16[512,1152]{1,0:T(8,128)(2,1)S(1)}, bf16[512,1152]{1,0:T(8,128)(2,1)S(1)}, u32[]{:S(2)}, u32[]{:S(2)}) collective-permute-start(bf16[512,1152]{1,0:T(8,128)(2,1)S(1)} %multiply_convert_fusion.text_ref.own_ref), channel_id=1, source_target_pairs={{0,8},{4,12},{8,0},{12,4},{16,24},{20,28},{24,16},{28,20},{1,9},{5... | collective-permute-start | bytes 3538952 | tf_op jit(solution)/shard_map/ppermute | solution.py:257
  7.8 1.5 %collective-permute-start.4 = (bf16[512,1152]{1,0:T(8,128)(2,1)S(1)}, bf16[512,1152]{1,0:T(8,128)(2,1)S(1)}, u32[]{:S(2)}, u32[]{:S(2)}) collective-permute-start(bf16[512,1152]{1,0:T(8,128)(2,1)S(1)} %multiply_convert_fusion.text_ref.own_ref), channel_id=1, source_target_pairs={{0,16},{4,20},{8,24},{12,28},{16,0},{20,4},{24,8},{28,12},{1,17},{... | collective-permute-start | bytes 3538952 | tf_op jit(solution)/shard_map/ppermute | solution.py:257
  9.3 0.2 multiply_reduce_fusion.1
  9.5 0.2 multiply_convert_fusion.1.image_ref.own_ref
  9.8 0.1 collective-permute-start.2
  11.1 2.7 %diagonal.1 = (f32[512,1152]{1,0:T(8,128)S(1)}, f32[512,1152]{1,0:T(8,128)S(1)}) custom-call(f32[1]{0:T(128)S(6)} %copy.7.scale_ref, f32[1]{0:T(128)S(6)} %copy.8.shift_ref, bf16[512,1152]{1,0:T(8,128)(2,1)S(1)} %multiply_convert_fusion.1.image_ref.own_ref, bf16[512,1152]{1,0:T(8,128)(2,1)S(1)} %multiply_convert_fusion.text_ref.own_ref), custom_call_target="tpu_custom_call" | custom-call | flops 2415919104 | bytes 4718592 | tf_op jit(solution)/shard_map/diagonal/pallas_call | solution.py:28
  13.9 0.1 fusion
  14.0 20.3 %collective-permute-done.refs_2_ = bf16[512,1152]{1,0:T(8,128)(2,1)S(1)} collective-permute-done((bf16[512,1152]{1,0:T(8,128)(2,1)S(1)}, bf16[512,1152]{1,0:T(8,128)(2,1)S(1)}, u32[]{:S(2)}, u32[]{:S(2)}) %collective-permute-start) | collective-permute-done | bytes 1179680 | tf_op jit(solution)/shard_map/ppermute | solution.py:252
  34.3 1.7 %collective-permute-start.9 = (bf16[512,1152]{1,0:T(8,128)(2,1)S(1)}, bf16[512,1152]{1,0:T(8,128)(2,1)S(1)}, u32[]{:S(2)}, u32[]{:S(2)}) collective-permute-start(bf16[512,1152]{1,0:T(8,128)(2,1)S(1)} %multiply_convert_fusion.1.image_ref.own_ref), channel_id=1, source_target_pairs={{0,3},{1,0},{2,1},{3,2},{4,7},{5,4},{6,5},{7,6},{8,11},{9,8},{10,9... | collective-permute-start | bytes 3538952 | tf_op jit(solution)/shard_map/ppermute | solution.py:252
  36.0 1.5 %collective-permute-start.5 = (bf16[256,1152]{1,0:T(8,128)(2,1)S(1)}, bf16[256,1152]{1,0:T(8,128)(2,1)S(1)}, u32[]{:S(2)}, u32[]{:S(2)}) collective-permute-start(bf16[256,1152]{1,0:T(8,128)(2,1)S(1)} %get-tuple-element.30), channel_id=1, source_target_pairs={{0,8},{4,12},{8,0},{12,4},{16,24},{20,28},{24,16},{28,20},{1,9},{5... | collective-permute-start | bytes 1769480 | tf_op jit(solution)/shard_map/ppermute | solution.py:257
  37.5 1.5 %collective-permute-start.6 = (bf16[256,1152]{1,0:T(8,128)(2,1)S(1)}, bf16[256,1152]{1,0:T(8,128)(2,1)S(1)}, u32[]{:S(2)}, u32[]{:S(2)}) collective-permute-start(bf16[256,1152]{1,0:T(8,128)(2,1)S(1)} %get-tuple-element.30), channel_id=1, source_target_pairs={{0,16},{4,20},{8,24},{12,28},{16,0},{20,4},{24,8},{28,12},{1,17},{... | collective-permute-start | bytes 1769480 | tf_op jit(solution)/shard_map/ppermute | solution.py:257
  39.0 0.5 collective-permute-start.7
  39.6 0.5 collective-permute-start.8
  40.1 4.3 %add_near.1 = (f32[512,1152]{1,0:T(8,128)S(1)}, f32[512,1152]{1,0:T(8,128)S(1)}) custom-call(f32[1]{0:T(128)S(6)} %copy.7.scale_ref, f32[1]{0:T(128)S(6)} %copy.8.shift_ref, s32[2,8]{1,0:T(2,128)S(1)} %copy-done.2, bf16[512,1152]{1,0:T(8,128)(2,1)S(1)} %multiply_convert_fusion.1.image_ref.own_ref, ...), custom_call_target="tpu_custom_call" | custom-call | flops 2415919104 | bytes 4718592 | tf_op jit(solution)/shard_map/add_near/pallas_call | solution.py:28
  44.4 8.7 %finish.2 = f32[512,1152]{1,0:T(8,128)} custom-call(f32[1]{0:T(128)S(6)} %copy.7.scale_ref, f32[1]{0:T(128)S(6)} %copy.8.shift_ref, s32[2,8]{1,0:T(2,128)S(1)} %copy-done.2, bf16[512,1152]{1,0:T(8,128)(2,1)S(1)} %multiply_convert_fusion.1.image_ref.own_ref, f32[512,1152]{1,0:T(8,128)S(1)} %copy-done.1, f32[512,1152]{1,0:T(8,128)S(1)} %get-tuple-element.23.sum_ref, ...), custom_call_target="tpu_custom_call" | custom-call | flops 3623878656 | bytes 4718592 | tf_op jit(solution)/shard_map/finish/pallas_call | solution.py:28
  53.1 0.7 collective-permute-done.6.refs_1_
  53.8 2.5 %add_up.1.sum_ref = f32[512,1152]{1,0:T(8,128)S(1)} custom-call(f32[1]{0:T(128)S(6)} %copy.7.scale_ref, f32[1]{0:T(128)S(6)} %copy.8.shift_ref, s32[2,8]{1,0:T(2,128)S(1)} %copy-done.2, bf16[512,1152]{1,0:T(8,128)(2,1)S(1)} %multiply_convert_fusion.text_ref.own_ref, f32[512,1152]{1,0:T(8,128)S(1)} %get-tuple-element.29.sum_ref, ...), custom_call_target="tpu_custom_call" | custom-call | flops 1207959552 | bytes 4718592 | tf_op jit(solution)/shard_map/add_up/pallas_call | solution.py:28
  56.3 6.3 %collective-permute-done.7.refs_0_ = bf16[256,1152]{1,0:T(8,128)(2,1)S(1)} collective-permute-done((bf16[256,1152]{1,0:T(8,128)(2,1)S(1)}, bf16[256,1152]{1,0:T(8,128)(2,1)S(1)}, u32[]{:S(2)}, u32[]{:S(2)}) %collective-permute-start.7) | collective-permute-done | bytes 589856 | tf_op jit(solution)/shard_map/ppermute | solution.py:257
  62.6 1.2 %collective-permute-done.8.refs_1_ = bf16[256,1152]{1,0:T(8,128)(2,1)S(1)} collective-permute-done((bf16[256,1152]{1,0:T(8,128)(2,1)S(1)}, bf16[256,1152]{1,0:T(8,128)(2,1)S(1)}, u32[]{:S(2)}, u32[]{:S(2)}) %collective-permute-start.8) | collective-permute-done | bytes 589856 | tf_op jit(solution)/shard_map/ppermute | solution.py:257
  63.8 6.8 %finish.3 = f32[512,1152]{1,0:T(8,128)} custom-call(f32[1]{0:T(128)S(6)} %copy.7.scale_ref, f32[1]{0:T(128)S(6)} %copy.8.shift_ref, s32[2,8]{1,0:T(2,128)S(1)} %copy-done.2, bf16[512,1152]{1,0:T(8,128)(2,1)S(1)} %multiply_convert_fusion.text_ref.own_ref, f32[512,1152]{1,0:T(8,128)S(1)} %copy-done, f32[512,1152]{1,0:T(8,128)S(1)} %add_up.1.sum_ref, ...), custom_call_target="tpu_custom_call" | custom-call | flops 2415919104 | bytes 4718592 | tf_op jit(solution)/shard_map/finish/pallas_call | solution.py:28
  (14 shorter events, 0.0 us)
Async XLA Ops:
  0.6 2.4 %copy-start = (f32[512,1152]{1,0:T(8,128)S(1)}, f32[512,1152]{1,0:T(8,128)}, u32[]{:S(2)}) copy-start(f32[512,1152]{1,0:T(8,128)} %raw_ref.3) | copy-start | bytes 7077892
  2.7 6.6 %copy-start.1 = (f32[512,1152]{1,0:T(8,128)S(1)}, f32[512,1152]{1,0:T(8,128)}, u32[]{:S(2)}) copy-start(f32[512,1152]{1,0:T(8,128)} %raw_ref.2) | copy-start | bytes 7077892
  3.2 31.1 %collective-permute-start = (bf16[512,1152]{1,0:T(8,128)(2,1)S(1)}, bf16[512,1152]{1,0:T(8,128)(2,1)S(1)}, u32[]{:S(2)}, u32[]{:S(2)}) collective-permute-start(bf16[512,1152]{1,0:T(8,128)(2,1)S(1)} %multiply_convert_fusion.text_ref.own_ref), channel_id=1, source_target_pairs={{0,1},{1,2},{2,3},{3,0},{4,5},{5,6},{6,7},{7,4},{8,9},{9,10},{10,1... | collective-permute-start | bytes 3538952 | tf_op jit(solution)/shard_map/ppermute | solution.py:252
  6.3 32.8 %collective-permute-start.1 = (bf16[512,1152]{1,0:T(8,128)(2,1)S(1)}, bf16[512,1152]{1,0:T(8,128)(2,1)S(1)}, u32[]{:S(2)}, u32[]{:S(2)}) collective-permute-start(bf16[512,1152]{1,0:T(8,128)(2,1)S(1)} %multiply_convert_fusion.text_ref.own_ref), channel_id=1, source_target_pairs={{0,4},{4,0},{8,12},{12,8},{16,20},{20,16},{24,28},{28,24},{1,5},{5... | collective-permute-start | bytes 3538952 | tf_op jit(solution)/shard_map/ppermute | solution.py:257
  6.3 29.7 %collective-permute-start.3 = (bf16[512,1152]{1,0:T(8,128)(2,1)S(1)}, bf16[512,1152]{1,0:T(8,128)(2,1)S(1)}, u32[]{:S(2)}, u32[]{:S(2)}) collective-permute-start(bf16[512,1152]{1,0:T(8,128)(2,1)S(1)} %multiply_convert_fusion.text_ref.own_ref), channel_id=1, source_target_pairs={{0,8},{4,12},{8,0},{12,4},{16,24},{20,28},{24,16},{28,20},{1,9},{5... | collective-permute-start | bytes 3538952 | tf_op jit(solution)/shard_map/ppermute | solution.py:257
  7.8 29.7 %collective-permute-start.4 = (bf16[512,1152]{1,0:T(8,128)(2,1)S(1)}, bf16[512,1152]{1,0:T(8,128)(2,1)S(1)}, u32[]{:S(2)}, u32[]{:S(2)}) collective-permute-start(bf16[512,1152]{1,0:T(8,128)(2,1)S(1)} %multiply_convert_fusion.text_ref.own_ref), channel_id=1, source_target_pairs={{0,16},{4,20},{8,24},{12,28},{16,0},{20,4},{24,8},{28,12},{1,17},{... | collective-permute-start | bytes 3538952 | tf_op jit(solution)/shard_map/ppermute | solution.py:257
  9.8 29.8 %collective-permute-start.2 = (bf16[512,1152]{1,0:T(8,128)(2,1)S(1)}, bf16[512,1152]{1,0:T(8,128)(2,1)S(1)}, u32[]{:S(2)}, u32[]{:S(2)}) collective-permute-start(bf16[512,1152]{1,0:T(8,128)(2,1)S(1)} %multiply_convert_fusion.1.image_ref.own_ref), channel_id=1, source_target_pairs={{0,4},{4,0},{8,12},{12,8},{16,20},{20,16},{24,28},{28,24},{1,5},{5... | collective-permute-start | bytes 3538952 | tf_op jit(solution)/shard_map/ppermute | solution.py:257
  13.9 26.2 %copy-start.2 = (s32[2,8]{1,0:T(2,128)S(1)}, s32[2,8]{1,0:T(2,128)}, u32[]{:S(2)}) copy-start(s32[2,8]{1,0:T(2,128)} %grid_ref.7) | copy-start | bytes 196
  34.3 29.5 %collective-permute-start.9 = (bf16[512,1152]{1,0:T(8,128)(2,1)S(1)}, bf16[512,1152]{1,0:T(8,128)(2,1)S(1)}, u32[]{:S(2)}, u32[]{:S(2)}) collective-permute-start(bf16[512,1152]{1,0:T(8,128)(2,1)S(1)} %multiply_convert_fusion.1.image_ref.own_ref), channel_id=1, source_target_pairs={{0,3},{1,0},{2,1},{3,2},{4,7},{5,4},{6,5},{7,6},{8,11},{9,8},{10,9... | collective-permute-start | bytes 3538952 | tf_op jit(solution)/shard_map/ppermute | solution.py:252
  36.0 17.1 %collective-permute-start.5 = (bf16[256,1152]{1,0:T(8,128)(2,1)S(1)}, bf16[256,1152]{1,0:T(8,128)(2,1)S(1)}, u32[]{:S(2)}, u32[]{:S(2)}) collective-permute-start(bf16[256,1152]{1,0:T(8,128)(2,1)S(1)} %get-tuple-element.30), channel_id=1, source_target_pairs={{0,8},{4,12},{8,0},{12,4},{16,24},{20,28},{24,16},{28,20},{1,9},{5... | collective-permute-start | bytes 1769480 | tf_op jit(solution)/shard_map/ppermute | solution.py:257
  37.5 16.3 %collective-permute-start.6 = (bf16[256,1152]{1,0:T(8,128)(2,1)S(1)}, bf16[256,1152]{1,0:T(8,128)(2,1)S(1)}, u32[]{:S(2)}, u32[]{:S(2)}) collective-permute-start(bf16[256,1152]{1,0:T(8,128)(2,1)S(1)} %get-tuple-element.30), channel_id=1, source_target_pairs={{0,16},{4,20},{8,24},{12,28},{16,0},{20,4},{24,8},{28,12},{1,17},{... | collective-permute-start | bytes 1769480 | tf_op jit(solution)/shard_map/ppermute | solution.py:257
  39.0 23.5 %collective-permute-start.7 = (bf16[256,1152]{1,0:T(8,128)(2,1)S(1)}, bf16[256,1152]{1,0:T(8,128)(2,1)S(1)}, u32[]{:S(2)}, u32[]{:S(2)}) collective-permute-start(bf16[256,1152]{1,0:T(8,128)(2,1)S(1)} %get-tuple-element.31), channel_id=1, source_target_pairs={{0,8},{4,12},{8,0},{12,4},{16,24},{20,28},{24,16},{28,20},{1,9},{5... | collective-permute-start | bytes 1769480 | tf_op jit(solution)/shard_map/ppermute | solution.py:257
  39.6 24.2 %collective-permute-start.8 = (bf16[256,1152]{1,0:T(8,128)(2,1)S(1)}, bf16[256,1152]{1,0:T(8,128)(2,1)S(1)}, u32[]{:S(2)}, u32[]{:S(2)}) collective-permute-start(bf16[256,1152]{1,0:T(8,128)(2,1)S(1)} %get-tuple-element.31), channel_id=1, source_target_pairs={{0,16},{4,20},{8,24},{12,28},{16,0},{20,4},{24,8},{28,12},{1,17},{... | collective-permute-start | bytes 1769480 | tf_op jit(solution)/shard_map/ppermute | solution.py:257

commit v6 on v4

--- a/solution.py
+++ b/solution.py
@@ -13,7 +13,7 @@
 MIB = 1024 * 1024
 VMEM = pl.BlockSpec(memory_space=pltpu.VMEM)
 SMEM = pl.BlockSpec(memory_space=pltpu.SMEM)
-BLOCK, STRIP, COLUMNS, SLICE, LANES = 512, 256, 384, 64, 128
+BLOCK, STRIP, COLUMNS, SLICE, LANES = 256, 256, 256, 64, 128
 
 
 def cost(rows, other_rows, width):
@@ -69,18 +69,48 @@
     return drawn
 
 
-def add_pairs(scales, shift, own_ref, rows, others, before_ref, out_ref, weights_ref, raw_ref=None, matched=False):
+def side_by_side(others, all_ref):
+    if all_ref is None:
+        return others
+    left = 0
+    for other_ref in others:
+        count = other_ref.shape[0]
+        all_ref[left : left + count, :] = other_ref[...]
+        left += count
+    return [all_ref]
+
+
+def factors_of(factors, counts, top, bottom):
+    last, column = None, None
+    edge = 0
+    for factor, count in zip(factors, counts):
+        if top < edge + count and edge < bottom:
+            if last is None:
+                last = factor
+            else:
+                if column is None:
+                    column = top + lax.broadcasted_iota(jnp.int32, (1, bottom - top), 1)
+                last = jnp.where(column < edge, last, factor)
+        edge += count
+    return last
+
+
+def add_pairs(
+    scale, factors, shift, own_ref, rows, counts, others, before_ref, out_ref, weights_ref,
+    raw_ref=None, matched=False,
+):
     first, block = rows
     own = own_ref[first : first + block, :]
     pieces = strips(block, SLICE)
     places, left = [], 0
-    for (scale, factor), other_ref in zip(scales, others):
+    for other_ref in others:
         count, width = other_ref.shape
         for top, bottom in strips(count, STRIP):
             products = lax.dot_general(
                 own, other_ref[top:bottom, :], (((1,), (1,)), ((), ())),
                 preferred_element_type=jnp.float32,
             )
+            factor = factors_of(factors, counts, left + top, left + bottom)
             for low, high in pieces:
                 weights_ref[first + low : first + high, left + top : left + bottom] = coupled(
                     products[low:high], scale, factor, shift, (first + low, top) if matched else None
@@ -115,12 +145,18 @@
     return [(first, min(BLOCK, count - first)) for first in range(0, count, BLOCK)]
 
 
-def scales_of(bits, scale_ref, grid_ref):
+def drawn_factors(bits, scale_ref, grid_ref):
     scale = scale_ref[0]
     return [
-        (scale, scale if bit is None else jnp.where(is_drawn(grid_ref, bit), scale, 0.0))
-        for bit in bits
+        scale if bit is None else jnp.where(is_drawn(grid_ref, bit), scale, 0.0) for bit in bits
     ]
+
+
+def all_scratch(others):
+    count, width = sum(x.shape[0] for x in others), others[0].shape[1]
+    if all(x.shape[0] % STRIP == 0 for x in others):
+        return []
+    return [pltpu.VMEM((count, width), jnp.bfloat16)]
 
 
 def diagonal_kernel(scale_ref, shift_ref, image_ref, text_ref, image_sum_ref, text_sum_ref, weights_ref):
@@ -128,8 +164,8 @@
     row_count, width = image_ref.shape
     for rows in blocks_of(row_count):
         add_pairs(
-            [(scale, scale)], shift, image_ref, rows, [text_ref], None, image_sum_ref, weights_ref,
-            matched=True,
+            scale, [scale], shift, image_ref, rows, [row_count], [text_ref], None, image_sum_ref,
+            weights_ref, matched=True,
         )
     for first, last in strips(row_count, STRIP):
         for left, right in strips(width, COLUMNS):
@@ -155,16 +191,18 @@
     bit, scale_ref, shift_ref, grid_ref, image_ref, text_ref, image_sum_ref, text_sum_ref, texts_ref,
     images_ref, image_out_ref, text_out_ref, weights_ref,
 ):
-    scales, shift = scales_of([bit], scale_ref, grid_ref), shift_ref[0]
+    scale, shift = scale_ref[0], shift_ref[0]
+    factors = drawn_factors([bit], scale_ref, grid_ref)
     row_count = image_ref.shape[0]
-    for rows in blocks_of(row_count):
-        add_pairs(
-            scales, shift, image_ref, rows, [texts_ref], image_sum_ref, image_out_ref, weights_ref
-        )
-    for rows in blocks_of(row_count):
-        add_pairs(
-            scales, shift, text_ref, rows, [images_ref], text_sum_ref, text_out_ref, weights_ref
-        )
+    for own_ref, other_ref, sum_ref, out_ref in (
+        (image_ref, texts_ref, image_sum_ref, image_out_ref),
+        (text_ref, images_ref, text_sum_ref, text_out_ref),
+    ):
+        for rows in blocks_of(row_count):
+            add_pairs(
+                scale, factors, shift, own_ref, rows, [row_count], [other_ref], sum_ref, out_ref,
+                weights_ref,
+            )
 
 
 def add_near(scale, shift, grid, image_half, text_half, image_sum, text_sum, texts, images, bit):
@@ -181,10 +219,15 @@
 
 
 def add_up_kernel(bits, scale_ref, shift_ref, grid_ref, own_ref, sum_ref, *refs):
-    *other_refs, out_ref, weights_ref = refs
-    scales = scales_of(bits, scale_ref, grid_ref)
+    other_refs, (out_ref, weights_ref, *all_refs) = refs[: len(bits)], refs[len(bits) :]
+    factors = drawn_factors(bits, scale_ref, grid_ref)
+    counts = [x.shape[0] for x in other_refs]
+    others = side_by_side(other_refs, *(all_refs or [None]))
     for rows in blocks_of(own_ref.shape[0]):
-        add_pairs(scales, shift_ref[0], own_ref, rows, other_refs, sum_ref, out_ref, weights_ref)
+        add_pairs(
+            scale_ref[0], factors, shift_ref[0], own_ref, rows, counts, others, sum_ref, out_ref,
+            weights_ref,
+        )
 
 
 def add_up(scale, shift, grid, own, total, others, bits):
@@ -197,18 +240,20 @@
         [((rows, width), jnp.float32)],
         (rows, count, width),
         smem=3,
-        scratch=[pltpu.VMEM((rows, count), jnp.bfloat16)],
+        scratch=[pltpu.VMEM((rows, count), jnp.bfloat16), *all_scratch(others)],
     )[0]
 
 
 def finish_kernel(bits, scale_ref, shift_ref, grid_ref, own_ref, raw_ref, sum_ref, *refs):
-    *other_refs, out_ref, weights_ref, total_ref, sems = refs
-    scales = scales_of(bits, scale_ref, grid_ref)
+    other_refs, (out_ref, weights_ref, total_ref, sems, *all_refs) = refs[: len(bits)], refs[len(bits) :]
+    factors = drawn_factors(bits, scale_ref, grid_ref)
+    counts = [x.shape[0] for x in other_refs]
+    others = side_by_side(other_refs, *(all_refs or [None]))
     copies = []
     for first, block in blocks_of(own_ref.shape[0]):
         sums = add_pairs(
-            scales, shift_ref[0], own_ref, (first, block), other_refs, sum_ref, total_ref, weights_ref,
-            raw_ref,
+            scale_ref[0], factors, shift_ref[0], own_ref, (first, block), counts, others, sum_ref,
+            total_ref, weights_ref, raw_ref,
         )
         for (squares, products), (low, high) in zip(sums, strips(block, SLICE)):
             inverse = lax.rsqrt(jnp.sum(squares, axis=-1, keepdims=True) + epsilon)
@@ -242,6 +287,7 @@
             pltpu.VMEM((rows, count), jnp.bfloat16),
             pltpu.VMEM((rows, width), jnp.float32),
             pltpu.SemaphoreType.DMA((len(strips(rows, SLICE)),)),
+            *all_scratch(others),
         ],
     )[0]
 

time: 68.7 us -> 68 us (0.990)
  Pallas kernels: 24.3 us -> 22.1 us
  waiting for transfers between devices: 24.7 us -> 26.2 us
    pallas_call x5, Pallas kernels: 24.3 us -> 22.1 us  [call(): pl.pallas_call(body, grid=grid or (), in_specs=[SMEM] * smem + [VMEM] * (...]
    ppermute x3, waiting for transfers between devices: 24.2 us -> 25.4 us  [passed_along(): return lax.ppermute(x, axis, [(i, (i + by) % count) for i in range(count)])]
  transfers between devices with their start and end apart: 11 -> 11, of which waited for: 4 -> 5; matrix products, arithmetic and copies ran while one was open for 1% -> 1% of each run, Pallas kernels for 29% -> 27%
where the time goes in v6:
time: 68 us; the launch traced here: 67.8 us
  waiting for transfers between devices  26.2 us (39%)
  Pallas kernels  22.1 us (32%)
  starting transfers between devices  14.2 us (21%)
  other arithmetic  2.68 us (4%)
  between operations  2.2 us (3%)
    ppermute x3, waiting for transfers between devices, passed_along(): return lax.ppermute(x, axis, [(i, (i + by) % count) for i in range(count)])  25.4 us
    pallas_call x5, Pallas kernels, call(): pl.pallas_call(body, grid=grid or (), in_specs=[SMEM] * smem + [VMEM] * (...  22.1 us
    ppermute x8, starting transfers between devices, exchanged(): return lax.ppermute(x, 'blk', [(i, i ^ 1 << bit) for i in range(count)])  8.69 us
    ppermute x3, starting transfers between devices, passed_along(): return lax.ppermute(x, axis, [(i, (i + by) % count) for i in range(count)])  5.52 us
    reduce_sum x2, other arithmetic, normalized(): total = jnp.sum(raw * raw, axis=-1, keepdims=True)  2.27 us
  transfers between devices with their start and end apart: 11, of which 5 were waited for; matrix products, arithmetic and copies ran while one was open for 1% of the time, Pallas kernels for 27%

profile of v6, /device:TPU:0, one launch (start us, length us, event | category | flops | bytes accessed | tf_op | source)
XLA Modules:
  0.0 67.8 jit_solution(478797899029261379)
XLA Ops:
  0.6 2.0 %multiply_reduce_fusion = f32[512]{0:T(512)S(1)} fusion(f32[512,1152]{1,0:T(8,128)} %raw_ref.3), kind=kLoop, calls=%fused_computation.1 | loop fusion | flops 1179136 | bytes 2361344 | tf_op jit(solution)/shard_map/reduce_sum | solution.py:46
  2.7 0.3 copy-done
  3.2 3.1 %collective-permute-start = (bf16[512,1152]{1,0:T(8,128)(2,1)S(1)}, bf16[512,1152]{1,0:T(8,128)(2,1)S(1)}, u32[]{:S(2)}, u32[]{:S(2)}) collective-permute-start(bf16[512,1152]{1,0:T(8,128)(2,1)S(1)} %multiply_convert_fusion.text_ref.own_ref), channel_id=1, source_target_pairs={{0,1},{1,2},{2,3},{3,0},{4,5},{5,6},{6,7},{7,4},{8,9},{9,10},{10,1... | collective-permute-start | bytes 3538952 | tf_op jit(solution)/shard_map/ppermute | solution.py:297
  6.3 0.2 multiply_reduce_fusion.1
  6.5 0.2 multiply_convert_fusion.1.image_ref.own_ref
  6.7 0.6 collective-permute-start.2
  7.3 1.5 %collective-permute-start.3 = (bf16[512,1152]{1,0:T(8,128)(2,1)S(1)}, bf16[512,1152]{1,0:T(8,128)(2,1)S(1)}, u32[]{:S(2)}, u32[]{:S(2)}) collective-permute-start(bf16[512,1152]{1,0:T(8,128)(2,1)S(1)} %multiply_convert_fusion.text_ref.own_ref), channel_id=1, source_target_pairs={{0,8},{4,12},{8,0},{12,4},{16,24},{20,28},{24,16},{28,20},{1,9},{5... | collective-permute-start | bytes 3538952 | tf_op jit(solution)/shard_map/ppermute | solution.py:302
  8.8 1.5 %collective-permute-start.4 = (bf16[512,1152]{1,0:T(8,128)(2,1)S(1)}, bf16[512,1152]{1,0:T(8,128)(2,1)S(1)}, u32[]{:S(2)}, u32[]{:S(2)}) collective-permute-start(bf16[512,1152]{1,0:T(8,128)(2,1)S(1)} %multiply_convert_fusion.text_ref.own_ref), channel_id=1, source_target_pairs={{0,16},{4,20},{8,24},{12,28},{16,0},{20,4},{24,8},{28,12},{1,17},{... | collective-permute-start | bytes 3538952 | tf_op jit(solution)/shard_map/ppermute | solution.py:302
  11.7 2.7 %diagonal.1 = (f32[512,1152]{1,0:T(8,128)S(1)}, f32[512,1152]{1,0:T(8,128)S(1)}) custom-call(f32[1]{0:T(128)S(6)} %copy.7.scale_ref, f32[1]{0:T(128)S(6)} %copy.8.shift_ref, bf16[512,1152]{1,0:T(8,128)(2,1)S(1)} %multiply_convert_fusion.1.image_ref.own_ref, bf16[512,1152]{1,0:T(8,128)(2,1)S(1)} %multiply_convert_fusion.text_ref.own_ref), custom_call_target="tpu_custom_call" | custom-call | flops 2415919104 | bytes 4718592 | tf_op jit(solution)/shard_map/diagonal/pallas_call | solution.py:28
  14.5 19.8 %collective-permute-done.refs_2_ = bf16[512,1152]{1,0:T(8,128)(2,1)S(1)} collective-permute-done((bf16[512,1152]{1,0:T(8,128)(2,1)S(1)}, bf16[512,1152]{1,0:T(8,128)(2,1)S(1)}, u32[]{:S(2)}, u32[]{:S(2)}) %collective-permute-start) | collective-permute-done | bytes 1179680 | tf_op jit(solution)/shard_map/ppermute | solution.py:297
  34.3 1.7 %collective-permute-start.7 = (bf16[384,1152]{1,0:T(8,128)(2,1)S(1)}, bf16[384,1152]{1,0:T(8,128)(2,1)S(1)}, u32[]{:S(2)}, u32[]{:S(2)}) collective-permute-start(bf16[384,1152]{1,0:T(8,128)(2,1)S(1)} %slice.8), channel_id=1, source_target_pairs={{0,3},{1,0},{2,1},{3,2},{4,7},{5,4},{6,5},{7,6},{8,11},{9,8},{10,9... | collective-permute-start | bytes 2654216 | tf_op jit(solution)/shard_map/ppermute | solution.py:297
  36.0 1.5 %collective-permute-start.5 = (bf16[384,1152]{1,0:T(8,128)(2,1)S(1)}, bf16[384,1152]{1,0:T(8,128)(2,1)S(1)}, u32[]{:S(2)}, u32[]{:S(2)}) collective-permute-start(bf16[384,1152]{1,0:T(8,128)(2,1)S(1)} %slice.8), channel_id=1, source_target_pairs={{0,8},{4,12},{8,0},{12,4},{16,24},{20,28},{24,16},{28,20},{1,9},{5... | collective-permute-start | bytes 2654216 | tf_op jit(solution)/shard_map/ppermute | solution.py:302
  37.5 1.5 %collective-permute-start.6 = (bf16[384,1152]{1,0:T(8,128)(2,1)S(1)}, bf16[384,1152]{1,0:T(8,128)(2,1)S(1)}, u32[]{:S(2)}, u32[]{:S(2)}) collective-permute-start(bf16[384,1152]{1,0:T(8,128)(2,1)S(1)} %slice.8), channel_id=1, source_target_pairs={{0,16},{4,20},{8,24},{12,28},{16,0},{20,4},{24,8},{28,12},{1,17},{... | collective-permute-start | bytes 2654216 | tf_op jit(solution)/shard_map/ppermute | solution.py:302
  39.0 4.2 %add_near.1 = (f32[512,1152]{1,0:T(8,128)S(1)}, f32[512,1152]{1,0:T(8,128)S(1)}) custom-call(f32[1]{0:T(128)S(6)} %copy.7.scale_ref, f32[1]{0:T(128)S(6)} %copy.8.shift_ref, s32[2,8]{1,0:T(2,128)S(1)} %copy-done.2, bf16[512,1152]{1,0:T(8,128)(2,1)S(1)} %multiply_convert_fusion.1.image_ref.own_ref, ...), custom_call_target="tpu_custom_call" | custom-call | flops 2415919104 | bytes 4718592 | tf_op jit(solution)/shard_map/add_near/pallas_call | solution.py:28
  43.3 0.7 %collective-permute-start.10 = (bf16[128,1152]{1,0:T(8,128)(2,1)S(1)}, bf16[128,1152]{1,0:T(8,128)(2,1)S(1)}, u32[]{:S(2)}, u32[]{:S(2)}) collective-permute-start(bf16[128,1152]{1,0:T(8,128)(2,1)S(1)} %slice.9), channel_id=1, source_target_pairs={{0,3},{1,0},{2,1},{3,2},{4,7},{5,4},{6,5},{7,6},{8,11},{9,8},{10,9... | collective-permute-start | bytes 884744 | tf_op jit(solution)/shard_map/ppermute | solution.py:297
  44.0 6.7 %finish.2 = f32[512,1152]{1,0:T(8,128)} custom-call(f32[1]{0:T(128)S(6)} %copy.7.scale_ref, f32[1]{0:T(128)S(6)} %copy.8.shift_ref, s32[2,8]{1,0:T(2,128)S(1)} %copy-done.2, bf16[512,1152]{1,0:T(8,128)(2,1)S(1)} %multiply_convert_fusion.1.image_ref.own_ref, f32[512,1152]{1,0:T(8,128)S(1)} %copy-done.1, f32[512,1152]{1,0:T(8,128)S(1)} %get-tuple-element.22.sum_ref, ...), custom_call_target="tpu_custom_call" | custom-call | flops 3623878656 | bytes 4718592 | tf_op jit(solution)/shard_map/finish/pallas_call | solution.py:28
  50.7 0.6 collective-permute-start.8
  51.3 5.6 %collective-permute-done.7.refs_2_ = bf16[384,1152]{1,0:T(8,128)(2,1)S(1)} collective-permute-done((bf16[384,1152]{1,0:T(8,128)(2,1)S(1)}, bf16[384,1152]{1,0:T(8,128)(2,1)S(1)}, u32[]{:S(2)}, u32[]{:S(2)}) %collective-permute-start.7) | collective-permute-done | bytes 884768 | tf_op jit(solution)/shard_map/ppermute | solution.py:297
  56.9 1.5 %collective-permute-start.9 = (bf16[128,1152]{1,0:T(8,128)(2,1)S(1)}, bf16[128,1152]{1,0:T(8,128)(2,1)S(1)}, u32[]{:S(2)}, u32[]{:S(2)}) collective-permute-start(bf16[128,1152]{1,0:T(8,128)(2,1)S(1)} %slice.9), channel_id=1, source_target_pairs={{0,16},{4,20},{8,24},{12,28},{16,0},{20,4},{24,8},{28,12},{1,17},{... | collective-permute-start | bytes 884744 | tf_op jit(solution)/shard_map/ppermute | solution.py:302
  58.4 0.2 collective-permute-done.5.refs_0_
  58.6 0.2 collective-permute-done.6.refs_1_
  58.8 4.6 %add_up.1.sum_ref = f32[512,1152]{1,0:T(8,128)S(1)} custom-call(f32[1]{0:T(128)S(6)} %copy.7.scale_ref, f32[1]{0:T(128)S(6)} %copy.8.shift_ref, s32[2,8]{1,0:T(2,128)S(1)} %copy-done.2, bf16[512,1152]{1,0:T(8,128)(2,1)S(1)} %multiply_convert_fusion.text_ref.own_ref, f32[512,1152]{1,0:T(8,128)S(1)} %get-tuple-element.25.sum_ref, ...), custom_call_target="tpu_custom_call" | custom-call | flops 2717908992 | bytes 4718592 | tf_op jit(solution)/shard_map/add_up/pallas_call | solution.py:28
  63.4 0.4 collective-permute-done.9.refs_1_
  63.8 3.9 %finish.3 = f32[512,1152]{1,0:T(8,128)} custom-call(f32[1]{0:T(128)S(6)} %copy.7.scale_ref, f32[1]{0:T(128)S(6)} %copy.8.shift_ref, s32[2,8]{1,0:T(2,128)S(1)} %copy-done.2, bf16[512,1152]{1,0:T(8,128)(2,1)S(1)} %multiply_convert_fusion.text_ref.own_ref, f32[512,1152]{1,0:T(8,128)S(1)} %copy-done, f32[512,1152]{1,0:T(8,128)S(1)} %add_up.1.sum_ref, ...), custom_call_target="tpu_custom_call" | custom-call | flops 905969664 | bytes 4718592 | tf_op jit(solution)/shard_map/finish/pallas_call | solution.py:28
  (17 shorter events, 0.3 us)
Async XLA Ops:
  0.6 2.4 %copy-start = (f32[512,1152]{1,0:T(8,128)S(1)}, f32[512,1152]{1,0:T(8,128)}, u32[]{:S(2)}) copy-start(f32[512,1152]{1,0:T(8,128)} %raw_ref.3) | copy-start | bytes 7077892
  2.7 3.6 %copy-start.1 = (f32[512,1152]{1,0:T(8,128)S(1)}, f32[512,1152]{1,0:T(8,128)}, u32[]{:S(2)}) copy-start(f32[512,1152]{1,0:T(8,128)} %raw_ref.2) | copy-start | bytes 7077892
  3.2 31.1 %collective-permute-start = (bf16[512,1152]{1,0:T(8,128)(2,1)S(1)}, bf16[512,1152]{1,0:T(8,128)(2,1)S(1)}, u32[]{:S(2)}, u32[]{:S(2)}) collective-permute-start(bf16[512,1152]{1,0:T(8,128)(2,1)S(1)} %multiply_convert_fusion.text_ref.own_ref), channel_id=1, source_target_pairs={{0,1},{1,2},{2,3},{3,0},{4,5},{5,6},{6,7},{7,4},{8,9},{9,10},{10,1... | collective-permute-start | bytes 3538952 | tf_op jit(solution)/shard_map/ppermute | solution.py:297
  6.3 29.7 %collective-permute-start.1 = (bf16[512,1152]{1,0:T(8,128)(2,1)S(1)}, bf16[512,1152]{1,0:T(8,128)(2,1)S(1)}, u32[]{:S(2)}, u32[]{:S(2)}) collective-permute-start(bf16[512,1152]{1,0:T(8,128)(2,1)S(1)} %multiply_convert_fusion.text_ref.own_ref), channel_id=1, source_target_pairs={{0,4},{4,0},{8,12},{12,8},{16,20},{20,16},{24,28},{28,24},{1,5},{5... | collective-permute-start | bytes 3538952 | tf_op jit(solution)/shard_map/ppermute | solution.py:302
  6.7 30.8 %collective-permute-start.2 = (bf16[512,1152]{1,0:T(8,128)(2,1)S(1)}, bf16[512,1152]{1,0:T(8,128)(2,1)S(1)}, u32[]{:S(2)}, u32[]{:S(2)}) collective-permute-start(bf16[512,1152]{1,0:T(8,128)(2,1)S(1)} %multiply_convert_fusion.1.image_ref.own_ref), channel_id=1, source_target_pairs={{0,4},{4,0},{8,12},{12,8},{16,20},{20,16},{24,28},{28,24},{1,5},{5... | collective-permute-start | bytes 3538952 | tf_op jit(solution)/shard_map/ppermute | solution.py:302
  7.3 36.0 %collective-permute-start.3 = (bf16[512,1152]{1,0:T(8,128)(2,1)S(1)}, bf16[512,1152]{1,0:T(8,128)(2,1)S(1)}, u32[]{:S(2)}, u32[]{:S(2)}) collective-permute-start(bf16[512,1152]{1,0:T(8,128)(2,1)S(1)} %multiply_convert_fusion.text_ref.own_ref), channel_id=1, source_target_pairs={{0,8},{4,12},{8,0},{12,4},{16,24},{20,28},{24,16},{28,20},{1,9},{5... | collective-permute-start | bytes 3538952 | tf_op jit(solution)/shard_map/ppermute | solution.py:302
  8.8 35.2 %collective-permute-start.4 = (bf16[512,1152]{1,0:T(8,128)(2,1)S(1)}, bf16[512,1152]{1,0:T(8,128)(2,1)S(1)}, u32[]{:S(2)}, u32[]{:S(2)}) collective-permute-start(bf16[512,1152]{1,0:T(8,128)(2,1)S(1)} %multiply_convert_fusion.text_ref.own_ref), channel_id=1, source_target_pairs={{0,16},{4,20},{8,24},{12,28},{16,0},{20,4},{24,8},{28,12},{1,17},{... | collective-permute-start | bytes 3538952 | tf_op jit(solution)/shard_map/ppermute | solution.py:302
  11.7 27.3 %copy-start.2 = (s32[2,8]{1,0:T(2,128)S(1)}, s32[2,8]{1,0:T(2,128)}, u32[]{:S(2)}) copy-start(s32[2,8]{1,0:T(2,128)} %grid_ref.7) | copy-start | bytes 196
  34.3 22.6 %collective-permute-start.7 = (bf16[384,1152]{1,0:T(8,128)(2,1)S(1)}, bf16[384,1152]{1,0:T(8,128)(2,1)S(1)}, u32[]{:S(2)}, u32[]{:S(2)}) collective-permute-start(bf16[384,1152]{1,0:T(8,128)(2,1)S(1)} %slice.8), channel_id=1, source_target_pairs={{0,3},{1,0},{2,1},{3,2},{4,7},{5,4},{6,5},{7,6},{8,11},{9,8},{10,9... | collective-permute-start | bytes 2654216 | tf_op jit(solution)/shard_map/ppermute | solution.py:297
  36.0 22.6 %collective-permute-start.5 = (bf16[384,1152]{1,0:T(8,128)(2,1)S(1)}, bf16[384,1152]{1,0:T(8,128)(2,1)S(1)}, u32[]{:S(2)}, u32[]{:S(2)}) collective-permute-start(bf16[384,1152]{1,0:T(8,128)(2,1)S(1)} %slice.8), channel_id=1, source_target_pairs={{0,8},{4,12},{8,0},{12,4},{16,24},{20,28},{24,16},{28,20},{1,9},{5... | collective-permute-start | bytes 2654216 | tf_op jit(solution)/shard_map/ppermute | solution.py:302
  37.5 21.3 %collective-permute-start.6 = (bf16[384,1152]{1,0:T(8,128)(2,1)S(1)}, bf16[384,1152]{1,0:T(8,128)(2,1)S(1)}, u32[]{:S(2)}, u32[]{:S(2)}) collective-permute-start(bf16[384,1152]{1,0:T(8,128)(2,1)S(1)} %slice.8), channel_id=1, source_target_pairs={{0,16},{4,20},{8,24},{12,28},{16,0},{20,4},{24,8},{28,12},{1,17},{... | collective-permute-start | bytes 2654216 | tf_op jit(solution)/shard_map/ppermute | solution.py:302
  43.3 20.1 %collective-permute-start.10 = (bf16[128,1152]{1,0:T(8,128)(2,1)S(1)}, bf16[128,1152]{1,0:T(8,128)(2,1)S(1)}, u32[]{:S(2)}, u32[]{:S(2)}) collective-permute-start(bf16[128,1152]{1,0:T(8,128)(2,1)S(1)} %slice.9), channel_id=1, source_target_pairs={{0,3},{1,0},{2,1},{3,2},{4,7},{5,4},{6,5},{7,6},{8,11},{9,8},{10,9... | collective-permute-start | bytes 884744 | tf_op jit(solution)/shard_map/ppermute | solution.py:297
  50.7 12.7 %collective-permute-start.8 = (bf16[128,1152]{1,0:T(8,128)(2,1)S(1)}, bf16[128,1152]{1,0:T(8,128)(2,1)S(1)}, u32[]{:S(2)}, u32[]{:S(2)}) collective-permute-start(bf16[128,1152]{1,0:T(8,128)(2,1)S(1)} %slice.9), channel_id=1, source_target_pairs={{0,8},{4,12},{8,0},{12,4},{16,24},{20,28},{24,16},{28,20},{1,9},{5... | collective-permute-start | bytes 884744 | tf_op jit(solution)/shard_map/ppermute | solution.py:302
  56.9 6.9 %collective-permute-start.9 = (bf16[128,1152]{1,0:T(8,128)(2,1)S(1)}, bf16[128,1152]{1,0:T(8,128)(2,1)S(1)}, u32[]{:S(2)}, u32[]{:S(2)}) collective-permute-start(bf16[128,1152]{1,0:T(8,128)(2,1)S(1)} %slice.9), channel_id=1, source_target_pairs={{0,16},{4,20},{8,24},{12,28},{16,0},{20,4},{24,8},{28,12},{1,17},{... | collective-permute-start | bytes 884744 | tf_op jit(solution)/shard_map/ppermute | solution.py:302

commit v7 on v6

--- a/solution.py
+++ b/solution.py
@@ -45,6 +45,50 @@
 def normalized(raw):
     total = jnp.sum(raw * raw, axis=-1, keepdims=True)
     return (raw * lax.rsqrt(total + epsilon)).astype(jnp.bfloat16)
+
+
+def halves_kernel(raw_ref, half_ref, held_ref, ready_ref, in_sems, out_sems):
+    chunks = [pl.ds(first, last - first) for first, last in strips(raw_ref.shape[0], SLICE)]
+    reads = [
+        pltpu.make_async_copy(raw_ref.at[rows, :], held_ref.at[rows, :], in_sems.at[number])
+        for number, rows in enumerate(chunks)
+    ]
+    writes = [
+        pltpu.make_async_copy(ready_ref.at[rows, :], half_ref.at[rows, :], out_sems.at[number])
+        for number, rows in enumerate(chunks)
+    ]
+    for read in reads:
+        read.start()
+    for read, write, rows in zip(reads, writes, chunks):
+        read.wait()
+        for first, last in strips(rows.size, SLICE // 2):
+            part = pl.ds(rows.start + first, last - first)
+            raw = held_ref[part, :]
+            total = jnp.sum(raw * raw, axis=-1, keepdims=True)
+            ready_ref[part, :] = (raw * lax.rsqrt(total + epsilon)).astype(jnp.bfloat16)
+        write.start()
+    for write in writes:
+        write.wait()
+
+
+def halves(raw):
+    rows, width = raw.shape
+    count = len(strips(rows, SLICE))
+    return pl.pallas_call(
+        halves_kernel,
+        in_specs=[pl.BlockSpec(memory_space=pl.ANY)],
+        out_specs=pl.BlockSpec(memory_space=pl.ANY),
+        out_shape=jax.ShapeDtypeStruct((rows, width), jnp.bfloat16),
+        scratch_shapes=[
+            pltpu.VMEM((rows, width), jnp.float32),
+            pltpu.VMEM((rows, width), jnp.bfloat16),
+            pltpu.SemaphoreType.DMA((count,)),
+            pltpu.SemaphoreType.DMA((count,)),
+        ],
+        name="halves",
+        compiler_params=pltpu.CompilerParams(vmem_limit_bytes=125 * MIB // 2),
+        cost_estimate=cost(rows, 1, width),
+    )(raw)
 
 
 def coupled(products, scale, factor, shift, places=None):
@@ -305,7 +349,7 @@
 def with_partners(bits, visual, caption, grid, scale, shift):
     cut = visual.shape[0] * 3 // 4
     near, far = [bit for bit in bits if bit == 0], [bit for bit in bits if bit != 0]
-    text_half = normalized(caption)
+    text_half = halves(caption)
     text_z = passed_along(text_half, "group", 1)
     far_texts = [exchanged(text_half, bit) for bit in far]
     image_half = normalized(visual)
@@ -317,6 +361,9 @@
     )
     image_z_first = passed_along(image_first, "group", -1)
     image_z_last = passed_along(image_last, "group", -1)
+    image_first, image_last, far_texts = lax.optimization_barrier(
+        (image_first, image_last, far_texts)
+    )
     far_images_first = [exchanged(image_first, bit) for bit in far]
     for (texts, images), bit in zip(boths, near):
         image_sum, text_sum = add_near(

time: 68 us -> 68.2 us (level)
  Pallas kernels: 22.1 us -> 24.4 us
  waiting for transfers between devices: 26.2 us -> 24 us
  starting transfers between devices: 14.2 us -> 15.1 us
    pallas_call x0 -> x1, Pallas kernels: none -> 2.68 us  [halves(): pl.pallas_call(halves_kernel, in_specs=[pl.BlockSpec(memory_space=pl.ANY)...]
    ppermute x3, waiting for transfers between devices: 25.4 us -> 23.1 us  [passed_along(): return lax.ppermute(x, axis, [(i, (i + by) % count) for i in range(count)])]
    reduce_sum x2 -> x1, other arithmetic: 2.27 us -> 1.89 us  [normalized(): total = jnp.sum(raw * raw, axis=-1, keepdims=True)]
  transfers between devices with their start and end apart: 11 -> 11, of which waited for: 5 -> 5; matrix products, arithmetic and copies ran while one was open for 1% -> 3% of each run, Pallas kernels for 27% -> 26%
where the time goes in v7:
time: 68.2 us; the launch traced here: 68 us
  Pallas kernels  24.4 us (36%)
  waiting for transfers between devices  24 us (35%)
  starting transfers between devices  15.1 us (22%)
  between operations  2.22 us (3%)
  other arithmetic  2.1 us (3%)
    ppermute x3, waiting for transfers between devices, passed_along(): return lax.ppermute(x, axis, [(i, (i + by) % count) for i in range(count)])  23.1 us
    pallas_call x5, Pallas kernels, call(): pl.pallas_call(body, grid=grid or (), in_specs=[SMEM] * smem + [VMEM] * (...  21.8 us
    ppermute x8, starting transfers between devices, exchanged(): return lax.ppermute(x, 'blk', [(i, i ^ 1 << bit) for i in range(count)])  9.17 us
    ppermute x3, starting transfers between devices, passed_along(): return lax.ppermute(x, axis, [(i, (i + by) % count) for i in range(count)])  5.96 us
    pallas_call x1, Pallas kernels, halves(): pl.pallas_call(halves_kernel, in_specs=[pl.BlockSpec(memory_space=pl.ANY)...  2.68 us
    reduce_sum x1, other arithmetic, normalized(): total = jnp.sum(raw * raw, axis=-1, keepdims=True)  1.89 us
  transfers between devices with their start and end apart: 11, of which 5 were waited for; matrix products, arithmetic and copies ran while one was open for 3% of the time, Pallas kernels for 26%

profile of v7, /device:TPU:0, one launch (start us, length us, event | category | flops | bytes accessed | tf_op | source)
XLA Modules:
  0.0 68.0 jit_solution(12123818372658550725)
XLA Ops:
  0.6 2.7 %halves.1.text_ref.own_ref = bf16[512,1152]{1,0:T(8,128)(2,1)} custom-call(f32[512,1152]{1,0:T(8,128)} %raw_ref.5), custom_call_target="tpu_custom_call" | custom-call | flops 2359296 | bytes 4718592 | tf_op jit(solution)/shard_map/halves/pallas_call | solution.py:77
  3.3 3.1 %collective-permute-start = (bf16[512,1152]{1,0:T(8,128)(2,1)}, bf16[512,1152]{1,0:T(8,128)(2,1)S(1)}, u32[]{:S(2)}, u32[]{:S(2)}) collective-permute-start(bf16[512,1152]{1,0:T(8,128)(2,1)} %halves.1.text_ref.own_ref), channel_id=1, source_target_pairs={{0,1},{1,2},{2,3},{3,0},{4,5},{5,6},{6,7},{7,4},{8,9},{9,10},{10,1... | collective-permute-start | bytes 3538952 | tf_op jit(solution)/shard_map/ppermute | solution.py:341
  6.4 1.5 %collective-permute-start.3 = (bf16[512,1152]{1,0:T(8,128)(2,1)}, bf16[512,1152]{1,0:T(8,128)(2,1)S(1)}, u32[]{:S(2)}, u32[]{:S(2)}) collective-permute-start(bf16[512,1152]{1,0:T(8,128)(2,1)} %halves.1.text_ref.own_ref), channel_id=1, source_target_pairs={{0,8},{4,12},{8,0},{12,4},{16,24},{20,28},{24,16},{28,20},{1,9},{5... | collective-permute-start | bytes 3538952 | tf_op jit(solution)/shard_map/ppermute | solution.py:346
  7.9 1.5 %collective-permute-start.4 = (bf16[512,1152]{1,0:T(8,128)(2,1)}, bf16[512,1152]{1,0:T(8,128)(2,1)S(1)}, u32[]{:S(2)}, u32[]{:S(2)}) collective-permute-start(bf16[512,1152]{1,0:T(8,128)(2,1)} %halves.1.text_ref.own_ref), channel_id=1, source_target_pairs={{0,16},{4,20},{8,24},{12,28},{16,0},{20,4},{24,8},{28,12},{1,17},{... | collective-permute-start | bytes 3538952 | tf_op jit(solution)/shard_map/ppermute | solution.py:346
  9.4 1.9 %multiply_reduce_fusion = f32[512]{0:T(512)S(1)} fusion(f32[512,1152]{1,0:T(8,128)} %raw_ref.4), kind=kLoop, calls=%fused_computation.1 | loop fusion | flops 1179136 | bytes 2361344 | tf_op jit(solution)/shard_map/reduce_sum | solution.py:46
  11.3 0.2 multiply_convert_fusion.image_ref.own_ref
  11.5 0.1 collective-permute-start.2
  11.6 0.1 slice.8
  13.1 2.7 %diagonal.1 = (f32[512,1152]{1,0:T(8,128)S(1)}, f32[512,1152]{1,0:T(8,128)S(1)}) custom-call(f32[1]{0:T(128)S(6)} %copy.7.scale_ref, f32[1]{0:T(128)S(6)} %copy.8.shift_ref, bf16[512,1152]{1,0:T(8,128)(2,1)S(1)} %multiply_convert_fusion.image_ref.own_ref, bf16[512,1152]{1,0:T(8,128)(2,1)S(1)} %copy-done), custom_call_target="tpu_custom_call" | custom-call | flops 2415919104 | bytes 4718592 | tf_op jit(solution)/shard_map/diagonal/pallas_call | solution.py:28
  15.8 18.8 %collective-permute-done.refs_2_ = bf16[512,1152]{1,0:T(8,128)(2,1)S(1)} collective-permute-done((bf16[512,1152]{1,0:T(8,128)(2,1)}, bf16[512,1152]{1,0:T(8,128)(2,1)S(1)}, u32[]{:S(2)}, u32[]{:S(2)}) %collective-permute-start) | collective-permute-done | bytes 1179680 | tf_op jit(solution)/shard_map/ppermute | solution.py:341
  34.6 1.7 %collective-permute-start.7 = (bf16[384,1152]{1,0:T(8,128)(2,1)S(1)}, bf16[384,1152]{1,0:T(8,128)(2,1)S(1)}, u32[]{:S(2)}, u32[]{:S(2)}) collective-permute-start(bf16[384,1152]{1,0:T(8,128)(2,1)S(1)} %slice.8), channel_id=1, source_target_pairs={{0,3},{1,0},{2,1},{3,2},{4,7},{5,4},{6,5},{7,6},{8,11},{9,8},{10,9... | collective-permute-start | bytes 2654216 | tf_op jit(solution)/shard_map/ppermute | solution.py:341
  36.4 1.5 %collective-permute-start.5 = (bf16[384,1152]{1,0:T(8,128)(2,1)S(1)}, bf16[384,1152]{1,0:T(8,128)(2,1)S(1)}, u32[]{:S(2)}, u32[]{:S(2)}) collective-permute-start(bf16[384,1152]{1,0:T(8,128)(2,1)S(1)} %slice.8), channel_id=1, source_target_pairs={{0,8},{4,12},{8,0},{12,4},{16,24},{20,28},{24,16},{28,20},{1,9},{5... | collective-permute-start | bytes 2654216 | tf_op jit(solution)/shard_map/ppermute | solution.py:346
  37.9 1.5 %collective-permute-start.6 = (bf16[384,1152]{1,0:T(8,128)(2,1)S(1)}, bf16[384,1152]{1,0:T(8,128)(2,1)S(1)}, u32[]{:S(2)}, u32[]{:S(2)}) collective-permute-start(bf16[384,1152]{1,0:T(8,128)(2,1)S(1)} %slice.8), channel_id=1, source_target_pairs={{0,16},{4,20},{8,24},{12,28},{16,0},{20,4},{24,8},{28,12},{1,17},{... | collective-permute-start | bytes 2654216 | tf_op jit(solution)/shard_map/ppermute | solution.py:346
  39.4 1.1 %collective-permute-start.10 = (bf16[128,1152]{1,0:T(8,128)(2,1)S(1)}, bf16[128,1152]{1,0:T(8,128)(2,1)S(1)}, u32[]{:S(2)}, u32[]{:S(2)}) collective-permute-start(bf16[128,1152]{1,0:T(8,128)(2,1)S(1)} %slice.9), channel_id=1, source_target_pairs={{0,3},{1,0},{2,1},{3,2},{4,7},{5,4},{6,5},{7,6},{8,11},{9,8},{10,9... | collective-permute-start | bytes 884744 | tf_op jit(solution)/shard_map/ppermute | solution.py:341
  40.5 4.2 %add_near.1 = (f32[512,1152]{1,0:T(8,128)S(1)}, f32[512,1152]{1,0:T(8,128)S(1)}) custom-call(f32[1]{0:T(128)S(6)} %copy.7.scale_ref, f32[1]{0:T(128)S(6)} %copy.8.shift_ref, s32[2,8]{1,0:T(2,128)S(1)} %copy-done.3, bf16[512,1152]{1,0:T(8,128)(2,1)S(1)} %multiply_convert_fusion.image_ref.own_ref, bf16[512,1152]{1,0:T(8,128)(2,1)S(1)} %copy-done, ...), custom_call_target="tpu_custom_call" | custom-call | flops 2415919104 | bytes 4718592 | tf_op jit(solution)/shard_map/add_near/pallas_call | solution.py:28
  44.7 6.6 %finish.2 = f32[512,1152]{1,0:T(8,128)} custom-call(f32[1]{0:T(128)S(6)} %copy.7.scale_ref, f32[1]{0:T(128)S(6)} %copy.8.shift_ref, s32[2,8]{1,0:T(2,128)S(1)} %copy-done.3, bf16[512,1152]{1,0:T(8,128)(2,1)S(1)} %multiply_convert_fusion.image_ref.own_ref, f32[512,1152]{1,0:T(8,128)S(1)} %copy-done.2, f32[512,1152]{1,0:T(8,128)S(1)} %get-tuple-element.28.sum_ref, ...), custom_call_target="tpu_custom_call" | custom-call | flops 3623878656 | bytes 4718592 | tf_op jit(solution)/shard_map/finish/pallas_call | solution.py:28
  51.3 1.6 %collective-permute-start.8 = (bf16[128,1152]{1,0:T(8,128)(2,1)S(1)}, bf16[128,1152]{1,0:T(8,128)(2,1)S(1)}, u32[]{:S(2)}, u32[]{:S(2)}) collective-permute-start(bf16[128,1152]{1,0:T(8,128)(2,1)S(1)} %slice.9), channel_id=1, source_target_pairs={{0,8},{4,12},{8,0},{12,4},{16,24},{20,28},{24,16},{28,20},{1,9},{5... | collective-permute-start | bytes 884744 | tf_op jit(solution)/shard_map/ppermute | solution.py:346
  52.9 4.3 %collective-permute-done.7.refs_2_ = bf16[384,1152]{1,0:T(8,128)(2,1)S(1)} collective-permute-done((bf16[384,1152]{1,0:T(8,128)(2,1)S(1)}, bf16[384,1152]{1,0:T(8,128)(2,1)S(1)}, u32[]{:S(2)}, u32[]{:S(2)}) %collective-permute-start.7) | collective-permute-done | bytes 884768 | tf_op jit(solution)/shard_map/ppermute | solution.py:341
  57.2 1.5 %collective-permute-start.9 = (bf16[128,1152]{1,0:T(8,128)(2,1)S(1)}, bf16[128,1152]{1,0:T(8,128)(2,1)S(1)}, u32[]{:S(2)}, u32[]{:S(2)}) collective-permute-start(bf16[128,1152]{1,0:T(8,128)(2,1)S(1)} %slice.9), channel_id=1, source_target_pairs={{0,16},{4,20},{8,24},{12,28},{16,0},{20,4},{24,8},{28,12},{1,17},{... | collective-permute-start | bytes 884744 | tf_op jit(solution)/shard_map/ppermute | solution.py:346
  58.7 0.2 collective-permute-done.5.refs_0_
  58.9 0.2 collective-permute-done.6.refs_1_
  59.1 4.5 %add_up.1.sum_ref = f32[512,1152]{1,0:T(8,128)S(1)} custom-call(f32[1]{0:T(128)S(6)} %copy.7.scale_ref, f32[1]{0:T(128)S(6)} %copy.8.shift_ref, s32[2,8]{1,0:T(2,128)S(1)} %copy-done.3, bf16[512,1152]{1,0:T(8,128)(2,1)S(1)} %copy-done, f32[512,1152]{1,0:T(8,128)S(1)} %get-tuple-element.33.sum_ref, bf16[384,1152]{1,0:T(8,128)(2,1)S(1)} %collective-permute-done.5.refs_0_, ...), custom_call_target="tpu_custom_call" | custom-call | flops 2717908992 | bytes 4718592 | tf_op jit(solution)/shard_map/add_up/pallas_call | solution.py:28
  63.7 0.5 collective-permute-done.9.refs_1_
  64.1 3.8 %finish.3 = f32[512,1152]{1,0:T(8,128)} custom-call(f32[1]{0:T(128)S(6)} %copy.7.scale_ref, f32[1]{0:T(128)S(6)} %copy.8.shift_ref, s32[2,8]{1,0:T(2,128)S(1)} %copy-done.3, bf16[512,1152]{1,0:T(8,128)(2,1)S(1)} %copy-done, f32[512,1152]{1,0:T(8,128)S(1)} %copy-done.1, f32[512,1152]{1,0:T(8,128)S(1)} %add_up.1.sum_ref, ...), custom_call_target="tpu_custom_call" | custom-call | flops 905969664 | bytes 4718592 | tf_op jit(solution)/shard_map/finish/pallas_call | solution.py:28
  (17 shorter events, 0.1 us)
Async XLA Ops:
  3.3 8.0 %copy-start.2 = (f32[512,1152]{1,0:T(8,128)S(1)}, f32[512,1152]{1,0:T(8,128)}, u32[]{:S(2)}) copy-start(f32[512,1152]{1,0:T(8,128)} %raw_ref.4) | copy-start | bytes 7077892
  3.3 31.3 %collective-permute-start = (bf16[512,1152]{1,0:T(8,128)(2,1)}, bf16[512,1152]{1,0:T(8,128)(2,1)S(1)}, u32[]{:S(2)}, u32[]{:S(2)}) collective-permute-start(bf16[512,1152]{1,0:T(8,128)(2,1)} %halves.1.text_ref.own_ref), channel_id=1, source_target_pairs={{0,1},{1,2},{2,3},{3,0},{4,5},{5,6},{6,7},{7,4},{8,9},{9,10},{10,1... | collective-permute-start | bytes 3538952 | tf_op jit(solution)/shard_map/ppermute | solution.py:341
  6.4 33.0 %collective-permute-start.1 = (bf16[512,1152]{1,0:T(8,128)(2,1)}, bf16[512,1152]{1,0:T(8,128)(2,1)S(1)}, u32[]{:S(2)}, u32[]{:S(2)}) collective-permute-start(bf16[512,1152]{1,0:T(8,128)(2,1)} %halves.1.text_ref.own_ref), channel_id=1, source_target_pairs={{0,4},{4,0},{8,12},{12,8},{16,20},{20,16},{24,28},{28,24},{1,5},{5... | collective-permute-start | bytes 3538952 | tf_op jit(solution)/shard_map/ppermute | solution.py:346
  6.4 29.9 %collective-permute-start.3 = (bf16[512,1152]{1,0:T(8,128)(2,1)}, bf16[512,1152]{1,0:T(8,128)(2,1)S(1)}, u32[]{:S(2)}, u32[]{:S(2)}) collective-permute-start(bf16[512,1152]{1,0:T(8,128)(2,1)} %halves.1.text_ref.own_ref), channel_id=1, source_target_pairs={{0,8},{4,12},{8,0},{12,4},{16,24},{20,28},{24,16},{28,20},{1,9},{5... | collective-permute-start | bytes 3538952 | tf_op jit(solution)/shard_map/ppermute | solution.py:346
  7.9 28.5 %collective-permute-start.4 = (bf16[512,1152]{1,0:T(8,128)(2,1)}, bf16[512,1152]{1,0:T(8,128)(2,1)S(1)}, u32[]{:S(2)}, u32[]{:S(2)}) collective-permute-start(bf16[512,1152]{1,0:T(8,128)(2,1)} %halves.1.text_ref.own_ref), channel_id=1, source_target_pairs={{0,16},{4,20},{8,24},{12,28},{16,0},{20,4},{24,8},{28,12},{1,17},{... | collective-permute-start | bytes 3538952 | tf_op jit(solution)/shard_map/ppermute | solution.py:346
  11.3 1.7 %copy-start = (bf16[512,1152]{1,0:T(8,128)(2,1)S(1)}, bf16[512,1152]{1,0:T(8,128)(2,1)}, u32[]{:S(2)}) copy-start(bf16[512,1152]{1,0:T(8,128)(2,1)} %halves.1.text_ref.own_ref) | copy-start | bytes 3538948
  11.5 29.0 %collective-permute-start.2 = (bf16[512,1152]{1,0:T(8,128)(2,1)S(1)}, bf16[512,1152]{1,0:T(8,128)(2,1)S(1)}, u32[]{:S(2)}, u32[]{:S(2)}) collective-permute-start(bf16[512,1152]{1,0:T(8,128)(2,1)S(1)} %multiply_convert_fusion.image_ref.own_ref), channel_id=1, source_target_pairs={{0,4},{4,0},{8,12},{12,8},{16,20},{20,16},{24,28},{28,24},{1,5},{5... | collective-permute-start | bytes 3538952 | tf_op jit(solution)/shard_map/ppermute | solution.py:346
  13.0 27.5 %copy-start.3 = (s32[2,8]{1,0:T(2,128)S(1)}, s32[2,8]{1,0:T(2,128)}, u32[]{:S(2)}) copy-start(s32[2,8]{1,0:T(2,128)} %grid_ref.7) | copy-start | bytes 196
  34.6 22.6 %collective-permute-start.7 = (bf16[384,1152]{1,0:T(8,128)(2,1)S(1)}, bf16[384,1152]{1,0:T(8,128)(2,1)S(1)}, u32[]{:S(2)}, u32[]{:S(2)}) collective-permute-start(bf16[384,1152]{1,0:T(8,128)(2,1)S(1)} %slice.8), channel_id=1, source_target_pairs={{0,3},{1,0},{2,1},{3,2},{4,7},{5,4},{6,5},{7,6},{8,11},{9,8},{10,9... | collective-permute-start | bytes 2654216 | tf_op jit(solution)/shard_map/ppermute | solution.py:341
  36.4 22.6 %collective-permute-start.5 = (bf16[384,1152]{1,0:T(8,128)(2,1)S(1)}, bf16[384,1152]{1,0:T(8,128)(2,1)S(1)}, u32[]{:S(2)}, u32[]{:S(2)}) collective-permute-start(bf16[384,1152]{1,0:T(8,128)(2,1)S(1)} %slice.8), channel_id=1, source_target_pairs={{0,8},{4,12},{8,0},{12,4},{16,24},{20,28},{24,16},{28,20},{1,9},{5... | collective-permute-start | bytes 2654216 | tf_op jit(solution)/shard_map/ppermute | solution.py:346
  37.9 21.3 %collective-permute-start.6 = (bf16[384,1152]{1,0:T(8,128)(2,1)S(1)}, bf16[384,1152]{1,0:T(8,128)(2,1)S(1)}, u32[]{:S(2)}, u32[]{:S(2)}) collective-permute-start(bf16[384,1152]{1,0:T(8,128)(2,1)S(1)} %slice.8), channel_id=1, source_target_pairs={{0,16},{4,20},{8,24},{12,28},{16,0},{20,4},{24,8},{28,12},{1,17},{... | collective-permute-start | bytes 2654216 | tf_op jit(solution)/shard_map/ppermute | solution.py:346
  39.4 24.3 %collective-permute-start.10 = (bf16[128,1152]{1,0:T(8,128)(2,1)S(1)}, bf16[128,1152]{1,0:T(8,128)(2,1)S(1)}, u32[]{:S(2)}, u32[]{:S(2)}) collective-permute-start(bf16[128,1152]{1,0:T(8,128)(2,1)S(1)} %slice.9), channel_id=1, source_target_pairs={{0,3},{1,0},{2,1},{3,2},{4,7},{5,4},{6,5},{7,6},{8,11},{9,8},{10,9... | collective-permute-start | bytes 884744 | tf_op jit(solution)/shard_map/ppermute | solution.py:341
  51.3 12.8 %copy-start.1 = (f32[512,1152]{1,0:T(8,128)S(1)}, f32[512,1152]{1,0:T(8,128)}, u32[]{:S(2)}) copy-start(f32[512,1152]{1,0:T(8,128)} %raw_ref.5) | copy-start | bytes 7077892
  51.3 12.3 %collective-permute-start.8 = (bf16[128,1152]{1,0:T(8,128)(2,1)S(1)}, bf16[128,1152]{1,0:T(8,128)(2,1)S(1)}, u32[]{:S(2)}, u32[]{:S(2)}) collective-permute-start(bf16[128,1152]{1,0:T(8,128)(2,1)S(1)} %slice.9), channel_id=1, source_target_pairs={{0,8},{4,12},{8,0},{12,4},{16,24},{20,28},{24,16},{28,20},{1,9},{5... | collective-permute-start | bytes 884744 | tf_op jit(solution)/shard_map/ppermute | solution.py:346
  57.2 6.9 %collective-permute-start.9 = (bf16[128,1152]{1,0:T(8,128)(2,1)S(1)}, bf16[128,1152]{1,0:T(8,128)(2,1)S(1)}, u32[]{:S(2)}, u32[]{:S(2)}) collective-permute-start(bf16[128,1152]{1,0:T(8,128)(2,1)S(1)} %slice.9), channel_id=1, source_target_pairs={{0,16},{4,20},{8,24},{12,28},{16,0},{20,4},{24,8},{28,12},{1,17},{... | collective-permute-start | bytes 884744 | tf_op jit(solution)/shard_map/ppermute | solution.py:346

commit v8 on v6

--- a/solution.py
+++ b/solution.py
@@ -70,14 +70,54 @@
 
 
 def side_by_side(others, all_ref):
-    if all_ref is None:
-        return others
+    if all(x.shape[0] % STRIP == 0 for x in others):
+        return list(others)
     left = 0
     for other_ref in others:
         count = other_ref.shape[0]
         all_ref[left : left + count, :] = other_ref[...]
         left += count
-    return [all_ref]
+    return [all_ref.at[:left, :]]
+
+
+def for_drawn(bits, scale_ref, grid_ref, other_refs, all_ref, run):
+    scale = scale_ref[0]
+    flagged = [(ref, bit) for ref, bit in zip(other_refs, bits) if bit is not None]
+    if len(flagged) != 2:
+        run(
+            side_by_side(other_refs, all_ref), [x.shape[0] for x in other_refs],
+            drawn_factors(bits, scale_ref, grid_ref),
+        )
+        return
+    (one_ref, one), (two_ref, two) = flagged
+    first, second = is_drawn(grid_ref, one), is_drawn(grid_ref, two)
+    fixed = [ref for ref, bit in zip(other_refs, bits) if bit is None]
+    count = one_ref.shape[0]
+
+    @pl.when(first & second)
+    def _():
+        others = side_by_side([*fixed, one_ref, two_ref], all_ref)
+        run(others, [sum(x.shape[0] for x in others)], [scale])
+
+    @pl.when(jnp.logical_not(first & second))
+    def _():
+        left, others = 0, list(fixed)
+        if any(x.shape[0] % STRIP for x in (*fixed, one_ref)):
+            others = []
+            for ref in fixed:
+                all_ref[left : left + ref.shape[0], :] = ref[...]
+                left += ref.shape[0]
+
+        @pl.when(first)
+        def _():
+            all_ref[left : left + count, :] = one_ref[...]
+
+        @pl.when(jnp.logical_not(first))
+        def _():
+            all_ref[left : left + count, :] = two_ref[...]
+
+        others.append(all_ref.at[: left + count, :])
+        run(others, [sum(x.shape[0] for x in others)], [scale])
 
 
 def factors_of(factors, counts, top, bottom):
@@ -153,10 +193,7 @@
 
 
 def all_scratch(others):
-    count, width = sum(x.shape[0] for x in others), others[0].shape[1]
-    if all(x.shape[0] % STRIP == 0 for x in others):
-        return []
-    return [pltpu.VMEM((count, width), jnp.bfloat16)]
+    return pltpu.VMEM((sum(x.shape[0] for x in others), others[0].shape[1]), jnp.bfloat16)
 
 
 def diagonal_kernel(scale_ref, shift_ref, image_ref, text_ref, image_sum_ref, text_sum_ref, weights_ref):
@@ -219,15 +256,16 @@
 
 
 def add_up_kernel(bits, scale_ref, shift_ref, grid_ref, own_ref, sum_ref, *refs):
-    other_refs, (out_ref, weights_ref, *all_refs) = refs[: len(bits)], refs[len(bits) :]
-    factors = drawn_factors(bits, scale_ref, grid_ref)
-    counts = [x.shape[0] for x in other_refs]
-    others = side_by_side(other_refs, *(all_refs or [None]))
-    for rows in blocks_of(own_ref.shape[0]):
-        add_pairs(
-            scale_ref[0], factors, shift_ref[0], own_ref, rows, counts, others, sum_ref, out_ref,
-            weights_ref,
-        )
+    other_refs, (out_ref, weights_ref, all_ref) = refs[: len(bits)], refs[len(bits) :]
+
+    def run(others, counts, factors):
+        for rows in blocks_of(own_ref.shape[0]):
+            add_pairs(
+                scale_ref[0], factors, shift_ref[0], own_ref, rows, counts, others, sum_ref, out_ref,
+                weights_ref,
+            )
+
+    for_drawn(bits, scale_ref, grid_ref, other_refs, all_ref, run)
 
 
 def add_up(scale, shift, grid, own, total, others, bits):
@@ -240,36 +278,37 @@
         [((rows, width), jnp.float32)],
         (rows, count, width),
         smem=3,
-        scratch=[pltpu.VMEM((rows, count), jnp.bfloat16), *all_scratch(others)],
+        scratch=[pltpu.VMEM((rows, count), jnp.bfloat16), all_scratch(others)],
     )[0]
 
 
 def finish_kernel(bits, scale_ref, shift_ref, grid_ref, own_ref, raw_ref, sum_ref, *refs):
-    other_refs, (out_ref, weights_ref, total_ref, sems, *all_refs) = refs[: len(bits)], refs[len(bits) :]
-    factors = drawn_factors(bits, scale_ref, grid_ref)
-    counts = [x.shape[0] for x in other_refs]
-    others = side_by_side(other_refs, *(all_refs or [None]))
-    copies = []
-    for first, block in blocks_of(own_ref.shape[0]):
-        sums = add_pairs(
-            scale_ref[0], factors, shift_ref[0], own_ref, (first, block), counts, others, sum_ref,
-            total_ref, weights_ref, raw_ref,
-        )
-        for (squares, products), (low, high) in zip(sums, strips(block, SLICE)):
-            inverse = lax.rsqrt(jnp.sum(squares, axis=-1, keepdims=True) + epsilon)
-            radial = jnp.sum(products, axis=-1, keepdims=True) * (inverse * inverse * inverse)
-            here = pl.ds(first + low, high - low)
-            for top, bottom in strips(own_ref.shape[1], COLUMNS):
-                total_ref[here, top:bottom] = (
-                    total_ref[here, top:bottom] * inverse - raw_ref[here, top:bottom] * radial
+    other_refs, (out_ref, weights_ref, total_ref, sems, all_ref) = refs[: len(bits)], refs[len(bits) :]
+
+    def run(others, counts, factors):
+        copies = []
+        for first, block in blocks_of(own_ref.shape[0]):
+            sums = add_pairs(
+                scale_ref[0], factors, shift_ref[0], own_ref, (first, block), counts, others, sum_ref,
+                total_ref, weights_ref, raw_ref,
+            )
+            for (squares, products), (low, high) in zip(sums, strips(block, SLICE)):
+                inverse = lax.rsqrt(jnp.sum(squares, axis=-1, keepdims=True) + epsilon)
+                radial = jnp.sum(products, axis=-1, keepdims=True) * (inverse * inverse * inverse)
+                here = pl.ds(first + low, high - low)
+                for top, bottom in strips(own_ref.shape[1], COLUMNS):
+                    total_ref[here, top:bottom] = (
+                        total_ref[here, top:bottom] * inverse - raw_ref[here, top:bottom] * radial
+                    )
+                copy = pltpu.make_async_copy(
+                    total_ref.at[here, :], out_ref.at[here, :], sems.at[len(copies)]
                 )
-            copy = pltpu.make_async_copy(
-                total_ref.at[here, :], out_ref.at[here, :], sems.at[len(copies)]
-            )
-            copy.start()
-            copies.append(copy)
-    for copy in copies:
-        copy.wait()
+                copy.start()
+                copies.append(copy)
+        for copy in copies:
+            copy.wait()
+
+    for_drawn(bits, scale_ref, grid_ref, other_refs, all_ref, run)
 
 
 def finish(scale, shift, grid, own, raw, total, others, bits):
@@ -287,7 +326,7 @@
             pltpu.VMEM((rows, count), jnp.bfloat16),
             pltpu.VMEM((rows, width), jnp.float32),
             pltpu.SemaphoreType.DMA((len(strips(rows, SLICE)),)),
-            *all_scratch(others),
+            all_scratch(others),
         ],
     )[0]
 

time: 68 us -> 67.9 us (level)
  no operation moved by 1% of the time
where the time goes in v8:
time: 67.9 us; the launch traced here: 67.8 us
  waiting for transfers between devices  26.2 us (39%)
  Pallas kernels  22.3 us (33%)
  starting transfers between devices  14.1 us (21%)
  other arithmetic  2.68 us (4%)
  between operations  2.22 us (3%)
    ppermute x3, waiting for transfers between devices, passed_along(): return lax.ppermute(x, axis, [(i, (i + by) % count) for i in range(count)])  25.4 us
    pallas_call x5, Pallas kernels, call(): pl.pallas_call(body, grid=grid or (), in_specs=[SMEM] * smem + [VMEM] * (...  22.3 us
    ppermute x8, starting transfers between devices, exchanged(): return lax.ppermute(x, 'blk', [(i, i ^ 1 << bit) for i in range(count)])  8.71 us
    ppermute x3, starting transfers between devices, passed_along(): return lax.ppermute(x, axis, [(i, (i + by) % count) for i in range(count)])  5.34 us
    reduce_sum x2, other arithmetic, normalized(): total = jnp.sum(raw * raw, axis=-1, keepdims=True)  2.27 us
  transfers between devices with their start and end apart: 11, of which 5 were waited for; matrix products, arithmetic and copies ran while one was open for 1% of the time, Pallas kernels for 27%

profile of v8, /device:TPU:0, one launch (start us, length us, event | category | flops | bytes accessed | tf_op | source)
XLA Modules:
  0.0 67.8 jit_solution(1169264746869765314)
XLA Ops:
  0.6 2.0 %multiply_reduce_fusion = f32[512]{0:T(512)S(1)} fusion(f32[512,1152]{1,0:T(8,128)} %raw_ref.3), kind=kLoop, calls=%fused_computation.1 | loop fusion | flops 1179136 | bytes 2361344 | tf_op jit(solution)/shard_map/reduce_sum | solution.py:46
  2.7 0.3 copy-done
  3.2 3.1 %collective-permute-start = (bf16[512,1152]{1,0:T(8,128)(2,1)S(1)}, bf16[512,1152]{1,0:T(8,128)(2,1)S(1)}, u32[]{:S(2)}, u32[]{:S(2)}) collective-permute-start(bf16[512,1152]{1,0:T(8,128)(2,1)S(1)} %multiply_convert_fusion.text_ref.own_ref), channel_id=1, source_target_pairs={{0,1},{1,2},{2,3},{3,0},{4,5},{5,6},{6,7},{7,4},{8,9},{9,10},{10,1... | collective-permute-start | bytes 3538952 | tf_op jit(solution)/shard_map/ppermute | solution.py:336
  6.3 0.2 multiply_reduce_fusion.1
  6.5 0.2 multiply_convert_fusion.1.image_ref.own_ref
  6.7 0.6 collective-permute-start.2
  7.3 1.5 %collective-permute-start.3 = (bf16[512,1152]{1,0:T(8,128)(2,1)S(1)}, bf16[512,1152]{1,0:T(8,128)(2,1)S(1)}, u32[]{:S(2)}, u32[]{:S(2)}) collective-permute-start(bf16[512,1152]{1,0:T(8,128)(2,1)S(1)} %multiply_convert_fusion.text_ref.own_ref), channel_id=1, source_target_pairs={{0,8},{4,12},{8,0},{12,4},{16,24},{20,28},{24,16},{28,20},{1,9},{5... | collective-permute-start | bytes 3538952 | tf_op jit(solution)/shard_map/ppermute | solution.py:341
  8.8 1.5 %collective-permute-start.4 = (bf16[512,1152]{1,0:T(8,128)(2,1)S(1)}, bf16[512,1152]{1,0:T(8,128)(2,1)S(1)}, u32[]{:S(2)}, u32[]{:S(2)}) collective-permute-start(bf16[512,1152]{1,0:T(8,128)(2,1)S(1)} %multiply_convert_fusion.text_ref.own_ref), channel_id=1, source_target_pairs={{0,16},{4,20},{8,24},{12,28},{16,0},{20,4},{24,8},{28,12},{1,17},{... | collective-permute-start | bytes 3538952 | tf_op jit(solution)/shard_map/ppermute | solution.py:341
  11.7 2.7 %diagonal.1 = (f32[512,1152]{1,0:T(8,128)S(1)}, f32[512,1152]{1,0:T(8,128)S(1)}) custom-call(f32[1]{0:T(128)S(6)} %copy.7.scale_ref, f32[1]{0:T(128)S(6)} %copy.8.shift_ref, bf16[512,1152]{1,0:T(8,128)(2,1)S(1)} %multiply_convert_fusion.1.image_ref.own_ref, bf16[512,1152]{1,0:T(8,128)(2,1)S(1)} %multiply_convert_fusion.text_ref.own_ref), custom_call_target="tpu_custom_call" | custom-call | flops 2415919104 | bytes 4718592 | tf_op jit(solution)/shard_map/diagonal/pallas_call | solution.py:28
  14.5 19.8 %collective-permute-done.refs_2_ = bf16[512,1152]{1,0:T(8,128)(2,1)S(1)} collective-permute-done((bf16[512,1152]{1,0:T(8,128)(2,1)S(1)}, bf16[512,1152]{1,0:T(8,128)(2,1)S(1)}, u32[]{:S(2)}, u32[]{:S(2)}) %collective-permute-start) | collective-permute-done | bytes 1179680 | tf_op jit(solution)/shard_map/ppermute | solution.py:336
  34.3 1.7 %collective-permute-start.7 = (bf16[384,1152]{1,0:T(8,128)(2,1)S(1)}, bf16[384,1152]{1,0:T(8,128)(2,1)S(1)}, u32[]{:S(2)}, u32[]{:S(2)}) collective-permute-start(bf16[384,1152]{1,0:T(8,128)(2,1)S(1)} %slice.8), channel_id=1, source_target_pairs={{0,3},{1,0},{2,1},{3,2},{4,7},{5,4},{6,5},{7,6},{8,11},{9,8},{10,9... | collective-permute-start | bytes 2654216 | tf_op jit(solution)/shard_map/ppermute | solution.py:336
  36.0 1.5 %collective-permute-start.5 = (bf16[384,1152]{1,0:T(8,128)(2,1)S(1)}, bf16[384,1152]{1,0:T(8,128)(2,1)S(1)}, u32[]{:S(2)}, u32[]{:S(2)}) collective-permute-start(bf16[384,1152]{1,0:T(8,128)(2,1)S(1)} %slice.8), channel_id=1, source_target_pairs={{0,8},{4,12},{8,0},{12,4},{16,24},{20,28},{24,16},{28,20},{1,9},{5... | collective-permute-start | bytes 2654216 | tf_op jit(solution)/shard_map/ppermute | solution.py:341
  37.5 1.5 %collective-permute-start.6 = (bf16[384,1152]{1,0:T(8,128)(2,1)S(1)}, bf16[384,1152]{1,0:T(8,128)(2,1)S(1)}, u32[]{:S(2)}, u32[]{:S(2)}) collective-permute-start(bf16[384,1152]{1,0:T(8,128)(2,1)S(1)} %slice.8), channel_id=1, source_target_pairs={{0,16},{4,20},{8,24},{12,28},{16,0},{20,4},{24,8},{28,12},{1,17},{... | collective-permute-start | bytes 2654216 | tf_op jit(solution)/shard_map/ppermute | solution.py:341
  39.0 4.2 %add_near.1 = (f32[512,1152]{1,0:T(8,128)S(1)}, f32[512,1152]{1,0:T(8,128)S(1)}) custom-call(f32[1]{0:T(128)S(6)} %copy.7.scale_ref, f32[1]{0:T(128)S(6)} %copy.8.shift_ref, s32[2,8]{1,0:T(2,128)S(1)} %copy-done.2, bf16[512,1152]{1,0:T(8,128)(2,1)S(1)} %multiply_convert_fusion.1.image_ref.own_ref, ...), custom_call_target="tpu_custom_call" | custom-call | flops 2415919104 | bytes 4718592 | tf_op jit(solution)/shard_map/add_near/pallas_call | solution.py:28
  43.3 0.5 collective-permute-start.10
  43.8 6.8 %finish.2 = f32[512,1152]{1,0:T(8,128)} custom-call(f32[1]{0:T(128)S(6)} %copy.7.scale_ref, f32[1]{0:T(128)S(6)} %copy.8.shift_ref, s32[2,8]{1,0:T(2,128)S(1)} %copy-done.2, bf16[512,1152]{1,0:T(8,128)(2,1)S(1)} %multiply_convert_fusion.1.image_ref.own_ref, f32[512,1152]{1,0:T(8,128)S(1)} %copy-done.1, f32[512,1152]{1,0:T(8,128)S(1)} %get-tuple-element.22.sum_ref, ...), custom_call_target="tpu_custom_call" | custom-call | flops 3623878656 | bytes 4718592 | tf_op jit(solution)/shard_map/finish/pallas_call | solution.py:28
  50.7 0.6 collective-permute-start.8
  51.3 5.6 %collective-permute-done.7.refs_2_ = bf16[384,1152]{1,0:T(8,128)(2,1)S(1)} collective-permute-done((bf16[384,1152]{1,0:T(8,128)(2,1)S(1)}, bf16[384,1152]{1,0:T(8,128)(2,1)S(1)}, u32[]{:S(2)}, u32[]{:S(2)}) %collective-permute-start.7) | collective-permute-done | bytes 884768 | tf_op jit(solution)/shard_map/ppermute | solution.py:336
  56.9 1.5 %collective-permute-start.9 = (bf16[128,1152]{1,0:T(8,128)(2,1)S(1)}, bf16[128,1152]{1,0:T(8,128)(2,1)S(1)}, u32[]{:S(2)}, u32[]{:S(2)}) collective-permute-start(bf16[128,1152]{1,0:T(8,128)(2,1)S(1)} %slice.9), channel_id=1, source_target_pairs={{0,16},{4,20},{8,24},{12,28},{16,0},{20,4},{24,8},{28,12},{1,17},{... | collective-permute-start | bytes 884744 | tf_op jit(solution)/shard_map/ppermute | solution.py:341
  58.4 0.2 collective-permute-done.5.refs_0_
  58.6 0.2 collective-permute-done.6.refs_1_
  58.8 4.6 %add_up.1.sum_ref = f32[512,1152]{1,0:T(8,128)S(1)} custom-call(f32[1]{0:T(128)S(6)} %copy.7.scale_ref, f32[1]{0:T(128)S(6)} %copy.8.shift_ref, s32[2,8]{1,0:T(2,128)S(1)} %copy-done.2, bf16[512,1152]{1,0:T(8,128)(2,1)S(1)} %multiply_convert_fusion.text_ref.own_ref, f32[512,1152]{1,0:T(8,128)S(1)} %get-tuple-element.25.sum_ref, ...), custom_call_target="tpu_custom_call" | custom-call | flops 2717908992 | bytes 4718592 | tf_op jit(solution)/shard_map/add_up/pallas_call | solution.py:28
  63.4 0.4 collective-permute-done.9.refs_1_
  63.8 3.9 %finish.3 = f32[512,1152]{1,0:T(8,128)} custom-call(f32[1]{0:T(128)S(6)} %copy.7.scale_ref, f32[1]{0:T(128)S(6)} %copy.8.shift_ref, s32[2,8]{1,0:T(2,128)S(1)} %copy-done.2, bf16[512,1152]{1,0:T(8,128)(2,1)S(1)} %multiply_convert_fusion.text_ref.own_ref, f32[512,1152]{1,0:T(8,128)S(1)} %copy-done, f32[512,1152]{1,0:T(8,128)S(1)} %add_up.1.sum_ref, ...), custom_call_target="tpu_custom_call" | custom-call | flops 905969664 | bytes 4718592 | tf_op jit(solution)/shard_map/finish/pallas_call | solution.py:28
  (17 shorter events, 0.3 us)
Async XLA Ops:
  0.6 2.4 %copy-start = (f32[512,1152]{1,0:T(8,128)S(1)}, f32[512,1152]{1,0:T(8,128)}, u32[]{:S(2)}) copy-start(f32[512,1152]{1,0:T(8,128)} %raw_ref.3) | copy-start | bytes 7077892
  2.7 3.6 %copy-start.1 = (f32[512,1152]{1,0:T(8,128)S(1)}, f32[512,1152]{1,0:T(8,128)}, u32[]{:S(2)}) copy-start(f32[512,1152]{1,0:T(8,128)} %raw_ref.2) | copy-start | bytes 7077892
  3.2 31.1 %collective-permute-start = (bf16[512,1152]{1,0:T(8,128)(2,1)S(1)}, bf16[512,1152]{1,0:T(8,128)(2,1)S(1)}, u32[]{:S(2)}, u32[]{:S(2)}) collective-permute-start(bf16[512,1152]{1,0:T(8,128)(2,1)S(1)} %multiply_convert_fusion.text_ref.own_ref), channel_id=1, source_target_pairs={{0,1},{1,2},{2,3},{3,0},{4,5},{5,6},{6,7},{7,4},{8,9},{9,10},{10,1... | collective-permute-start | bytes 3538952 | tf_op jit(solution)/shard_map/ppermute | solution.py:336
  6.3 29.7 %collective-permute-start.1 = (bf16[512,1152]{1,0:T(8,128)(2,1)S(1)}, bf16[512,1152]{1,0:T(8,128)(2,1)S(1)}, u32[]{:S(2)}, u32[]{:S(2)}) collective-permute-start(bf16[512,1152]{1,0:T(8,128)(2,1)S(1)} %multiply_convert_fusion.text_ref.own_ref), channel_id=1, source_target_pairs={{0,4},{4,0},{8,12},{12,8},{16,20},{20,16},{24,28},{28,24},{1,5},{5... | collective-permute-start | bytes 3538952 | tf_op jit(solution)/shard_map/ppermute | solution.py:341
  6.7 30.8 %collective-permute-start.2 = (bf16[512,1152]{1,0:T(8,128)(2,1)S(1)}, bf16[512,1152]{1,0:T(8,128)(2,1)S(1)}, u32[]{:S(2)}, u32[]{:S(2)}) collective-permute-start(bf16[512,1152]{1,0:T(8,128)(2,1)S(1)} %multiply_convert_fusion.1.image_ref.own_ref), channel_id=1, source_target_pairs={{0,4},{4,0},{8,12},{12,8},{16,20},{20,16},{24,28},{28,24},{1,5},{5... | collective-permute-start | bytes 3538952 | tf_op jit(solution)/shard_map/ppermute | solution.py:341
  7.3 36.0 %collective-permute-start.3 = (bf16[512,1152]{1,0:T(8,128)(2,1)S(1)}, bf16[512,1152]{1,0:T(8,128)(2,1)S(1)}, u32[]{:S(2)}, u32[]{:S(2)}) collective-permute-start(bf16[512,1152]{1,0:T(8,128)(2,1)S(1)} %multiply_convert_fusion.text_ref.own_ref), channel_id=1, source_target_pairs={{0,8},{4,12},{8,0},{12,4},{16,24},{20,28},{24,16},{28,20},{1,9},{5... | collective-permute-start | bytes 3538952 | tf_op jit(solution)/shard_map/ppermute | solution.py:341
  8.8 35.0 %collective-permute-start.4 = (bf16[512,1152]{1,0:T(8,128)(2,1)S(1)}, bf16[512,1152]{1,0:T(8,128)(2,1)S(1)}, u32[]{:S(2)}, u32[]{:S(2)}) collective-permute-start(bf16[512,1152]{1,0:T(8,128)(2,1)S(1)} %multiply_convert_fusion.text_ref.own_ref), channel_id=1, source_target_pairs={{0,16},{4,20},{8,24},{12,28},{16,0},{20,4},{24,8},{28,12},{1,17},{... | collective-permute-start | bytes 3538952 | tf_op jit(solution)/shard_map/ppermute | solution.py:341
  11.7 27.3 %copy-start.2 = (s32[2,8]{1,0:T(2,128)S(1)}, s32[2,8]{1,0:T(2,128)}, u32[]{:S(2)}) copy-start(s32[2,8]{1,0:T(2,128)} %grid_ref.7) | copy-start | bytes 196
  34.3 22.6 %collective-permute-start.7 = (bf16[384,1152]{1,0:T(8,128)(2,1)S(1)}, bf16[384,1152]{1,0:T(8,128)(2,1)S(1)}, u32[]{:S(2)}, u32[]{:S(2)}) collective-permute-start(bf16[384,1152]{1,0:T(8,128)(2,1)S(1)} %slice.8), channel_id=1, source_target_pairs={{0,3},{1,0},{2,1},{3,2},{4,7},{5,4},{6,5},{7,6},{8,11},{9,8},{10,9... | collective-permute-start | bytes 2654216 | tf_op jit(solution)/shard_map/ppermute | solution.py:336
  36.0 22.6 %collective-permute-start.5 = (bf16[384,1152]{1,0:T(8,128)(2,1)S(1)}, bf16[384,1152]{1,0:T(8,128)(2,1)S(1)}, u32[]{:S(2)}, u32[]{:S(2)}) collective-permute-start(bf16[384,1152]{1,0:T(8,128)(2,1)S(1)} %slice.8), channel_id=1, source_target_pairs={{0,8},{4,12},{8,0},{12,4},{16,24},{20,28},{24,16},{28,20},{1,9},{5... | collective-permute-start | bytes 2654216 | tf_op jit(solution)/shard_map/ppermute | solution.py:341
  37.5 21.3 %collective-permute-start.6 = (bf16[384,1152]{1,0:T(8,128)(2,1)S(1)}, bf16[384,1152]{1,0:T(8,128)(2,1)S(1)}, u32[]{:S(2)}, u32[]{:S(2)}) collective-permute-start(bf16[384,1152]{1,0:T(8,128)(2,1)S(1)} %slice.8), channel_id=1, source_target_pairs={{0,16},{4,20},{8,24},{12,28},{16,0},{20,4},{24,8},{28,12},{1,17},{... | collective-permute-start | bytes 2654216 | tf_op jit(solution)/shard_map/ppermute | solution.py:341
  43.3 20.1 %collective-permute-start.10 = (bf16[128,1152]{1,0:T(8,128)(2,1)S(1)}, bf16[128,1152]{1,0:T(8,128)(2,1)S(1)}, u32[]{:S(2)}, u32[]{:S(2)}) collective-permute-start(bf16[128,1152]{1,0:T(8,128)(2,1)S(1)} %slice.9), channel_id=1, source_target_pairs={{0,3},{1,0},{2,1},{3,2},{4,7},{5,4},{6,5},{7,6},{8,11},{9,8},{10,9... | collective-permute-start | bytes 884744 | tf_op jit(solution)/shard_map/ppermute | solution.py:336
  50.7 12.7 %collective-permute-start.8 = (bf16[128,1152]{1,0:T(8,128)(2,1)S(1)}, bf16[128,1152]{1,0:T(8,128)(2,1)S(1)}, u32[]{:S(2)}, u32[]{:S(2)}) collective-permute-start(bf16[128,1152]{1,0:T(8,128)(2,1)S(1)} %slice.9), channel_id=1, source_target_pairs={{0,8},{4,12},{8,0},{12,4},{16,24},{20,28},{24,16},{28,20},{1,9},{5... | collective-permute-start | bytes 884744 | tf_op jit(solution)/shard_map/ppermute | solution.py:341
  56.9 6.9 %collective-permute-start.9 = (bf16[128,1152]{1,0:T(8,128)(2,1)S(1)}, bf16[128,1152]{1,0:T(8,128)(2,1)S(1)}, u32[]{:S(2)}, u32[]{:S(2)}) collective-permute-start(bf16[128,1152]{1,0:T(8,128)(2,1)S(1)} %slice.9), channel_id=1, source_target_pairs={{0,16},{4,20},{8,24},{12,28},{16,0},{20,4},{24,8},{28,12},{1,17},{... | collective-permute-start | bytes 884744 | tf_op jit(solution)/shard_map/ppermute | solution.py:341

commit v9 on v8

--- a/solution.py
+++ b/solution.py
@@ -181,8 +181,8 @@
     return sums
 
 
-def blocks_of(count):
-    return [(first, min(BLOCK, count - first)) for first in range(0, count, BLOCK)]
+def blocks_of(count, size=BLOCK):
+    return [(first, min(size, count - first)) for first in range(0, count, size)]
 
 
 def drawn_factors(bits, scale_ref, grid_ref):
@@ -282,12 +282,12 @@
     )[0]
 
 
-def finish_kernel(bits, scale_ref, shift_ref, grid_ref, own_ref, raw_ref, sum_ref, *refs):
+def finish_kernel(bits, size, scale_ref, shift_ref, grid_ref, own_ref, raw_ref, sum_ref, *refs):
     other_refs, (out_ref, weights_ref, total_ref, sems, all_ref) = refs[: len(bits)], refs[len(bits) :]
 
     def run(others, counts, factors):
         copies = []
-        for first, block in blocks_of(own_ref.shape[0]):
+        for first, block in blocks_of(own_ref.shape[0], size):
             sums = add_pairs(
                 scale_ref[0], factors, shift_ref[0], own_ref, (first, block), counts, others, sum_ref,
                 total_ref, weights_ref, raw_ref,
@@ -311,11 +311,11 @@
     for_drawn(bits, scale_ref, grid_ref, other_refs, all_ref, run)
 
 
-def finish(scale, shift, grid, own, raw, total, others, bits):
+def finish(scale, shift, grid, own, raw, total, others, bits, size=BLOCK):
     rows, width = own.shape
     count = sum(x.shape[0] for x in others)
     return call(
-        functools.partial(finish_kernel, tuple(bits)),
+        functools.partial(finish_kernel, tuple(bits), size),
         "finish",
         [scale, shift, grid, own, raw, total, *others],
         [((rows, width), jnp.float32)],
@@ -375,7 +375,7 @@
     )
     text_gradient = finish(
         scale, shift, grid, text_half, caption, text_sum,
-        [*far_images_last, image_z_last], [*far, None],
+        [*far_images_last, image_z_last], [*far, None], BLOCK // 2,
     )
     return image_gradient, text_gradient
 

time: 67.9 us -> 68.5 us (level)
  waiting for transfers between devices: 26.2 us -> 28.4 us
  Pallas kernels: 22.3 us -> 20.6 us
    pallas_call x5, Pallas kernels: 22.3 us -> 20.6 us  [call(): pl.pallas_call(body, grid=grid or (), in_specs=[SMEM] * smem + [VMEM] * (...]
    ppermute x8, waiting for transfers between devices: 0.82 us -> 2 us  [exchanged(): return lax.ppermute(x, 'blk', [(i, i ^ 1 << bit) for i in range(count)])]
    ppermute x3, waiting for transfers between devices: 25.4 us -> 26.4 us  [passed_along(): return lax.ppermute(x, axis, [(i, (i + by) % count) for i in range(count)])]
  transfers between devices with their start and end apart: 11 -> 11, of which waited for: 5 -> 6; matrix products, arithmetic and copies ran while one was open for 1% -> 1% of each run, Pallas kernels for 27% -> 24%
where the time goes in v9:
time: 68.5 us; the launch traced here: 68.3 us
  waiting for transfers between devices  28.4 us (41%)
  Pallas kernels  20.6 us (30%)
  starting transfers between devices  14 us (20%)
  other arithmetic  2.68 us (4%)
  between operations  2.21 us (3%)
    ppermute x3, waiting for transfers between devices, passed_along(): return lax.ppermute(x, axis, [(i, (i + by) % count) for i in range(count)])  26.4 us
    pallas_call x5, Pallas kernels, call(): pl.pallas_call(body, grid=grid or (), in_specs=[SMEM] * smem + [VMEM] * (...  20.6 us
    ppermute x8, starting transfers between devices, exchanged(): return lax.ppermute(x, 'blk', [(i, i ^ 1 << bit) for i in range(count)])  8.69 us
    ppermute x3, starting transfers between devices, passed_along(): return lax.ppermute(x, axis, [(i, (i + by) % count) for i in range(count)])  5.34 us
    reduce_sum x2, other arithmetic, normalized(): total = jnp.sum(raw * raw, axis=-1, keepdims=True)  2.27 us
    ppermute x8, waiting for transfers between devices, exchanged(): return lax.ppermute(x, 'blk', [(i, i ^ 1 << bit) for i in range(count)])  2 us
  transfers between devices with their start and end apart: 11, of which 6 were waited for; matrix products, arithmetic and copies ran while one was open for 1% of the time, Pallas kernels for 24%

profile of v9, /device:TPU:0, one launch (start us, length us, event | category | flops | bytes accessed | tf_op | source)
XLA Modules:
  0.0 68.3 jit_solution(13658061323457011956)
XLA Ops:
  0.6 2.0 %multiply_reduce_fusion = f32[512]{0:T(512)S(1)} fusion(f32[512,1152]{1,0:T(8,128)} %raw_ref.3), kind=kLoop, calls=%fused_computation.1 | loop fusion | flops 1179136 | bytes 2361344 | tf_op jit(solution)/shard_map/reduce_sum | solution.py:46
  2.7 0.3 copy-done
  3.2 3.1 %collective-permute-start = (bf16[512,1152]{1,0:T(8,128)(2,1)S(1)}, bf16[512,1152]{1,0:T(8,128)(2,1)S(1)}, u32[]{:S(2)}, u32[]{:S(2)}) collective-permute-start(bf16[512,1152]{1,0:T(8,128)(2,1)S(1)} %multiply_convert_fusion.text_ref.own_ref), channel_id=1, source_target_pairs={{0,1},{1,2},{2,3},{3,0},{4,5},{5,6},{6,7},{7,4},{8,9},{9,10},{10,1... | collective-permute-start | bytes 3538952 | tf_op jit(solution)/shard_map/ppermute | solution.py:336
  6.3 0.2 multiply_reduce_fusion.1
  6.7 0.6 collective-permute-start.2
  7.3 1.5 %collective-permute-start.3 = (bf16[512,1152]{1,0:T(8,128)(2,1)S(1)}, bf16[512,1152]{1,0:T(8,128)(2,1)S(1)}, u32[]{:S(2)}, u32[]{:S(2)}) collective-permute-start(bf16[512,1152]{1,0:T(8,128)(2,1)S(1)} %multiply_convert_fusion.text_ref.own_ref), channel_id=1, source_target_pairs={{0,8},{4,12},{8,0},{12,4},{16,24},{20,28},{24,16},{28,20},{1,9},{5... | collective-permute-start | bytes 3538952 | tf_op jit(solution)/shard_map/ppermute | solution.py:341
  8.8 1.5 %collective-permute-start.4 = (bf16[512,1152]{1,0:T(8,128)(2,1)S(1)}, bf16[512,1152]{1,0:T(8,128)(2,1)S(1)}, u32[]{:S(2)}, u32[]{:S(2)}) collective-permute-start(bf16[512,1152]{1,0:T(8,128)(2,1)S(1)} %multiply_convert_fusion.text_ref.own_ref), channel_id=1, source_target_pairs={{0,16},{4,20},{8,24},{12,28},{16,0},{20,4},{24,8},{28,12},{1,17},{... | collective-permute-start | bytes 3538952 | tf_op jit(solution)/shard_map/ppermute | solution.py:341
  11.7 2.7 %diagonal.1 = (f32[512,1152]{1,0:T(8,128)S(1)}, f32[512,1152]{1,0:T(8,128)S(1)}) custom-call(f32[1]{0:T(128)S(6)} %copy.7.scale_ref, f32[1]{0:T(128)S(6)} %copy.8.shift_ref, bf16[512,1152]{1,0:T(8,128)(2,1)S(1)} %multiply_convert_fusion.1.image_ref.own_ref, bf16[512,1152]{1,0:T(8,128)(2,1)S(1)} %multiply_convert_fusion.text_ref.own_ref), custom_call_target="tpu_custom_call" | custom-call | flops 2415919104 | bytes 4718592 | tf_op jit(solution)/shard_map/diagonal/pallas_call | solution.py:28
  14.5 19.8 %collective-permute-done.refs_2_ = bf16[512,1152]{1,0:T(8,128)(2,1)S(1)} collective-permute-done((bf16[512,1152]{1,0:T(8,128)(2,1)S(1)}, bf16[512,1152]{1,0:T(8,128)(2,1)S(1)}, u32[]{:S(2)}, u32[]{:S(2)}) %collective-permute-start) | collective-permute-done | bytes 1179680 | tf_op jit(solution)/shard_map/ppermute | solution.py:336
  34.3 1.7 %collective-permute-start.7 = (bf16[384,1152]{1,0:T(8,128)(2,1)S(1)}, bf16[384,1152]{1,0:T(8,128)(2,1)S(1)}, u32[]{:S(2)}, u32[]{:S(2)}) collective-permute-start(bf16[384,1152]{1,0:T(8,128)(2,1)S(1)} %slice.8), channel_id=1, source_target_pairs={{0,3},{1,0},{2,1},{3,2},{4,7},{5,4},{6,5},{7,6},{8,11},{9,8},{10,9... | collective-permute-start | bytes 2654216 | tf_op jit(solution)/shard_map/ppermute | solution.py:336
  36.0 1.5 %collective-permute-start.5 = (bf16[384,1152]{1,0:T(8,128)(2,1)S(1)}, bf16[384,1152]{1,0:T(8,128)(2,1)S(1)}, u32[]{:S(2)}, u32[]{:S(2)}) collective-permute-start(bf16[384,1152]{1,0:T(8,128)(2,1)S(1)} %slice.8), channel_id=1, source_target_pairs={{0,8},{4,12},{8,0},{12,4},{16,24},{20,28},{24,16},{28,20},{1,9},{5... | collective-permute-start | bytes 2654216 | tf_op jit(solution)/shard_map/ppermute | solution.py:341
  37.5 1.5 %collective-permute-start.6 = (bf16[384,1152]{1,0:T(8,128)(2,1)S(1)}, bf16[384,1152]{1,0:T(8,128)(2,1)S(1)}, u32[]{:S(2)}, u32[]{:S(2)}) collective-permute-start(bf16[384,1152]{1,0:T(8,128)(2,1)S(1)} %slice.8), channel_id=1, source_target_pairs={{0,16},{4,20},{8,24},{12,28},{16,0},{20,4},{24,8},{28,12},{1,17},{... | collective-permute-start | bytes 2654216 | tf_op jit(solution)/shard_map/ppermute | solution.py:341
  39.0 4.2 %add_near.1 = (f32[512,1152]{1,0:T(8,128)S(1)}, f32[512,1152]{1,0:T(8,128)S(1)}) custom-call(f32[1]{0:T(128)S(6)} %copy.7.scale_ref, f32[1]{0:T(128)S(6)} %copy.8.shift_ref, s32[2,8]{1,0:T(2,128)S(1)} %copy-done.2, bf16[512,1152]{1,0:T(8,128)(2,1)S(1)} %multiply_convert_fusion.1.image_ref.own_ref, ...), custom_call_target="tpu_custom_call" | custom-call | flops 2415919104 | bytes 4718592 | tf_op jit(solution)/shard_map/add_near/pallas_call | solution.py:28
  43.3 0.5 collective-permute-start.10
  43.8 5.9 %finish.2 = f32[512,1152]{1,0:T(8,128)} custom-call(f32[1]{0:T(128)S(6)} %copy.7.scale_ref, f32[1]{0:T(128)S(6)} %copy.8.shift_ref, s32[2,8]{1,0:T(2,128)S(1)} %copy-done.2, bf16[512,1152]{1,0:T(8,128)(2,1)S(1)} %multiply_convert_fusion.1.image_ref.own_ref, f32[512,1152]{1,0:T(8,128)S(1)} %copy-done.1, f32[512,1152]{1,0:T(8,128)S(1)} %get-tuple-element.22.sum_ref, ...), custom_call_target="tpu_custom_call" | custom-call | flops 3623878656 | bytes 4718592 | tf_op jit(solution)/shard_map/finish/pallas_call | solution.py:28
  49.7 0.6 collective-permute-start.8
  50.3 6.6 %collective-permute-done.7.refs_2_ = bf16[384,1152]{1,0:T(8,128)(2,1)S(1)} collective-permute-done((bf16[384,1152]{1,0:T(8,128)(2,1)S(1)}, bf16[384,1152]{1,0:T(8,128)(2,1)S(1)}, u32[]{:S(2)}, u32[]{:S(2)}) %collective-permute-start.7) | collective-permute-done | bytes 884768 | tf_op jit(solution)/shard_map/ppermute | solution.py:336
  56.9 1.5 %collective-permute-start.9 = (bf16[128,1152]{1,0:T(8,128)(2,1)S(1)}, bf16[128,1152]{1,0:T(8,128)(2,1)S(1)}, u32[]{:S(2)}, u32[]{:S(2)}) collective-permute-start(bf16[128,1152]{1,0:T(8,128)(2,1)S(1)} %slice.9), channel_id=1, source_target_pairs={{0,16},{4,20},{8,24},{12,28},{16,0},{20,4},{24,8},{28,12},{1,17},{... | collective-permute-start | bytes 884744 | tf_op jit(solution)/shard_map/ppermute | solution.py:341
  58.4 0.2 collective-permute-done.5.refs_0_
  58.6 0.2 collective-permute-done.6.refs_1_
  58.8 3.4 %add_up.1.sum_ref = f32[512,1152]{1,0:T(8,128)S(1)} custom-call(f32[1]{0:T(128)S(6)} %copy.7.scale_ref, f32[1]{0:T(128)S(6)} %copy.8.shift_ref, s32[2,8]{1,0:T(2,128)S(1)} %copy-done.2, bf16[512,1152]{1,0:T(8,128)(2,1)S(1)} %multiply_convert_fusion.text_ref.own_ref, f32[512,1152]{1,0:T(8,128)S(1)} %get-tuple-element.25.sum_ref, ...), custom_call_target="tpu_custom_call" | custom-call | flops 2717908992 | bytes 4718592 | tf_op jit(solution)/shard_map/add_up/pallas_call | solution.py:28
  62.2 0.4 collective-permute-done.8.refs_0_
  62.6 1.2 %collective-permute-done.9.refs_1_ = bf16[128,1152]{1,0:T(8,128)(2,1)S(1)} collective-permute-done((bf16[128,1152]{1,0:T(8,128)(2,1)S(1)}, bf16[128,1152]{1,0:T(8,128)(2,1)S(1)}, u32[]{:S(2)}, u32[]{:S(2)}) %collective-permute-start.9) | collective-permute-done | bytes 294944 | tf_op jit(solution)/shard_map/ppermute | solution.py:341
  63.8 4.3 %finish.3 = f32[512,1152]{1,0:T(8,128)} custom-call(f32[1]{0:T(128)S(6)} %copy.7.scale_ref, f32[1]{0:T(128)S(6)} %copy.8.shift_ref, s32[2,8]{1,0:T(2,128)S(1)} %copy-done.2, bf16[512,1152]{1,0:T(8,128)(2,1)S(1)} %multiply_convert_fusion.text_ref.own_ref, f32[512,1152]{1,0:T(8,128)S(1)} %copy-done, f32[512,1152]{1,0:T(8,128)S(1)} %add_up.1.sum_ref, ...), custom_call_target="tpu_custom_call" | custom-call | flops 905969664 | bytes 4718592 | tf_op jit(solution)/shard_map/finish/pallas_call | solution.py:28
  (17 shorter events, 0.5 us)
Async XLA Ops:
  0.6 2.4 %copy-start = (f32[512,1152]{1,0:T(8,128)S(1)}, f32[512,1152]{1,0:T(8,128)}, u32[]{:S(2)}) copy-start(f32[512,1152]{1,0:T(8,128)} %raw_ref.3) | copy-start | bytes 7077892
  2.7 3.6 %copy-start.1 = (f32[512,1152]{1,0:T(8,128)S(1)}, f32[512,1152]{1,0:T(8,128)}, u32[]{:S(2)}) copy-start(f32[512,1152]{1,0:T(8,128)} %raw_ref.2) | copy-start | bytes 7077892
  3.2 31.1 %collective-permute-start = (bf16[512,1152]{1,0:T(8,128)(2,1)S(1)}, bf16[512,1152]{1,0:T(8,128)(2,1)S(1)}, u32[]{:S(2)}, u32[]{:S(2)}) collective-permute-start(bf16[512,1152]{1,0:T(8,128)(2,1)S(1)} %multiply_convert_fusion.text_ref.own_ref), channel_id=1, source_target_pairs={{0,1},{1,2},{2,3},{3,0},{4,5},{5,6},{6,7},{7,4},{8,9},{9,10},{10,1... | collective-permute-start | bytes 3538952 | tf_op jit(solution)/shard_map/ppermute | solution.py:336
  6.3 29.7 %collective-permute-start.1 = (bf16[512,1152]{1,0:T(8,128)(2,1)S(1)}, bf16[512,1152]{1,0:T(8,128)(2,1)S(1)}, u32[]{:S(2)}, u32[]{:S(2)}) collective-permute-start(bf16[512,1152]{1,0:T(8,128)(2,1)S(1)} %multiply_convert_fusion.text_ref.own_ref), channel_id=1, source_target_pairs={{0,4},{4,0},{8,12},{12,8},{16,20},{20,16},{24,28},{28,24},{1,5},{5... | collective-permute-start | bytes 3538952 | tf_op jit(solution)/shard_map/ppermute | solution.py:341
  6.7 30.8 %collective-permute-start.2 = (bf16[512,1152]{1,0:T(8,128)(2,1)S(1)}, bf16[512,1152]{1,0:T(8,128)(2,1)S(1)}, u32[]{:S(2)}, u32[]{:S(2)}) collective-permute-start(bf16[512,1152]{1,0:T(8,128)(2,1)S(1)} %multiply_convert_fusion.1.image_ref.own_ref), channel_id=1, source_target_pairs={{0,4},{4,0},{8,12},{12,8},{16,20},{20,16},{24,28},{28,24},{1,5},{5... | collective-permute-start | bytes 3538952 | tf_op jit(solution)/shard_map/ppermute | solution.py:341
  7.3 36.0 %collective-permute-start.3 = (bf16[512,1152]{1,0:T(8,128)(2,1)S(1)}, bf16[512,1152]{1,0:T(8,128)(2,1)S(1)}, u32[]{:S(2)}, u32[]{:S(2)}) collective-permute-start(bf16[512,1152]{1,0:T(8,128)(2,1)S(1)} %multiply_convert_fusion.text_ref.own_ref), channel_id=1, source_target_pairs={{0,8},{4,12},{8,0},{12,4},{16,24},{20,28},{24,16},{28,20},{1,9},{5... | collective-permute-start | bytes 3538952 | tf_op jit(solution)/shard_map/ppermute | solution.py:341
  8.8 35.0 %collective-permute-start.4 = (bf16[512,1152]{1,0:T(8,128)(2,1)S(1)}, bf16[512,1152]{1,0:T(8,128)(2,1)S(1)}, u32[]{:S(2)}, u32[]{:S(2)}) collective-permute-start(bf16[512,1152]{1,0:T(8,128)(2,1)S(1)} %multiply_convert_fusion.text_ref.own_ref), channel_id=1, source_target_pairs={{0,16},{4,20},{8,24},{12,28},{16,0},{20,4},{24,8},{28,12},{1,17},{... | collective-permute-start | bytes 3538952 | tf_op jit(solution)/shard_map/ppermute | solution.py:341
  11.7 27.3 %copy-start.2 = (s32[2,8]{1,0:T(2,128)S(1)}, s32[2,8]{1,0:T(2,128)}, u32[]{:S(2)}) copy-start(s32[2,8]{1,0:T(2,128)} %grid_ref.7) | copy-start | bytes 196
  34.3 22.6 %collective-permute-start.7 = (bf16[384,1152]{1,0:T(8,128)(2,1)S(1)}, bf16[384,1152]{1,0:T(8,128)(2,1)S(1)}, u32[]{:S(2)}, u32[]{:S(2)}) collective-permute-start(bf16[384,1152]{1,0:T(8,128)(2,1)S(1)} %slice.8), channel_id=1, source_target_pairs={{0,3},{1,0},{2,1},{3,2},{4,7},{5,4},{6,5},{7,6},{8,11},{9,8},{10,9... | collective-permute-start | bytes 2654216 | tf_op jit(solution)/shard_map/ppermute | solution.py:336
  36.0 22.6 %collective-permute-start.5 = (bf16[384,1152]{1,0:T(8,128)(2,1)S(1)}, bf16[384,1152]{1,0:T(8,128)(2,1)S(1)}, u32[]{:S(2)}, u32[]{:S(2)}) collective-permute-start(bf16[384,1152]{1,0:T(8,128)(2,1)S(1)} %slice.8), channel_id=1, source_target_pairs={{0,8},{4,12},{8,0},{12,4},{16,24},{20,28},{24,16},{28,20},{1,9},{5... | collective-permute-start | bytes 2654216 | tf_op jit(solution)/shard_map/ppermute | solution.py:341
  37.5 21.3 %collective-permute-start.6 = (bf16[384,1152]{1,0:T(8,128)(2,1)S(1)}, bf16[384,1152]{1,0:T(8,128)(2,1)S(1)}, u32[]{:S(2)}, u32[]{:S(2)}) collective-permute-start(bf16[384,1152]{1,0:T(8,128)(2,1)S(1)} %slice.8), channel_id=1, source_target_pairs={{0,16},{4,20},{8,24},{12,28},{16,0},{20,4},{24,8},{28,12},{1,17},{... | collective-permute-start | bytes 2654216 | tf_op jit(solution)/shard_map/ppermute | solution.py:341
  43.3 19.3 %collective-permute-start.10 = (bf16[128,1152]{1,0:T(8,128)(2,1)S(1)}, bf16[128,1152]{1,0:T(8,128)(2,1)S(1)}, u32[]{:S(2)}, u32[]{:S(2)}) collective-permute-start(bf16[128,1152]{1,0:T(8,128)(2,1)S(1)} %slice.9), channel_id=1, source_target_pairs={{0,3},{1,0},{2,1},{3,2},{4,7},{5,4},{6,5},{7,6},{8,11},{9,8},{10,9... | collective-permute-start | bytes 884744 | tf_op jit(solution)/shard_map/ppermute | solution.py:336
  49.7 12.9 %collective-permute-start.8 = (bf16[128,1152]{1,0:T(8,128)(2,1)S(1)}, bf16[128,1152]{1,0:T(8,128)(2,1)S(1)}, u32[]{:S(2)}, u32[]{:S(2)}) collective-permute-start(bf16[128,1152]{1,0:T(8,128)(2,1)S(1)} %slice.9), channel_id=1, source_target_pairs={{0,8},{4,12},{8,0},{12,4},{16,24},{20,28},{24,16},{28,20},{1,9},{5... | collective-permute-start | bytes 884744 | tf_op jit(solution)/shard_map/ppermute | solution.py:341
  56.9 6.9 %collective-permute-start.9 = (bf16[128,1152]{1,0:T(8,128)(2,1)S(1)}, bf16[128,1152]{1,0:T(8,128)(2,1)S(1)}, u32[]{:S(2)}, u32[]{:S(2)}) collective-permute-start(bf16[128,1152]{1,0:T(8,128)(2,1)S(1)} %slice.9), channel_id=1, source_target_pairs={{0,16},{4,20},{8,24},{12,28},{16,0},{20,4},{24,8},{28,12},{1,17},{... | collective-permute-start | bytes 884744 | tf_op jit(solution)/shard_map/ppermute | solution.py:341

commit v10 on v8

--- a/solution.py
+++ b/solution.py
@@ -342,7 +342,7 @@
 
 
 def with_partners(bits, visual, caption, grid, scale, shift):
-    cut = visual.shape[0] * 3 // 4
+    cut = visual.shape[0] * 11 // 16
     near, far = [bit for bit in bits if bit == 0], [bit for bit in bits if bit != 0]
     text_half = normalized(caption)
     text_z = passed_along(text_half, "group", 1)

time: 67.9 us -> 68.1 us (level)
  waiting for transfers between devices: 26.2 us -> 28.4 us
  Pallas kernels: 22.3 us -> 20.3 us
    ppermute x8, waiting for transfers between devices: 0.82 us -> 3.59 us  [exchanged(): return lax.ppermute(x, 'blk', [(i, i ^ 1 << bit) for i in range(count)])]
    pallas_call x5, Pallas kernels: 22.3 us -> 20.3 us  [call(): pl.pallas_call(body, grid=grid or (), in_specs=[SMEM] * smem + [VMEM] * (...]
  transfers between devices with their start and end apart: 11 -> 11, of which waited for: 5 -> 6; matrix products, arithmetic and copies ran while one was open for 1% -> 1% of each run, Pallas kernels for 27% -> 24%
where the time goes in v10:
time: 68.1 us; the launch traced here: 68 us
  waiting for transfers between devices  28.4 us (42%)
  Pallas kernels  20.3 us (30%)
  starting transfers between devices  14 us (21%)
  other arithmetic  2.68 us (4%)
  between operations  2.21 us (3%)
    ppermute x3, waiting for transfers between devices, passed_along(): return lax.ppermute(x, axis, [(i, (i + by) % count) for i in range(count)])  24.8 us
    pallas_call x5, Pallas kernels, call(): pl.pallas_call(body, grid=grid or (), in_specs=[SMEM] * smem + [VMEM] * (...  20.3 us
    ppermute x8, starting transfers between devices, exchanged(): return lax.ppermute(x, 'blk', [(i, i ^ 1 << bit) for i in range(count)])  8.69 us
    ppermute x3, starting transfers between devices, passed_along(): return lax.ppermute(x, axis, [(i, (i + by) % count) for i in range(count)])  5.34 us
    ppermute x8, waiting for transfers between devices, exchanged(): return lax.ppermute(x, 'blk', [(i, i ^ 1 << bit) for i in range(count)])  3.59 us
    reduce_sum x2, other arithmetic, normalized(): total = jnp.sum(raw * raw, axis=-1, keepdims=True)  2.27 us
  transfers between devices with their start and end apart: 11, of which 6 were waited for; matrix products, arithmetic and copies ran while one was open for 1% of the time, Pallas kernels for 24%

profile of v10, /device:TPU:0, one launch (start us, length us, event | category | flops | bytes accessed | tf_op | source)
XLA Modules:
  0.0 68.0 jit_solution(8908843515268142501)
XLA Ops:
  0.6 2.0 %multiply_reduce_fusion = f32[512]{0:T(512)S(1)} fusion(f32[512,1152]{1,0:T(8,128)} %raw_ref.3), kind=kLoop, calls=%fused_computation.1 | loop fusion | flops 1179136 | bytes 2361344 | tf_op jit(solution)/shard_map/reduce_sum | solution.py:46
  2.7 0.3 copy-done
  3.2 3.1 %collective-permute-start = (bf16[512,1152]{1,0:T(8,128)(2,1)S(1)}, bf16[512,1152]{1,0:T(8,128)(2,1)S(1)}, u32[]{:S(2)}, u32[]{:S(2)}) collective-permute-start(bf16[512,1152]{1,0:T(8,128)(2,1)S(1)} %multiply_convert_fusion.text_ref.own_ref), channel_id=1, source_target_pairs={{0,1},{1,2},{2,3},{3,0},{4,5},{5,6},{6,7},{7,4},{8,9},{9,10},{10,1... | collective-permute-start | bytes 3538952 | tf_op jit(solution)/shard_map/ppermute | solution.py:336
  6.3 0.2 multiply_reduce_fusion.1
  6.7 0.6 collective-permute-start.2
  7.3 1.5 %collective-permute-start.3 = (bf16[512,1152]{1,0:T(8,128)(2,1)S(1)}, bf16[512,1152]{1,0:T(8,128)(2,1)S(1)}, u32[]{:S(2)}, u32[]{:S(2)}) collective-permute-start(bf16[512,1152]{1,0:T(8,128)(2,1)S(1)} %multiply_convert_fusion.text_ref.own_ref), channel_id=1, source_target_pairs={{0,8},{4,12},{8,0},{12,4},{16,24},{20,28},{24,16},{28,20},{1,9},{5... | collective-permute-start | bytes 3538952 | tf_op jit(solution)/shard_map/ppermute | solution.py:341
  8.8 1.5 %collective-permute-start.4 = (bf16[512,1152]{1,0:T(8,128)(2,1)S(1)}, bf16[512,1152]{1,0:T(8,128)(2,1)S(1)}, u32[]{:S(2)}, u32[]{:S(2)}) collective-permute-start(bf16[512,1152]{1,0:T(8,128)(2,1)S(1)} %multiply_convert_fusion.text_ref.own_ref), channel_id=1, source_target_pairs={{0,16},{4,20},{8,24},{12,28},{16,0},{20,4},{24,8},{28,12},{1,17},{... | collective-permute-start | bytes 3538952 | tf_op jit(solution)/shard_map/ppermute | solution.py:341
  11.7 2.7 %diagonal.1 = (f32[512,1152]{1,0:T(8,128)S(1)}, f32[512,1152]{1,0:T(8,128)S(1)}) custom-call(f32[1]{0:T(128)S(6)} %copy.7.scale_ref, f32[1]{0:T(128)S(6)} %copy.8.shift_ref, bf16[512,1152]{1,0:T(8,128)(2,1)S(1)} %multiply_convert_fusion.1.image_ref.own_ref, bf16[512,1152]{1,0:T(8,128)(2,1)S(1)} %multiply_convert_fusion.text_ref.own_ref), custom_call_target="tpu_custom_call" | custom-call | flops 2415919104 | bytes 4718592 | tf_op jit(solution)/shard_map/diagonal/pallas_call | solution.py:28
  14.5 19.8 %collective-permute-done.refs_2_ = bf16[512,1152]{1,0:T(8,128)(2,1)S(1)} collective-permute-done((bf16[512,1152]{1,0:T(8,128)(2,1)S(1)}, bf16[512,1152]{1,0:T(8,128)(2,1)S(1)}, u32[]{:S(2)}, u32[]{:S(2)}) %collective-permute-start) | collective-permute-done | bytes 1179680 | tf_op jit(solution)/shard_map/ppermute | solution.py:336
  34.3 1.7 %collective-permute-start.7 = (bf16[352,1152]{1,0:T(8,128)(2,1)S(1)}, bf16[352,1152]{1,0:T(8,128)(2,1)S(1)}, u32[]{:S(2)}, u32[]{:S(2)}) collective-permute-start(bf16[352,1152]{1,0:T(8,128)(2,1)S(1)} %slice.8), channel_id=1, source_target_pairs={{0,3},{1,0},{2,1},{3,2},{4,7},{5,4},{6,5},{7,6},{8,11},{9,8},{10,9... | collective-permute-start | bytes 2433032 | tf_op jit(solution)/shard_map/ppermute | solution.py:336
  36.0 1.5 %collective-permute-start.5 = (bf16[352,1152]{1,0:T(8,128)(2,1)S(1)}, bf16[352,1152]{1,0:T(8,128)(2,1)S(1)}, u32[]{:S(2)}, u32[]{:S(2)}) collective-permute-start(bf16[352,1152]{1,0:T(8,128)(2,1)S(1)} %slice.8), channel_id=1, source_target_pairs={{0,8},{4,12},{8,0},{12,4},{16,24},{20,28},{24,16},{28,20},{1,9},{5... | collective-permute-start | bytes 2433032 | tf_op jit(solution)/shard_map/ppermute | solution.py:341
  37.5 1.5 %collective-permute-start.6 = (bf16[352,1152]{1,0:T(8,128)(2,1)S(1)}, bf16[352,1152]{1,0:T(8,128)(2,1)S(1)}, u32[]{:S(2)}, u32[]{:S(2)}) collective-permute-start(bf16[352,1152]{1,0:T(8,128)(2,1)S(1)} %slice.8), channel_id=1, source_target_pairs={{0,16},{4,20},{8,24},{12,28},{16,0},{20,4},{24,8},{28,12},{1,17},{... | collective-permute-start | bytes 2433032 | tf_op jit(solution)/shard_map/ppermute | solution.py:341
  39.0 4.2 %add_near.1 = (f32[512,1152]{1,0:T(8,128)S(1)}, f32[512,1152]{1,0:T(8,128)S(1)}) custom-call(f32[1]{0:T(128)S(6)} %copy.7.scale_ref, f32[1]{0:T(128)S(6)} %copy.8.shift_ref, s32[2,8]{1,0:T(2,128)S(1)} %copy-done.2, bf16[512,1152]{1,0:T(8,128)(2,1)S(1)} %multiply_convert_fusion.1.image_ref.own_ref, ...), custom_call_target="tpu_custom_call" | custom-call | flops 2415919104 | bytes 4718592 | tf_op jit(solution)/shard_map/add_near/pallas_call | solution.py:28
  43.3 0.5 collective-permute-start.10
  43.8 5.9 %finish.2 = f32[512,1152]{1,0:T(8,128)} custom-call(f32[1]{0:T(128)S(6)} %copy.7.scale_ref, f32[1]{0:T(128)S(6)} %copy.8.shift_ref, s32[2,8]{1,0:T(2,128)S(1)} %copy-done.2, bf16[512,1152]{1,0:T(8,128)(2,1)S(1)} %multiply_convert_fusion.1.image_ref.own_ref, f32[512,1152]{1,0:T(8,128)S(1)} %copy-done.1, f32[512,1152]{1,0:T(8,128)S(1)} %get-tuple-element.22.sum_ref, ...), custom_call_target="tpu_custom_call" | custom-call | flops 3623878656 | bytes 4718592 | tf_op jit(solution)/shard_map/finish/pallas_call | solution.py:28
  49.7 0.6 collective-permute-start.8
  50.3 5.0 %collective-permute-done.7.refs_2_ = bf16[352,1152]{1,0:T(8,128)(2,1)S(1)} collective-permute-done((bf16[352,1152]{1,0:T(8,128)(2,1)S(1)}, bf16[352,1152]{1,0:T(8,128)(2,1)S(1)}, u32[]{:S(2)}, u32[]{:S(2)}) %collective-permute-start.7) | collective-permute-done | bytes 811040 | tf_op jit(solution)/shard_map/ppermute | solution.py:336
  55.3 1.5 %collective-permute-start.9 = (bf16[160,1152]{1,0:T(8,128)(2,1)S(1)}, bf16[160,1152]{1,0:T(8,128)(2,1)S(1)}, u32[]{:S(2)}, u32[]{:S(2)}) collective-permute-start(bf16[160,1152]{1,0:T(8,128)(2,1)S(1)} %slice.9), channel_id=1, source_target_pairs={{0,16},{4,20},{8,24},{12,28},{16,0},{20,4},{24,8},{28,12},{1,17},{... | collective-permute-start | bytes 1105928 | tf_op jit(solution)/shard_map/ppermute | solution.py:341
  56.8 0.2 collective-permute-done.5.refs_0_
  57.0 0.2 collective-permute-done.6.refs_1_
  57.2 3.4 %add_up.1.sum_ref = f32[512,1152]{1,0:T(8,128)S(1)} custom-call(f32[1]{0:T(128)S(6)} %copy.7.scale_ref, f32[1]{0:T(128)S(6)} %copy.8.shift_ref, s32[2,8]{1,0:T(2,128)S(1)} %copy-done.2, bf16[512,1152]{1,0:T(8,128)(2,1)S(1)} %multiply_convert_fusion.text_ref.own_ref, f32[512,1152]{1,0:T(8,128)S(1)} %get-tuple-element.25.sum_ref, ...), custom_call_target="tpu_custom_call" | custom-call | flops 2491416576 | bytes 4718592 | tf_op jit(solution)/shard_map/add_up/pallas_call | solution.py:28
  60.6 1.9 %collective-permute-done.8.refs_0_ = bf16[160,1152]{1,0:T(8,128)(2,1)S(1)} collective-permute-done((bf16[160,1152]{1,0:T(8,128)(2,1)S(1)}, bf16[160,1152]{1,0:T(8,128)(2,1)S(1)}, u32[]{:S(2)}, u32[]{:S(2)}) %collective-permute-start.8) | collective-permute-done | bytes 368672 | tf_op jit(solution)/shard_map/ppermute | solution.py:341
  62.6 1.2 %collective-permute-done.9.refs_1_ = bf16[160,1152]{1,0:T(8,128)(2,1)S(1)} collective-permute-done((bf16[160,1152]{1,0:T(8,128)(2,1)S(1)}, bf16[160,1152]{1,0:T(8,128)(2,1)S(1)}, u32[]{:S(2)}, u32[]{:S(2)}) %collective-permute-start.9) | collective-permute-done | bytes 368672 | tf_op jit(solution)/shard_map/ppermute | solution.py:341
  63.8 4.0 %finish.3 = f32[512,1152]{1,0:T(8,128)} custom-call(f32[1]{0:T(128)S(6)} %copy.7.scale_ref, f32[1]{0:T(128)S(6)} %copy.8.shift_ref, s32[2,8]{1,0:T(2,128)S(1)} %copy-done.2, bf16[512,1152]{1,0:T(8,128)(2,1)S(1)} %multiply_convert_fusion.text_ref.own_ref, f32[512,1152]{1,0:T(8,128)S(1)} %copy-done, f32[512,1152]{1,0:T(8,128)S(1)} %add_up.1.sum_ref, ...), custom_call_target="tpu_custom_call" | custom-call | flops 1132462080 | bytes 4718592 | tf_op jit(solution)/shard_map/finish/pallas_call | solution.py:28
  (17 shorter events, 0.5 us)
Async XLA Ops:
  0.6 2.4 %copy-start = (f32[512,1152]{1,0:T(8,128)S(1)}, f32[512,1152]{1,0:T(8,128)}, u32[]{:S(2)}) copy-start(f32[512,1152]{1,0:T(8,128)} %raw_ref.3) | copy-start | bytes 7077892
  2.7 3.6 %copy-start.1 = (f32[512,1152]{1,0:T(8,128)S(1)}, f32[512,1152]{1,0:T(8,128)}, u32[]{:S(2)}) copy-start(f32[512,1152]{1,0:T(8,128)} %raw_ref.2) | copy-start | bytes 7077892
  3.2 31.1 %collective-permute-start = (bf16[512,1152]{1,0:T(8,128)(2,1)S(1)}, bf16[512,1152]{1,0:T(8,128)(2,1)S(1)}, u32[]{:S(2)}, u32[]{:S(2)}) collective-permute-start(bf16[512,1152]{1,0:T(8,128)(2,1)S(1)} %multiply_convert_fusion.text_ref.own_ref), channel_id=1, source_target_pairs={{0,1},{1,2},{2,3},{3,0},{4,5},{5,6},{6,7},{7,4},{8,9},{9,10},{10,1... | collective-permute-start | bytes 3538952 | tf_op jit(solution)/shard_map/ppermute | solution.py:336
  6.3 29.7 %collective-permute-start.1 = (bf16[512,1152]{1,0:T(8,128)(2,1)S(1)}, bf16[512,1152]{1,0:T(8,128)(2,1)S(1)}, u32[]{:S(2)}, u32[]{:S(2)}) collective-permute-start(bf16[512,1152]{1,0:T(8,128)(2,1)S(1)} %multiply_convert_fusion.text_ref.own_ref), channel_id=1, source_target_pairs={{0,4},{4,0},{8,12},{12,8},{16,20},{20,16},{24,28},{28,24},{1,5},{5... | collective-permute-start | bytes 3538952 | tf_op jit(solution)/shard_map/ppermute | solution.py:341
  6.7 30.8 %collective-permute-start.2 = (bf16[512,1152]{1,0:T(8,128)(2,1)S(1)}, bf16[512,1152]{1,0:T(8,128)(2,1)S(1)}, u32[]{:S(2)}, u32[]{:S(2)}) collective-permute-start(bf16[512,1152]{1,0:T(8,128)(2,1)S(1)} %multiply_convert_fusion.1.image_ref.own_ref), channel_id=1, source_target_pairs={{0,4},{4,0},{8,12},{12,8},{16,20},{20,16},{24,28},{28,24},{1,5},{5... | collective-permute-start | bytes 3538952 | tf_op jit(solution)/shard_map/ppermute | solution.py:341
  7.3 36.0 %collective-permute-start.3 = (bf16[512,1152]{1,0:T(8,128)(2,1)S(1)}, bf16[512,1152]{1,0:T(8,128)(2,1)S(1)}, u32[]{:S(2)}, u32[]{:S(2)}) collective-permute-start(bf16[512,1152]{1,0:T(8,128)(2,1)S(1)} %multiply_convert_fusion.text_ref.own_ref), channel_id=1, source_target_pairs={{0,8},{4,12},{8,0},{12,4},{16,24},{20,28},{24,16},{28,20},{1,9},{5... | collective-permute-start | bytes 3538952 | tf_op jit(solution)/shard_map/ppermute | solution.py:341
  8.8 35.0 %collective-permute-start.4 = (bf16[512,1152]{1,0:T(8,128)(2,1)S(1)}, bf16[512,1152]{1,0:T(8,128)(2,1)S(1)}, u32[]{:S(2)}, u32[]{:S(2)}) collective-permute-start(bf16[512,1152]{1,0:T(8,128)(2,1)S(1)} %multiply_convert_fusion.text_ref.own_ref), channel_id=1, source_target_pairs={{0,16},{4,20},{8,24},{12,28},{16,0},{20,4},{24,8},{28,12},{1,17},{... | collective-permute-start | bytes 3538952 | tf_op jit(solution)/shard_map/ppermute | solution.py:341
  11.7 27.3 %copy-start.2 = (s32[2,8]{1,0:T(2,128)S(1)}, s32[2,8]{1,0:T(2,128)}, u32[]{:S(2)}) copy-start(s32[2,8]{1,0:T(2,128)} %grid_ref.7) | copy-start | bytes 196
  34.3 21.0 %collective-permute-start.7 = (bf16[352,1152]{1,0:T(8,128)(2,1)S(1)}, bf16[352,1152]{1,0:T(8,128)(2,1)S(1)}, u32[]{:S(2)}, u32[]{:S(2)}) collective-permute-start(bf16[352,1152]{1,0:T(8,128)(2,1)S(1)} %slice.8), channel_id=1, source_target_pairs={{0,3},{1,0},{2,1},{3,2},{4,7},{5,4},{6,5},{7,6},{8,11},{9,8},{10,9... | collective-permute-start | bytes 2433032 | tf_op jit(solution)/shard_map/ppermute | solution.py:336
  36.0 21.0 %collective-permute-start.5 = (bf16[352,1152]{1,0:T(8,128)(2,1)S(1)}, bf16[352,1152]{1,0:T(8,128)(2,1)S(1)}, u32[]{:S(2)}, u32[]{:S(2)}) collective-permute-start(bf16[352,1152]{1,0:T(8,128)(2,1)S(1)} %slice.8), channel_id=1, source_target_pairs={{0,8},{4,12},{8,0},{12,4},{16,24},{20,28},{24,16},{28,20},{1,9},{5... | collective-permute-start | bytes 2433032 | tf_op jit(solution)/shard_map/ppermute | solution.py:341
  37.5 19.7 %collective-permute-start.6 = (bf16[352,1152]{1,0:T(8,128)(2,1)S(1)}, bf16[352,1152]{1,0:T(8,128)(2,1)S(1)}, u32[]{:S(2)}, u32[]{:S(2)}) collective-permute-start(bf16[352,1152]{1,0:T(8,128)(2,1)S(1)} %slice.8), channel_id=1, source_target_pairs={{0,16},{4,20},{8,24},{12,28},{16,0},{20,4},{24,8},{28,12},{1,17},{... | collective-permute-start | bytes 2433032 | tf_op jit(solution)/shard_map/ppermute | solution.py:341
  43.3 19.3 %collective-permute-start.10 = (bf16[160,1152]{1,0:T(8,128)(2,1)S(1)}, bf16[160,1152]{1,0:T(8,128)(2,1)S(1)}, u32[]{:S(2)}, u32[]{:S(2)}) collective-permute-start(bf16[160,1152]{1,0:T(8,128)(2,1)S(1)} %slice.9), channel_id=1, source_target_pairs={{0,3},{1,0},{2,1},{3,2},{4,7},{5,4},{6,5},{7,6},{8,11},{9,8},{10,9... | collective-permute-start | bytes 1105928 | tf_op jit(solution)/shard_map/ppermute | solution.py:336
  49.7 12.9 %collective-permute-start.8 = (bf16[160,1152]{1,0:T(8,128)(2,1)S(1)}, bf16[160,1152]{1,0:T(8,128)(2,1)S(1)}, u32[]{:S(2)}, u32[]{:S(2)}) collective-permute-start(bf16[160,1152]{1,0:T(8,128)(2,1)S(1)} %slice.9), channel_id=1, source_target_pairs={{0,8},{4,12},{8,0},{12,4},{16,24},{20,28},{24,16},{28,20},{1,9},{5... | collective-permute-start | bytes 1105928 | tf_op jit(solution)/shard_map/ppermute | solution.py:341
  55.3 8.5 %collective-permute-start.9 = (bf16[160,1152]{1,0:T(8,128)(2,1)S(1)}, bf16[160,1152]{1,0:T(8,128)(2,1)S(1)}, u32[]{:S(2)}, u32[]{:S(2)}) collective-permute-start(bf16[160,1152]{1,0:T(8,128)(2,1)S(1)} %slice.9), channel_id=1, source_target_pairs={{0,16},{4,20},{8,24},{12,28},{16,0},{20,4},{24,8},{28,12},{1,17},{... | collective-permute-start | bytes 1105928 | tf_op jit(solution)/shard_map/ppermute | solution.py:341
